TPU v7x, 32 devices: a whole 2x2x4 slice. The times are simulated.
32 devices in a mesh: fsdp: 2 (over y), heads: 4 (over z), tensor: 4 (over x, core).
Axes of the slice: x: 2, y: 2, z: 4, core: 2. Of those that a mesh axis runs over, the one named last changes fastest.
Arguments:
- tokens: bfloat16 [2048, 2048], P('fsdp'), may hold values from -6 to 6
- attn_qkv: float32 [2048, 3, 2048], P('fsdp', None, ('heads', 'tensor')), may hold values from -0.125 to 0.125
- attn_out: float32 [2048, 2048], P('fsdp', ('heads', 'tensor')), may hold values from -0.5 to 0.5
- norm_gains: float32 [2, 2048], P(None, 'fsdp'), may hold values from 0.5 to 1.5
- expert_in: float32 [2048, 2, 16, 1024], P('fsdp', None, 'heads', 'tensor'), may hold values from -0.125 to 0.125
- expert_out: float32 [2048, 16, 1024], P('fsdp', 'heads', 'tensor'), may hold values from -0.375 to 0.375
- segment_ids: int32 [2048], P('fsdp'), may hold values from 0 to 15, never falling along the last dimension, each value on 1 to 1024 neighbouring positions
- keep_mask: int32 [2048], P('fsdp'), may hold values 0 or 1
- routes: int32 [2048, 8], P('fsdp'), may hold values from 0 to 15, all different within a row; in each aligned block of 1024 rows (0 to 1023, 1024 to 2047, ...) at most 640 rows name the same one
- gate_weights: float32 [2048, 8], P('fsdp'), may hold values from 0.1 to 0.5
- cotangent: bfloat16 [2048, 2048], P('fsdp'), may hold values from -6 to 6
Outputs:
- output: bfloat16 [2048, 2048], P('fsdp')
- input_grad: float32 [2048, 2048], P('fsdp')
- qkv_grad: float32 [2048, 3, 2048], P('fsdp', None, ('heads', 'tensor'))
- out_grad: float32 [2048, 2048], P('fsdp', ('heads', 'tensor'))
- gains_grad: float32 [2, 2048], P(None, 'fsdp')
- expert_in_grad: float32 [2048, 2, 16, 1024], P('fsdp', None, 'heads', 'tensor')
- expert_out_grad: float32 [2048, 16, 1024], P('fsdp', 'heads', 'tensor')
Inputs may be any that keep to these rules, and one draw needn't show every extreme that they name: `routes`: each token names 8 different experts; among the rows of one device (1024 tokens) no expert is named more than 640 times, a bound that some block reaches. `segment_ids`: never falling along the tokens; each document holds 1 to 1024 positions, one exactly 1024.
All inputs are finite; a program needn't handle non-finite values. No bound on the sum of `keep_mask` on one device may be relied on, other than what follows from the above.
Results may differ from a plain program's by a relative error of at most 0.014.
The roundings to bfloat16 on the way count: a program that leaves them out, or rounds other values in their place, can miss the bound.
Values may be sent and summed in bfloat16 or wider, within the bound.
No kernel may reach another device: no remote copies, remote signals or barrier semaphores. Data moves between devices by JAX's collectives and lax.ppermute only.
A program may use at most 320 MiB of HBM per device.

v0:
```python
import jax
import jax.numpy as jnp
from jax import lax
from jax.sharding import PartitionSpec as P

SEQ_LEN = 1024


epsilon = 1e-06


def norm_gain(values, gain_row):
    return (
        values * lax.rsqrt(jnp.mean(values * values, axis=-1, keepdims=True) + epsilon) * gain_row
    )


def swiglu(gate_pre, up_pre):
    return jax.nn.silu(gate_pre) * up_pre


def attention_probs(query_rows, key_rows, allowed, score_scale):
    scores = (
        jnp.einsum("sqe,ske->sqk", query_rows, key_rows, preferred_element_type=jnp.float32)
        * score_scale
    )
    scores = jnp.where(allowed, scores, -1e30)
    return jax.nn.softmax(scores, axis=-1)


def local(
    tokens,
    attn_qkv,
    attn_out,
    norm_gains,
    expert_in,
    expert_out,
    segment_ids,
    keep_mask,
    routes,
    gate_weights,
    cotangent,
):
    qkv_weight, out_weight, gain_rows = (
        lax.all_gather(attn_qkv.astype(jnp.bfloat16), "fsdp", axis=0, tiled=True),
        lax.all_gather(attn_out.astype(jnp.bfloat16), "fsdp", axis=0, tiled=True),
        lax.all_gather(norm_gains.astype(jnp.bfloat16), "fsdp", axis=1, tiled=True),
    )
    gain_rows = gain_rows.astype(jnp.float32)
    token_values = tokens.astype(jnp.float32)
    tok_count, model_width = token_values.shape
    head_width = qkv_weight.shape[2]
    seq_count = tok_count // SEQ_LEN
    score_scale = head_width ** (-0.5)
    normed_one = norm_gain(token_values, gain_rows[0]).astype(jnp.bfloat16)
    projected = jnp.einsum(
        "td,dcj->ctj", normed_one, qkv_weight, preferred_element_type=jnp.float32
    ).astype(jnp.bfloat16)
    heads_view = projected.reshape(3, seq_count, SEQ_LEN, head_width)
    seg_grid = segment_ids.reshape(seq_count, SEQ_LEN)
    keep_grid = keep_mask.reshape(seq_count, SEQ_LEN)
    diagonal = jnp.arange(SEQ_LEN)[:, None] == jnp.arange(SEQ_LEN)[None, :]
    allowed = (seg_grid[:, :, None] == seg_grid[:, None, :]) & (
        (keep_grid[:, None, :] == 1) | diagonal[None]
    )
    attn_probs = attention_probs(heads_view[0], heads_view[1], allowed, score_scale)
    attended = jnp.einsum(
        "sqk,ske->sqe",
        attn_probs.astype(jnp.bfloat16),
        heads_view[2],
        preferred_element_type=jnp.float32,
    )
    attended = attended.reshape(tok_count, head_width).astype(jnp.bfloat16)
    partial_branch = jnp.einsum(
        "tj,dj->td", attended, out_weight, preferred_element_type=jnp.float32
    )
    branch = lax.psum(partial_branch, ("heads", "tensor"))
    middle = token_values + branch
    normed_two = norm_gain(middle, gain_rows[1]).astype(jnp.bfloat16)
    weight_in, weight_out = (
        lax.all_gather(expert_in.astype(jnp.bfloat16), "fsdp", axis=0, tiled=True),
        lax.all_gather(expert_out.astype(jnp.bfloat16), "fsdp", axis=0, tiled=True),
    )
    local_experts = expert_in.shape[2]
    top_count = routes.shape[1]
    capacity = 5 * tok_count * top_count // (4 * local_experts * lax.axis_size("heads"))
    slot_count = local_experts * capacity
    local_routes = routes.reshape(-1) - lax.axis_index("heads") * local_experts
    is_local = (local_routes >= 0) & (local_routes < local_experts)
    one_hot = (local_routes[:, None] == jnp.arange(local_experts, dtype=jnp.int32)[None, :]).astype(
        jnp.int32
    )
    running = jnp.cumsum(one_hot, axis=0)
    slot_rank = jnp.sum(one_hot * running, axis=1) - 1
    positions = jnp.where(is_local, local_routes * capacity + slot_rank, slot_count)
    token_ids = jnp.arange(tok_count * top_count, dtype=jnp.int32) // top_count
    flat_gates = gate_weights.reshape(-1)
    slot_table = jnp.zeros((slot_count,), jnp.int32).at[positions].set(token_ids, mode="drop")
    filled = jnp.zeros((slot_count,), jnp.float32).at[positions].set(1.0, mode="drop")
    slot_gates = jnp.zeros((slot_count,), jnp.float32).at[positions].set(flat_gates, mode="drop")
    slot_rows = jnp.take(normed_two, slot_table, axis=0) * filled[:, None].astype(jnp.bfloat16)
    slot_rows = slot_rows.reshape(local_experts, capacity, model_width)
    gate_up = jnp.einsum("ecd,dgef->gecf", slot_rows, weight_in, preferred_element_type=jnp.float32)
    hidden = swiglu(gate_up[0], gate_up[1]).astype(jnp.bfloat16)
    expert_rows = jnp.einsum(
        "ecf,def->ecd", hidden, weight_out, preferred_element_type=jnp.float32
    ).reshape(slot_count, model_width)
    clipped = jnp.minimum(positions, slot_count - 1).reshape(tok_count, top_count)
    route_gates = jnp.where(is_local, flat_gates, 0.0).reshape(tok_count, top_count)
    mixture = jnp.zeros((tok_count, model_width), jnp.float32)
    for route_index in range(top_count):
        mixture = mixture + route_gates[:, route_index, None] * jnp.take(
            expert_rows, clipped[:, route_index], axis=0
        )
    mixture = lax.psum(mixture.astype(jnp.bfloat16), ("heads", "tensor")).astype(jnp.float32)
    output = (middle + mixture).astype(jnp.bfloat16)
    grad_out = cotangent.astype(jnp.float32)
    grad_rows = (jnp.take(grad_out, slot_table, axis=0) * slot_gates[:, None]).astype(jnp.bfloat16)
    grad_rows = grad_rows.reshape(local_experts, capacity, model_width)
    grad_hidden = jnp.einsum(
        "ecd,def->ecf", grad_rows, weight_out, preferred_element_type=jnp.float32
    )
    unused, pull_swiglu = jax.vjp(swiglu, gate_up[0], gate_up[1])
    grad_gate, grad_up = pull_swiglu(grad_hidden)
    grad_gate_up = jnp.stack([grad_gate, grad_up]).astype(jnp.bfloat16)
    grad_slots = jnp.einsum(
        "gecf,dgef->ecd", grad_gate_up, weight_in, preferred_element_type=jnp.float32
    )
    grad_slots = grad_slots.reshape(slot_count, model_width) * filled[:, None]
    grad_normed_two = (
        jnp.zeros((tok_count, model_width), jnp.float32).at[slot_table].add(grad_slots)
    )
    in_term = jnp.einsum(
        "ecd,gecf->dgef", slot_rows, grad_gate_up, preferred_element_type=jnp.float32
    )
    out_term = jnp.einsum("ecd,ecf->def", grad_rows, hidden, preferred_element_type=jnp.float32)
    expert_in_grad, expert_out_grad = (
        lax.psum_scatter(in_term, "fsdp", scatter_dimension=0, tiled=True),
        lax.psum_scatter(out_term, "fsdp", scatter_dimension=0, tiled=True),
    )
    grad_two = lax.psum(grad_normed_two, ("heads", "tensor"))
    unused, pull_two = jax.vjp(norm_gain, middle, gain_rows[1])
    grad_middle_norm, gain_two = pull_two(grad_two)
    grad_middle = grad_out + grad_middle_norm
    grad_branch = grad_middle.astype(jnp.bfloat16)
    out_grad_full = jnp.einsum(
        "td,tj->dj", grad_branch, attended, preferred_element_type=jnp.float32
    )
    grad_attended = jnp.dot(grad_branch, out_weight, preferred_element_type=jnp.float32).astype(
        jnp.bfloat16
    )
    grad_attended = grad_attended.reshape(seq_count, SEQ_LEN, head_width)
    again_probs = attention_probs(heads_view[0], heads_view[1], allowed, score_scale)
    grad_values = jnp.einsum(
        "sqk,sqe->ske",
        again_probs.astype(jnp.bfloat16),
        grad_attended,
        preferred_element_type=jnp.float32,
    )
    grad_probs = jnp.einsum(
        "sqe,ske->sqk", grad_attended, heads_view[2], preferred_element_type=jnp.float32
    )
    grad_scores = again_probs * (
        grad_probs - jnp.sum(again_probs * grad_probs, axis=-1, keepdims=True)
    )
    grad_scores = grad_scores.astype(jnp.bfloat16)
    grad_query = (
        jnp.einsum("sqk,ske->sqe", grad_scores, heads_view[1], preferred_element_type=jnp.float32)
        * score_scale
    )
    grad_key = (
        jnp.einsum("sqk,sqe->ske", grad_scores, heads_view[0], preferred_element_type=jnp.float32)
        * score_scale
    )
    grad_projected = (
        jnp.stack([grad_query, grad_key, grad_values])
        .reshape(3, tok_count, head_width)
        .astype(jnp.bfloat16)
    )
    qkv_grad_full = jnp.einsum(
        "td,ctj->dcj", normed_one, grad_projected, preferred_element_type=jnp.float32
    )
    grad_normed_one = jnp.einsum(
        "ctj,dcj->td", grad_projected, qkv_weight, preferred_element_type=jnp.float32
    )
    grad_one = lax.psum(grad_normed_one, ("heads", "tensor"))
    unused, pull_one = jax.vjp(norm_gain, token_values, gain_rows[0])
    grad_tokens_norm, gain_one = pull_one(grad_one)
    input_grad = grad_middle + grad_tokens_norm
    qkv_grad, out_grad, gains_grad = (
        lax.psum_scatter(qkv_grad_full, "fsdp", scatter_dimension=0, tiled=True),
        lax.psum_scatter(out_grad_full, "fsdp", scatter_dimension=0, tiled=True),
        lax.psum_scatter(jnp.stack([gain_one, gain_two]), "fsdp", scatter_dimension=1, tiled=True),
    )
    return (output, input_grad, qkv_grad, out_grad, gains_grad, expert_in_grad, expert_out_grad)


def solution(mesh):
    placed = (
        P("fsdp", None),
        P("fsdp", None, ("heads", "tensor")),
        P("fsdp", ("heads", "tensor")),
        P(None, "fsdp"),
        P("fsdp", None, "heads", "tensor"),
        P("fsdp", "heads", "tensor"),
        P("fsdp"),
        P("fsdp"),
        P("fsdp", None),
        P("fsdp", None),
        P("fsdp", None),
    )
    return jax.shard_map(
        local,
        mesh=mesh,
        in_specs=placed,
        out_specs=(
            P("fsdp", None),
            P("fsdp", None),
            P("fsdp", None, ("heads", "tensor")),
            P("fsdp", ("heads", "tensor")),
            P(None, "fsdp"),
            P("fsdp", None, "heads", "tensor"),
            P("fsdp", "heads", "tensor"),
        ),
        check_vma=False,
    )
```

profile of v0, /device:TPU:0, one launch (start us, length us, event | category | flops | bytes accessed | tf_op | source)
XLA Modules:
  0.0 1351.7 jit_solution(15955069644961626785)
XLA Ops:
  7.2 2.4 convert_element_type.88
  10.4 1.1 convert_element_type.93
  11.5 5.3 all_gather.15
  16.7 12.5 all_gather.17
  29.9 3.1 fusion.10
  33.6 8.0 all-gather.4.cloned.1.call-done
  41.7 5.1 fusion.58
  46.8 1.2 fusion.103
  50.7 4.7 fusion.104
  55.4 8.1 copy.80
  63.6 4.2 copy.81
  70.4 1.2 reduce-window.6
  73.2 30.5 %scatter_custom_fusion = s32[2560]{0:T(1024)S(1)} fusion(s32[8192]{0:T(1024)S(1)} %bitcast.155, s32[8192]{0:T(1024)S(1)} %add_select_fusion, s32[]{:T(128)} %constant.70.clone.1), kind=kCustom, calls=%fused_computation.175 | custom fusion | bytes 10244 | tf_op jit(solution)/shard_map/scatter | solution.py:98
  103.7 2.6 slice_reduce_fusion.14
  106.3 30.5 %scatter_custom_fusion.1 = f32[2560]{0:T(1024)S(1)} fusion(s32[8192]{0:T(1024)S(1)} %bitcast.156, f32[8192]{0:T(1024)S(1)} %broadcast.241, f32[]{:T(128)} %constant.49.clone.1), kind=kCustom, calls=%fused_computation.173 | custom fusion | bytes 10244 | tf_op jit(solution)/shard_map/scatter | solution.py:99
  136.8 30.5 %scatter_custom_fusion.2 = f32[2560]{0:T(1024)S(1)} fusion(s32[8192]{0:T(1024)S(1)} %bitcast.157, f32[8192]{0:T(1024)S(1)} %reshape.381, f32[]{:T(128)} %constant.49.clone.1), kind=kCustom, calls=%fused_computation.171 | custom fusion | bytes 10244 | tf_op jit(solution)/shard_map/scatter | solution.py:100
  167.4 7.1 convert_element_type.103
  175.6 23.4 %gather_fusion.1 = f32[2560,2048]{1,0:T(8,128)} fusion(f32[1024,2048]{1,0:T(8,128)} %convert_element_type.103, s32[3072]{0:T(1024)S(1)} %pad_clamp_fusion), kind=kCustom, calls=%fused_computation.9 | custom fusion | bytes 41953280 | tf_op jit(solution)/shard_map/jit(_take)/gather | solution.py:118
  200.8 26.1 %all-reduce.5.cloned.1.call-done = f32[1024,2048]{1,0:T(8,128)} async-done(((f32[1024,2048]{1,0:T(8,128)}), f32[1024,2048]{1,0:T(8,128)}) %all-reduce.5.cloned.1.call-update) | async-done | bytes 8388624 | tf_op jit(solution)/shard_map/psum | solution.py:77
  226.9 5.8 multiply_reduce_fusion.2
  232.8 3.6 copy-done.1
  236.4 3.0 multiply_convert_fusion.1
  239.4 23.5 %gather_fusion = bf16[2560,2048]{1,0:T(8,128)(2,1)} fusion(bf16[1024,2048]{1,0:T(8,128)(2,1)} %multiply_convert_fusion.1, s32[3072]{0:T(1024)S(1)} %pad_clamp_fusion), kind=kCustom, calls=%fused_computation.8 | custom fusion | bytes 20981760 | tf_op jit(solution)/shard_map/jit(_take)/gather | solution.py:101
  262.9 70.1 %all-gather.6.cloned.1.call-done = bf16[2048,2,4,256]{3,0,1,2:T(8,128)(2,1)} async-done(((bf16[1024,2,4,256]{3,0,1,2:T(8,128)(2,1)}), bf16[2048,2,4,256]{3,0,1,2:T(8,128)(2,1)}) %all-gather.6.cloned.1.call-update) | async-done | bytes 8388624 | tf_op jit(solution)/shard_map/all_gather | solution.py:81
  333.0 12.4 fusion.42
  345.4 45.9 %all-gather.8.cloned.1.call-done = bf16[2048,4,256]{2,0,1:T(8,128)(2,1)} async-done(((bf16[1024,4,256]{2,0,1:T(8,128)(2,1)}), bf16[2048,4,256]{2,0,1:T(8,128)(2,1)}) %all-gather.8.cloned.1.call-update) | async-done | bytes 4194320 | tf_op jit(solution)/shard_map/all_gather | solution.py:82
  391.3 11.9 fusion.57
  403.3 14.7 %fusion.12 = f32[4,640,2048,1]{2,1,0,3:T(8,128)} fusion(bf16[2048,2,4,256]{3,0,1,2:T(8,128)(2,1)} %all-gather.6.cloned.1.call-done, bf16[1,4,640,256]{3,2,1,0:T(8,128)(2,1)S(1)} %get-tuple-element.64, bf16[1,4,640,256]{3,2,1,0:T(8,128)(2,1)S(1)} %get-tuple-element.63), kind=kOutput, calls=%fused_computation.36 | convolution fusion | flops 5370019840 | bytes 31981568 | tf_op jit(solution)/shard_map/gecf,dgef->ecd/dot_general | solution.py:126
  418.0 16.0 %bitcast_multiply_fusion = f32[2560,2048]{1,0:T(8,128)} fusion(f32[4,640,2048,1]{2,1,0,3:T(8,128)} %fusion.12, f32[2560]{0:T(1024)S(1)} %scatter_custom_fusion.1), kind=kLoop, calls=%fused_computation.14 | loop fusion | flops 5242880 | bytes 41953280 | tf_op jit(solution)/shard_map/mul | solution.py:129
  434.0 37.2 %scatter_custom_fusion.3 = f32[1024,2048]{1,0:T(8,128)} fusion(s32[2560]{0:T(1024)S(1)} %compare_select_fusion.1, f32[2560,2048]{1,0:T(8,128)} %bitcast_multiply_fusion, f32[]{:T(128)} %constant.49.clone.1), kind=kCustom, calls=%fused_computation.71 | custom fusion | flops 5242880 | bytes 8389120 | tf_op jit(solution)/shard_map/scatter-add | solution.py:131
  471.9 2.7 slice_reduce_fusion.15
  474.6 11.5 fusion.105
  486.1 16.2 %gather_fusion.9 = f32[1024,2048]{1,0:T(8,128)} fusion(f32[2560,2048]{1,0:T(8,128)} %bitcast.132, s32[1024]{0:T(1024)S(1)} %get-tuple-element.89), kind=kCustom, calls=%fused_computation.7.clone | custom fusion | bytes 16781312 | tf_op jit(solution)/shard_map/jit(_take)/gather | solution.py:112
  502.3 16.2 %gather_fusion.8 = f32[1024,2048]{1,0:T(8,128)} fusion(f32[2560,2048]{1,0:T(8,128)} %bitcast.133, s32[1024]{0:T(1024)S(1)} %get-tuple-element.88), kind=kCustom, calls=%fused_computation.6.clone | custom fusion | bytes 16781312 | tf_op jit(solution)/shard_map/jit(_take)/gather | solution.py:112
  518.5 16.4 %gather_fusion.7 = f32[1024,2048]{1,0:T(8,128)} fusion(f32[2560,2048]{1,0:T(8,128)} %bitcast.134, s32[1024]{0:T(1024)S(1)} %get-tuple-element.87), kind=kCustom, calls=%fused_computation.5.clone | custom fusion | bytes 16781312 | tf_op jit(solution)/shard_map/jit(_take)/gather | solution.py:112
  534.9 16.3 %gather_fusion.6 = f32[1024,2048]{1,0:T(8,128)} fusion(f32[2560,2048]{1,0:T(8,128)} %bitcast.135, s32[1024]{0:T(1024)S(1)} %copy-done.38), kind=kCustom, calls=%fused_computation.4.clone | custom fusion | bytes 16781312 | tf_op jit(solution)/shard_map/jit(_take)/gather | solution.py:112
  551.2 16.0 %gather_fusion.5 = f32[1024,2048]{1,0:T(8,128)} fusion(f32[2560,2048]{1,0:T(8,128)} %bitcast.136, s32[1024]{0:T(1024)S(1)} %get-tuple-element.85), kind=kCustom, calls=%fused_computation.3.clone | custom fusion | bytes 16781312 | tf_op jit(solution)/shard_map/jit(_take)/gather | solution.py:112
  567.3 16.0 %gather_fusion.4 = f32[1024,2048]{1,0:T(8,128)} fusion(f32[2560,2048]{1,0:T(8,128)} %bitcast.137, s32[1024]{0:T(1024)S(1)} %get-tuple-element.84), kind=kCustom, calls=%fused_computation.2.clone | custom fusion | bytes 16781312 | tf_op jit(solution)/shard_map/jit(_take)/gather | solution.py:112
  583.3 17.4 %gather_fusion.3 = f32[1024,2048]{1,0:T(8,128)} fusion(f32[2560,2048]{1,0:T(8,128)} %bitcast.138, s32[1024]{0:T(1024)S(1)} %copy-done.37), kind=kCustom, calls=%fused_computation.1.clone | custom fusion | bytes 16781312 | tf_op jit(solution)/shard_map/jit(_take)/gather | solution.py:112
  600.9 16.3 %gather_fusion.2 = f32[1024,2048]{1,0:T(8,128)} fusion(f32[2560,2048]{1,0:T(8,128)} %bitcast.139, s32[1024]{0:T(1024)S(1)} %copy-done.36), kind=kCustom, calls=%fused_computation.clone | custom fusion | bytes 16781312 | tf_op jit(solution)/shard_map/jit(_take)/gather | solution.py:112
  617.3 24.9 %fusion.15 = bf16[1024,2048]{1,0:T(8,128)(2,1)} fusion(f32[1024,2048]{1,0:T(8,128)} %gather_fusion.9, f32[1024,2048]{1,0:T(8,128)} %gather_fusion.8, f32[1024,2048]{1,0:T(8,128)} %gather_fusion.7, f32[1024,2048]{1,0:T(8,128)} %gather_fusion.6, f32[1024,2048]{1,0:T(8,128)} %gather_fusion.5, f32[1024,2048]{1,0:T(8,128)} %gather_fusion.4, ...), kind=kLoop, calls=%fused_computation.41 | loop fusion | flops 50331648 | bytes 71344128 | tf_op jit(solution)/shard_map/convert_element_type | solution.py:115
  642.3 7.2 multiply_reduce_fusion
  649.6 107.2 %all-reduce.7.cloned.1.call-done = bf16[1024,2048]{1,0:T(8,128)(2,1)} async-done(((bf16[1024,2048]{1,0:T(8,128)(2,1)}), bf16[1024,2048]{1,0:T(8,128)(2,1)}) %all-reduce.7.cloned.1.call-update) | async-done | bytes 4194320 | tf_op jit(solution)/shard_map/psum | solution.py:115
  756.8 12.3 fusion.8
  769.2 1.3 fusion.61
  770.4 3.9 copy-done.4
  776.5 1.2 multiply_convert_fusion.2
  779.2 5.8 convolution_bitcast_fusion.1
  785.0 168.9 %all-reduce.11.cloned.1.call-done = f32[1024,2048]{1,0:T(8,128)} async-done(((f32[1024,2048]{1,0:T(8,128)}), f32[1024,2048]{1,0:T(8,128)}) %all-reduce.11.cloned.1.call-update) | async-done | bytes 8388624 | tf_op jit(solution)/shard_map/psum | solution.py:186
  954.0 6.4 fusion.7
  960.4 1.3 copy.69
  961.8 12.2 convolution_bitcast_fusion
  974.1 1.2 copy-done.13
  975.8 12.9 fusion.22
  989.6 6.3 fusion.49
  996.0 6.4 fusion.45
  1002.4 12.0 fusion.9
  1014.4 1.8 copy.70
  1016.2 67.5 %reduce-scatter.14.cloned.1.call-done = f32[1024,4,256]{0,2,1:T(8,128)} async-done(((f32[2048,4,256]{0,2,1:T(8,128)}), f32[1024,4,256]{0,2,1:T(8,128)}) %reduce-scatter.14.cloned.1.call-update) | async-done | bytes 4194320 | tf_op jit(solution)/shard_map/reduce_scatter | solution.py:139
  1083.7 5.2 copy.62
  1089.0 186.1 %reduce-scatter.12.cloned.1.call-done = f32[1024,2,4,256]{0,3,1,2:T(8,128)} async-done(((f32[2048,2,4,256]{0,3,1,2:T(8,128)}), f32[1024,2,4,256]{0,3,1,2:T(8,128)}) %reduce-scatter.12.cloned.1.call-update) | async-done | bytes 8388624 | tf_op jit(solution)/shard_map/reduce_scatter | solution.py:138
  1275.0 10.2 copy.61
  1285.2 13.1 reduce-scatter.10.cloned.1.call-done
  1298.3 46.1 %reduce-scatter.8.cloned.1.call-done = f32[1024,3,128]{2,0,1:T(8,128)} async-done(((f32[2048,3,128]{2,0,1:T(8,128)}), f32[1024,3,128]{2,0,1:T(8,128)}) %reduce-scatter.8.cloned.1.call-update) | async-done | bytes 1572880 | tf_op jit(solution)/shard_map/reduce_scatter | solution.py:191
  (199 shorter events, 18.1 us)
Async XLA Ops:
  7.2 34.5 %all-gather.4.cloned.1.call-start = ((), (), s32[]{:S(2)}) async-start(), calls=%async_computation.5 | async-start | bytes 2359296 | tf_op jit(solution)/shard_map/all_gather | solution.py:45
  9.6 217.3 %all-reduce.5.cloned.1.call-start = ((), (), s32[]{:S(2)}) async-start(), calls=%async_computation.6 | async-start | bytes 16777216 | tf_op jit(solution)/shard_map/psum | solution.py:77
  29.2 20.3 %copy-start.7 = (bf16[2048,128]{1,0:T(8,128)(2,1)}, bf16[2048,128]{1,0:T(8,128)(2,1)S(1)}, u32[]{:S(2)}) copy-start(bf16[2048,128]{1,0:T(8,128)(2,1)S(1)} %all_gather.17) | copy-start | bytes 1572868
  33.6 13.2 copy-start.26
  33.6 13.1 copy-start.20
  33.6 199.1 %copy-start.18 = (f32[1,2048]{1,0:T(1,128)}, f32[1,2048]{1,0:T(1,128)S(1)}, u32[]{:S(2)}) copy-start(f32[1,2048]{1,0:T(1,128)S(1)} %get-tuple-element.68) | copy-start | bytes 24580
  41.7 5.1 copy-start.61
  55.4 277.7 %all-gather.6.cloned.1.call-start = ((), (), s32[]{:S(2)}) async-start(), calls=%async_computation.7 | async-start | bytes 12582912 | tf_op jit(solution)/shard_map/all_gather | solution.py:81
  63.5 4.5 copy-start.34
  63.5 5.0 copy-start.35
  63.5 327.8 %all-gather.8.cloned.1.call-start = ((), (), s32[]{:S(2)}) async-start(), calls=%async_computation.8 | async-start | bytes 6291456 | tf_op jit(solution)/shard_map/all_gather | solution.py:82
  67.8 574.5 %all-reduce.9.cloned.1.call-start = ((), (), s32[]{:S(2)}) async-start(), calls=%async_computation.10 | async-start | bytes 16777216 | tf_op jit(solution)/shard_map/psum | solution.py:141
  167.3 224.0 %copy-start.16 = (f32[4,640]{1,0:T(4,128)}, f32[4,640]{1,0:T(4,128)S(1)}, u32[]{:S(2)}) copy-start(f32[4,640]{1,0:T(4,128)S(1)} %mul.352) | copy-start | bytes 30724
  167.3 224.0 %copy-start.24 = (pred[4,640]{1,0:T(4,128)(4,1)}, pred[4,640]{1,0:T(4,128)(4,1)S(1)}, u32[]{:S(2)}) copy-start(pred[4,640]{1,0:T(4,128)(4,1)S(1)} %broadcast_in_dim.82) | copy-start | bytes 7684
  167.3 165.7 %copy-start.51 = (bf16[4,640]{1,0:T(4,128)(2,1)}, bf16[4,640]{1,0:T(4,128)(2,1)S(1)}, u32[]{:S(2)}) copy-start(bf16[4,640]{1,0:T(4,128)(2,1)S(1)} %mul.325) | copy-start | bytes 15364
  232.7 3.7 copy-start.1
  232.7 30.2 %copy-start.32 = (f32[1024]{0:T(1024)}, f32[1024]{0:T(1024)S(1)}, u32[]{:S(2)}) copy-start(f32[1024]{0:T(1024)S(1)} %get-tuple-element.59) | copy-start | bytes 12292
  232.8 30.2 %copy-start.22 = (f32[1024]{0:T(1024)}, f32[1024]{0:T(1024)S(1)}, u32[]{:S(2)}) copy-start(f32[1024]{0:T(1024)S(1)} %fusion.85) | copy-start | bytes 12292
  403.2 14.7 %copy-start.12 = (bf16[1,4,640,256]{3,2,1,0:T(8,128)(2,1)}, bf16[1,4,640,256]{3,2,1,0:T(8,128)(2,1)S(1)}, u32[]{:S(2)}) copy-start(bf16[1,4,640,256]{3,2,1,0:T(8,128)(2,1)S(1)} %get-tuple-element.63) | copy-start | bytes 3932164
  403.2 14.7 %copy-start.14 = (bf16[1,4,640,256]{3,2,1,0:T(8,128)(2,1)}, bf16[1,4,640,256]{3,2,1,0:T(8,128)(2,1)S(1)}, u32[]{:S(2)}) copy-start(bf16[1,4,640,256]{3,2,1,0:T(8,128)(2,1)S(1)} %get-tuple-element.64) | copy-start | bytes 3932164
  403.3 71.4 %copy-start.5 = (bf16[4,640,256]{2,1,0:T(8,128)(2,1)}, bf16[4,640,256]{2,1,0:T(8,128)(2,1)S(1)}, u32[]{:S(2)}) copy-start(bf16[4,640,256]{2,1,0:T(8,128)(2,1)S(1)} %get-tuple-element.65) | copy-start | bytes 3932164
  434.0 37.3 %copy-start.30 = (s32[1024]{0:T(1024)S(1)}, s32[1024]{0:T(1024)}, u32[]{:S(2)}) copy-start(s32[1024]{0:T(1024)} %get-tuple-element.53) | copy-start | bytes 12292
  434.0 37.3 %copy-start.31 = (s32[1024]{0:T(1024)S(1)}, s32[1024]{0:T(1024)}, u32[]{:S(2)}) copy-start(s32[1024]{0:T(1024)} %get-tuple-element.54) | copy-start | bytes 12292
  434.0 37.9 %copy-start.2 = (f32[1024,8]{1,0:T(8,128)S(1)}, f32[1024,8]{1,0:T(8,128)}, u32[]{:S(2)}) copy-start(f32[1024,8]{1,0:T(8,128)} %get-tuple-element.56) | copy-start | bytes 98308
  471.3 285.6 %all-reduce.7.cloned.1.call-start = ((), (), s32[]{:S(2)}) async-start(), calls=%async_computation.9 | async-start | bytes 8388608 | tf_op jit(solution)/shard_map/psum | solution.py:115
  518.5 16.4 %copy-start.38 = (s32[1024]{0:T(1024)S(1)}, s32[1024]{0:T(1024)}, u32[]{:S(2)}) copy-start(s32[1024]{0:T(1024)} %get-tuple-element.86) | copy-start | bytes 12292
  567.2 16.1 %copy-start.37 = (s32[1024]{0:T(1024)S(1)}, s32[1024]{0:T(1024)}, u32[]{:S(2)}) copy-start(s32[1024]{0:T(1024)} %get-tuple-element.83) | copy-start | bytes 12292
  583.3 17.4 %copy-start.36 = (s32[1024]{0:T(1024)S(1)}, s32[1024]{0:T(1024)}, u32[]{:S(2)}) copy-start(s32[1024]{0:T(1024)} %get-tuple-element.82) | copy-start | bytes 12292
  600.7 16.4 %copy-start.43 = (f32[1024]{0:T(1024)S(1)}, f32[1024]{0:T(1024)}, u32[]{:S(2)}) copy-start(f32[1024]{0:T(1024)} %get-tuple-element.40) | copy-start | bytes 12292
  600.7 16.4 %copy-start.44 = (f32[1024]{0:T(1024)S(1)}, f32[1024]{0:T(1024)}, u32[]{:S(2)}) copy-start(f32[1024]{0:T(1024)} %get-tuple-element.41) | copy-start | bytes 12292
  600.7 16.4 %copy-start.45 = (f32[1024]{0:T(1024)S(1)}, f32[1024]{0:T(1024)}, u32[]{:S(2)}) copy-start(f32[1024]{0:T(1024)} %get-tuple-element.42) | copy-start | bytes 12292
  600.7 16.4 %copy-start.46 = (f32[1024]{0:T(1024)S(1)}, f32[1024]{0:T(1024)}, u32[]{:S(2)}) copy-start(f32[1024]{0:T(1024)} %get-tuple-element.43) | copy-start | bytes 12292
  600.8 16.4 %copy-start.47 = (f32[1024]{0:T(1024)S(1)}, f32[1024]{0:T(1024)}, u32[]{:S(2)}) copy-start(f32[1024]{0:T(1024)} %get-tuple-element.44) | copy-start | bytes 12292
  600.8 16.4 %copy-start.48 = (f32[1024]{0:T(1024)S(1)}, f32[1024]{0:T(1024)}, u32[]{:S(2)}) copy-start(f32[1024]{0:T(1024)} %get-tuple-element.45) | copy-start | bytes 12292
  600.8 16.4 %copy-start.49 = (f32[1024]{0:T(1024)S(1)}, f32[1024]{0:T(1024)}, u32[]{:S(2)}) copy-start(f32[1024]{0:T(1024)} %get-tuple-element.46) | copy-start | bytes 12292
  600.8 16.4 %copy-start.50 = (f32[1024]{0:T(1024)S(1)}, f32[1024]{0:T(1024)}, u32[]{:S(2)}) copy-start(f32[1024]{0:T(1024)} %get-tuple-element.47) | copy-start | bytes 12292
  600.8 16.4 %copy-start.53 = (pred[1024]{0:T(1024)(128)(4,1)S(1)}, pred[1024]{0:T(1024)(128)(4,1)}, u32[]{:S(2)}) copy-start(pred[1024]{0:T(1024)(128)(4,1)} %get-tuple-element.80) | copy-start | bytes 3076
  600.8 16.4 %copy-start.54 = (pred[1024]{0:T(1024)(128)(4,1)S(1)}, pred[1024]{0:T(1024)(128)(4,1)}, u32[]{:S(2)}) copy-start(pred[1024]{0:T(1024)(128)(4,1)} %get-tuple-element.81) | copy-start | bytes 3076
  600.8 16.4 %copy-start.55 = (pred[1024]{0:T(1024)(128)(4,1)S(1)}, pred[1024]{0:T(1024)(128)(4,1)}, u32[]{:S(2)}) copy-start(pred[1024]{0:T(1024)(128)(4,1)} %get-tuple-element.74) | copy-start | bytes 3076
  600.8 16.4 %copy-start.56 = (pred[1024]{0:T(1024)(128)(4,1)S(1)}, pred[1024]{0:T(1024)(128)(4,1)}, u32[]{:S(2)}) copy-start(pred[1024]{0:T(1024)(128)(4,1)} %get-tuple-element.75) | copy-start | bytes 3076
  600.8 16.4 %copy-start.57 = (pred[1024]{0:T(1024)(128)(4,1)S(1)}, pred[1024]{0:T(1024)(128)(4,1)}, u32[]{:S(2)}) copy-start(pred[1024]{0:T(1024)(128)(4,1)} %get-tuple-element.76) | copy-start | bytes 3076
  600.8 16.4 %copy-start.58 = (pred[1024]{0:T(1024)(128)(4,1)S(1)}, pred[1024]{0:T(1024)(128)(4,1)}, u32[]{:S(2)}) copy-start(pred[1024]{0:T(1024)(128)(4,1)} %get-tuple-element.77) | copy-start | bytes 3076
  600.9 16.4 %copy-start.59 = (pred[1024]{0:T(1024)(128)(4,1)S(1)}, pred[1024]{0:T(1024)(128)(4,1)}, u32[]{:S(2)}) copy-start(pred[1024]{0:T(1024)(128)(4,1)} %get-tuple-element.78) | copy-start | bytes 3076
  600.9 16.4 %copy-start.60 = (pred[1024]{0:T(1024)(128)(4,1)S(1)}, pred[1024]{0:T(1024)(128)(4,1)}, u32[]{:S(2)}) copy-start(pred[1024]{0:T(1024)(128)(4,1)} %get-tuple-element.79) | copy-start | bytes 3076
  617.3 25.0 %copy-start.19 = (f32[1,2048]{1,0:T(1,128)S(1)}, f32[1,2048]{1,0:T(1,128)}, u32[]{:S(2)}) copy-start(f32[1,2048]{1,0:T(1,128)} %copy-done.18) | copy-start | bytes 24580
  617.3 25.0 %copy-start.23 = (f32[1024]{0:T(1024)S(1)}, f32[1024]{0:T(1024)}, u32[]{:S(2)}) copy-start(f32[1024]{0:T(1024)} %copy-done.22) | copy-start | bytes 12292
  642.2 7.3 copy-start.33
  642.3 311.7 %all-reduce.11.cloned.1.call-start = ((), (), s32[]{:S(2)}) async-start(), calls=%async_computation.11 | async-start | bytes 16777216 | tf_op jit(solution)/shard_map/psum | solution.py:186
  649.6 119.6 %copy-start.8 = (bf16[2048,128]{1,0:T(8,128)(2,1)S(1)}, bf16[2048,128]{1,0:T(8,128)(2,1)}, u32[]{:S(2)}) copy-start(bf16[2048,128]{1,0:T(8,128)(2,1)} %copy-done.7) | copy-start | bytes 1572868
  769.1 6.0 copy-start
  769.1 5.2 copy-start.4
  769.1 5.2 copy-start.40
  769.1 5.2 copy-start.42
  779.1 174.8 %copy-start.21 = (f32[1,2048]{1,0:T(1,128)S(1)}, f32[1,2048]{1,0:T(1,128)}, u32[]{:S(2)}) copy-start(f32[1,2048]{1,0:T(1,128)} %copy-done.20) | copy-start | bytes 24580
  779.2 174.8 %copy-start.27 = (f32[1024]{0:T(1024)S(1)}, f32[1024]{0:T(1024)}, u32[]{:S(2)}) copy-start(f32[1024]{0:T(1024)} %copy-done.26) | copy-start | bytes 12292
  785.0 176.9 %copy-start.6 = (bf16[4,640,256]{2,1,0:T(8,128)(2,1)S(1)}, bf16[4,640,256]{2,1,0:T(8,128)(2,1)}, u32[]{:S(2)}) copy-start(bf16[4,640,256]{2,1,0:T(8,128)(2,1)} %copy-done.5) | copy-start | bytes 3932164
  785.0 176.9 %copy-start.17 = (f32[4,640]{1,0:T(4,128)S(1)}, f32[4,640]{1,0:T(4,128)}, u32[]{:S(2)}) copy-start(f32[4,640]{1,0:T(4,128)} %copy-done.16) | copy-start | bytes 30724
  785.0 176.9 %copy-start.25 = (pred[4,640]{1,0:T(4,128)(4,1)S(1)}, pred[4,640]{1,0:T(4,128)(4,1)}, u32[]{:S(2)}) copy-start(pred[4,640]{1,0:T(4,128)(4,1)} %copy-done.24) | copy-start | bytes 7684
  785.0 229.4 %reduce-scatter.16.cloned.1.call-start = ((), (), s32[]{:S(2)}) async-start(), calls=%async_computation.16 | async-start | bytes 1572864
  961.8 122.0 %reduce-scatter.14.cloned.1.call-start = ((), (), s32[]{:S(2)}) async-start(), calls=%async_computation.15 | async-start | bytes 12582912 | tf_op jit(solution)/shard_map/reduce_scatter | solution.py:139
  974.1 300.9 %reduce-scatter.12.cloned.1.call-start = ((), (), s32[]{:S(2)}) async-start(), calls=%async_computation.14 | async-start | bytes 25165824 | tf_op jit(solution)/shard_map/reduce_scatter | solution.py:138
  988.7 309.6 %reduce-scatter.10.cloned.1.call-start = ((), (), s32[]{:S(2)}) async-start(), calls=%async_computation.13 | async-start | bytes 1572864 | tf_op jit(solution)/shard_map/reduce_scatter | solution.py:192
  995.9 6.5 copy-start.29
  995.9 348.4 %reduce-scatter.8.cloned.1.call-start = ((), (), s32[]{:S(2)}) async-start(), calls=%async_computation.12 | async-start | bytes 4718592 | tf_op jit(solution)/shard_map/reduce_scatter | solution.py:191
  (12 other events, 18.8 us)
Sparse Core Ops, SparseCore 0:
  10.1 31.5 all-gather.3
  55.5 171.4 all-reduce.4
  229.1 103.8 all-gather.5
  334.5 56.7 all-gather.7
  471.4 169.9 all-reduce.8
  645.5 111.3 all-reduce.6
  785.1 168.8 all-reduce.10
  961.9 20.1 reduce-scatter.15
  984.5 99.2 reduce-scatter.13
  1085.9 189.0 reduce-scatter.11
  1277.9 20.3 reduce-scatter.9
  1301.0 43.3 reduce-scatter.7
where the time goes:
time: 1360 us; the launch traced here: 1350 us
  waiting for transfers between devices  739 us (54%)
  local copies, waits for them, and re-layouts  320 us (24%)
  other arithmetic  148 us (11%)
  matrix products  110 us (8%)
  blocking collectives  17.8 us (1%)
  between operations  15.6 us (1%)
    reduce_scatter x1, waiting for transfers between devices, local(): lax.psum_scatter(in_term, 'fsdp', scatter_dimension=0, tiled=True)  186 us
    psum x1, waiting for transfers between devices, local(): grad_one = lax.psum(grad_normed_one, ('heads', 'tensor'))  169 us
    gather x8, local copies, waits for them, and re-layouts, local(): jnp.take(expert_rows, clipped[:, route_index], axis=0)  131 us
    psum x1, waiting for transfers between devices, local(): lax.psum(mixture.astype(jnp.bfloat16), ('heads', 'tensor'))  107 us
    all_gather x1, waiting for transfers between devices, local(): lax.all_gather(expert_in.astype(jnp.bfloat16), 'fsdp', axis=0, tiled=True)  70.1 us
    reduce_scatter x1, waiting for transfers between devices, local(): lax.psum_scatter(out_term, 'fsdp', scatter_dimension=0, tiled=True)  67.5 us
    reduce_scatter x1, waiting for transfers between devices, local(): lax.psum_scatter(qkv_grad_full, 'fsdp', scatter_dimension=0, tiled=True)  46.1 us
    all_gather x1, waiting for transfers between devices, local(): lax.all_gather(expert_out.astype(jnp.bfloat16), 'fsdp', axis=0, tiled=True)  45.9 us
  transfers between devices with their start and end apart: 12, of which 10 were waited for; matrix products, arithmetic and copies ran while one was open for 33% of the time, Pallas kernels for 0%

commit v1 on v0

v1 whole, which is shorter than its diff:
```python
import jax
import jax.numpy as jnp
from jax import lax
from jax.sharding import PartitionSpec as P

SEQ_LEN = 1024
EPS = 1e-06
BF = jnp.bfloat16
F32 = jnp.float32
GROUP = ("heads", "tensor")
EVERY = ("fsdp", "heads", "tensor")

STEPS = {
    "z1": ("heads", 2, 0),
    "z0": ("heads", 1, 1),
    "x": ("tensor", 2, 2),
    "core": ("tensor", 1, 3),
}
ORDER_A = ("core", "x", "z0", "z1")
ORDER_B = ("core", "z0", "z1", "x")


def dot(a, b, ca=1, cb=0):
    return lax.dot_general(a, b, (((ca,), (cb,)), ((), ())), preferred_element_type=F32)


def after(value, *others):
    return lax.optimization_barrier((value,) + others)[0]


def swap(v, step):
    name, bit, _ = STEPS[step]
    return lax.ppermute(v, name, [(i, i ^ bit) for i in range(lax.axis_size(name))])


def place(step):
    name, bit, dim = STEPS[step]
    return (lax.axis_index(name) // bit) % 2, dim


def reduce_rows(v, order):
    rows, cols = v.shape
    v = v.reshape(2, 2, 2, 2, rows // 16, cols)
    for step in order:
        me, dim = place(step)
        got = swap(lax.dynamic_slice_in_dim(v, 1 - me, 1, dim), step)
        mine = lax.dynamic_slice_in_dim(v, me, 1, dim)
        v = (mine.astype(F32) + got.astype(F32)).astype(BF)
    return v.reshape(rows // 16, cols)


def gather_rows(v, order):
    rows, cols = v.shape
    v = v.reshape(1, 1, 1, 1, rows, cols)
    for step in order[::-1]:
        me, dim = place(step)
        got = swap(v, step)
        shape = list(v.shape)
        shape[dim] = 2
        wide = lax.dynamic_update_slice_in_dim(jnp.zeros(shape, v.dtype), v, me, dim)
        v = lax.dynamic_update_slice_in_dim(wide, got, 1 - me, dim)
    return v.reshape(16 * rows, cols)


def reduce_pair(pair):
    return reduce_rows(pair[0].astype(BF), ORDER_A), reduce_rows(pair[1].astype(BF), ORDER_B)


def gather_pair(pair):
    return gather_rows(pair[0], ORDER_A), gather_rows(pair[1], ORDER_B)


def two_way():
    return lax.axis_size("fsdp") == 2


def across(v):
    return lax.ppermute(v, "fsdp", [(0, 1), (1, 0)])


def spread(v, axis=0):
    if two_way():
        return v, across(v)
    full = lax.all_gather(v, "fsdp", axis=axis, tiled=True)
    half = full.shape[axis] // 2
    return (
        lax.slice_in_dim(full, 0, half, axis=axis),
        lax.slice_in_dim(full, half, 2 * half, axis=axis),
    )


def halves(v):
    half = v.shape[-1] // 2
    start = lax.axis_index("fsdp") * half if two_way() else 0
    return (
        lax.dynamic_slice_in_dim(v, start, half, v.ndim - 1),
        lax.dynamic_slice_in_dim(v, half - start, half, v.ndim - 1),
    )


def join(first, second):
    straight = jnp.concatenate([first, second], axis=-1)
    if not two_way():
        return straight
    crossed = jnp.concatenate([second, first], axis=-1)
    return jnp.where(lax.axis_index("fsdp") == 0, straight, crossed)


def collect(left, right):
    if two_way():
        got = across(dot(left[1], right, 0, 0).astype(BF))
        return dot(left[0], right, 0, 0) + got.astype(F32)
    whole = jnp.concatenate([dot(part, right, 0, 0) for part in left], axis=0)
    return lax.psum_scatter(whole, "fsdp", scatter_dimension=0, tiled=True)


def rms(first, second):
    total = jnp.sum(first * first, -1, keepdims=True) + jnp.sum(second * second, -1, keepdims=True)
    return lax.rsqrt(total / (first.shape[-1] + second.shape[-1]) + EPS)


def norm_back(grads, normed, gains, scale):
    m = [g * d for g, d in zip(gains, grads)]
    mean = (
        jnp.sum(m[0] * normed[0], -1, keepdims=True) + jnp.sum(m[1] * normed[1], -1, keepdims=True)
    ) / (m[0].shape[-1] + m[1].shape[-1])
    return [scale * (a - n * mean) for a, n in zip(m, normed)]


def local(
    tokens,
    attn_qkv,
    attn_out,
    norm_gains,
    expert_in,
    expert_out,
    segment_ids,
    keep_mask,
    routes,
    gate_weights,
    cotangent,
):
    tok_count, width = tokens.shape
    head_width = attn_qkv.shape[2]
    seq_count = tok_count // SEQ_LEN
    own_experts, hidden_width = expert_in.shape[2:]
    columns = own_experts * hidden_width
    rank = lax.axis_index("heads") * lax.axis_size("tensor") + lax.axis_index("tensor")
    shard = tok_count // (lax.axis_size("heads") * lax.axis_size("tensor"))

    gains = [g.astype(F32) for g in spread(norm_gains.astype(BF), 1)]
    gain_one, gain_two = [g[0] for g in gains], [g[1] for g in gains]
    w_qkv = spread(attn_qkv.astype(BF).reshape(-1, 3 * head_width))
    w_o = spread(after(attn_out, w_qkv[1]).astype(BF).T, 1)
    w_out = spread(after(expert_out, w_o[1]).astype(BF).reshape(-1, columns))
    w_in = spread(after(expert_in, w_out[1]).astype(BF).reshape(-1, 2 * columns))
    w_o_full = gather_pair(w_o)

    x = halves(tokens.astype(F32))
    r_one = rms(*x)
    h_one = [(v * r_one * g).astype(BF) for v, g in zip(x, gain_one)]
    projected = (dot(h_one[0], w_qkv[0]) + dot(h_one[1], w_qkv[1])).astype(BF)
    q, k, v = [
        projected[:, i * head_width : (i + 1) * head_width].reshape(seq_count, SEQ_LEN, head_width)
        for i in range(3)
    ]
    seg = segment_ids.reshape(seq_count, SEQ_LEN)
    keep = keep_mask.reshape(seq_count, SEQ_LEN)
    diagonal = jnp.arange(SEQ_LEN)[:, None] == jnp.arange(SEQ_LEN)[None, :]
    allowed = (seg[:, :, None] == seg[:, None, :]) & ((keep[:, None, :] == 1) | diagonal[None])
    score_scale = head_width ** (-0.5)
    scores = jnp.einsum("sqe,ske->sqk", q, k, preferred_element_type=F32) * score_scale
    probs = jax.nn.softmax(jnp.where(allowed, scores, -1e30), axis=-1)
    attended = jnp.einsum("sqk,ske->sqe", probs.astype(BF), v, preferred_element_type=F32)
    attended = attended.reshape(tok_count, head_width).astype(BF)

    attended_rows = lax.all_to_all(attended, GROUP, 0, 1, tiled=True)
    x_rows = halves(lax.dynamic_slice_in_dim(tokens, rank * shard, shard, 0).astype(F32))
    middle = [v + dot(attended_rows, w) for v, w in zip(x_rows, w_o_full)]
    r_two = rms(*middle)
    n_two = [v * r_two for v in middle]
    h_two = gather_pair([(n * g).astype(BF) for n, g in zip(n_two, gain_two)])

    first_expert = lax.axis_index("heads") * own_experts
    weights = jnp.concatenate(
        [
            jnp.broadcast_to(
                jnp.sum(
                    jnp.where(routes == first_expert + e, gate_weights, 0.0), 1, keepdims=True
                ),
                (tok_count, hidden_width),
            )
            for e in range(own_experts)
        ],
        axis=1,
    )
    grad_out = halves(cotangent)
    grad_act = weights * (dot(grad_out[0], w_out[0]) + dot(grad_out[1], w_out[1]))
    gate_up = dot(h_two[0], w_in[0]) + dot(h_two[1], w_in[1])
    gate, up = gate_up[:, :columns], gate_up[:, columns:]
    sig = jax.nn.sigmoid(gate)
    silu = gate * sig
    act = (weights * (silu * up)).astype(BF)
    grad_gate_up = jnp.concatenate(
        [grad_act * up * sig * (1.0 + gate * (1.0 - sig)), grad_act * silu], axis=1
    ).astype(BF)
    grad_two = reduce_pair([dot(grad_gate_up, w, 1, 1) for w in w_in])
    grad_two = [g.astype(F32) for g in grad_two]
    expert_out_grad = collect(grad_out, act)
    expert_in_grad = collect(h_two, grad_gate_up)

    mixture = reduce_pair([dot(act, w, 1, 1) for w in w_out])
    out_rows = join(*[(a + b.astype(F32)).astype(BF) for a, b in zip(middle, mixture)])
    half = width // 2
    output = jnp.concatenate(gather_pair([out_rows[:, :half], out_rows[:, half:]]), axis=1)

    out_in_rows = halves(lax.dynamic_slice_in_dim(cotangent, rank * shard, shard, 0).astype(F32))
    grad_middle = [
        a + b for a, b in zip(out_in_rows, norm_back(grad_two, n_two, gain_two, r_two))
    ]
    gain_two_part = join(*[jnp.sum(g * n, axis=0) for g, n in zip(grad_two, n_two)])
    grad_branch_rows = [g.astype(BF) for g in grad_middle]
    grad_attended = (
        dot(grad_branch_rows[0], w_o_full[0], 1, 1) + dot(grad_branch_rows[1], w_o_full[1], 1, 1)
    ).astype(BF)
    grad_attended = lax.all_to_all(grad_attended, GROUP, 1, 0, tiled=True)
    grad_attended = grad_attended.reshape(seq_count, SEQ_LEN, head_width)
    grad_branch = gather_pair(grad_branch_rows)
    out_grad = collect(grad_branch, attended)

    grad_v = jnp.einsum("sqk,sqe->ske", probs.astype(BF), grad_attended, preferred_element_type=F32)
    grad_probs = jnp.einsum("sqe,ske->sqk", grad_attended, v, preferred_element_type=F32)
    grad_scores = probs * (grad_probs - jnp.sum(probs * grad_probs, axis=-1, keepdims=True))
    grad_scores = grad_scores.astype(BF)
    grad_q = jnp.einsum("sqk,ske->sqe", grad_scores, k, preferred_element_type=F32) * score_scale
    grad_k = jnp.einsum("sqk,sqe->ske", grad_scores, q, preferred_element_type=F32) * score_scale
    grad_projected = jnp.concatenate([grad_q, grad_k, grad_v], axis=-1)
    grad_projected = grad_projected.reshape(tok_count, 3 * head_width).astype(BF)
    grad_one_part = [dot(grad_projected, w, 1, 1) for w in w_qkv]
    qkv_grad = collect(h_one, grad_projected)

    gain_one_part = join(
        *[jnp.sum(g * (v * r_one), axis=0) for g, v in zip(grad_one_part, x)]
    )
    gain_parts = lax.psum(jnp.stack([gain_one_part, gain_two_part]), EVERY)
    own_width = norm_gains.shape[1]
    gains_grad = lax.dynamic_slice_in_dim(
        gain_parts, lax.axis_index("fsdp") * own_width, own_width, 1
    )

    grad_one = [g.astype(F32) for g in reduce_pair(grad_one_part)]
    r_rows = rms(*x_rows)
    n_rows = [v * r_rows for v in x_rows]
    grad_rows = join(
        *[a + b for a, b in zip(grad_middle, norm_back(grad_one, n_rows, gain_one, r_rows))]
    ).astype(BF)
    input_grad = jnp.concatenate(
        gather_pair([grad_rows[:, :half], grad_rows[:, half:]]), axis=1
    ).astype(F32)

    return (
        output,
        input_grad,
        qkv_grad.reshape(attn_qkv.shape),
        out_grad,
        gains_grad,
        expert_in_grad.reshape(expert_in.shape),
        expert_out_grad.reshape(expert_out.shape),
    )


def solution(mesh):
    placed = (
        P("fsdp", None),
        P("fsdp", None, ("heads", "tensor")),
        P("fsdp", ("heads", "tensor")),
        P(None, "fsdp"),
        P("fsdp", None, "heads", "tensor"),
        P("fsdp", "heads", "tensor"),
        P("fsdp"),
        P("fsdp"),
        P("fsdp", None),
        P("fsdp", None),
        P("fsdp", None),
    )
    return jax.shard_map(
        local,
        mesh=mesh,
        in_specs=placed,
        out_specs=(
            P("fsdp", None),
            P("fsdp", None),
            P("fsdp", None, ("heads", "tensor")),
            P("fsdp", ("heads", "tensor")),
            P(None, "fsdp"),
            P("fsdp", None, "heads", "tensor"),
            P("fsdp", "heads", "tensor"),
        ),
        check_vma=False,
    )
```

time: 1360 us -> 723 us (0.53)
  waiting for transfers between devices: 739 us -> 322 us
  local copies, waits for them, and re-layouts: 320 us -> 120 us
  other arithmetic: 148 us -> 37 us
  starting transfers between devices: 0.67 us -> 80.1 us
  blocking collectives: 17.8 us -> 38.1 us
    ppermute x0 -> x73, waiting for transfers between devices: none -> 322 us  [the longest x64 169 us: swap(): lax.ppermute(v, name, [(i, i ^ bit) for i in range(lax.axis_size(name))])]
    reduce_scatter x4 -> x0, waiting for transfers between devices: 313 us -> none  [the longest x1 186 us: local(): lax.psum_scatter(in_term, 'fsdp', scatter_dimension=0, tiled=True)]
    psum x4 -> x0, waiting for transfers between devices: 302 us -> none  [the longest x1 169 us: local(): grad_one = lax.psum(grad_normed_one, ('heads', 'tensor'))]
    gather x10 -> x0, local copies, waits for them, and re-layouts: 178 us -> none  [the longest x8 131 us: local(): jnp.take(expert_rows, clipped[:, route_index], axis=0)]
    all_gather x3 -> x0, waiting for transfers between devices: 124 us -> none  [the longest x1 70.1 us: local(): lax.all_gather(expert_in.astype(jnp.bfloat16), 'fsdp', axis=0, tiled=True)]
    scatter x3 -> x0, local copies, waits for them, and re-layouts: 91.4 us -> none  [the longest x1 30.5 us: local(): jnp.zeros((slot_count,), jnp.float32).at[positions]]
    ppermute x0 -> x73, starting transfers between devices: none -> 71.4 us  [the longest x64 60.3 us: swap(): lax.ppermute(v, name, [(i, i ^ bit) for i in range(lax.axis_size(name))])]
    dynamic_update_slice x0 -> x74, local copies, waits for them, and re-layouts: none -> 54.2 us  [the longest x40 28.5 us: gather_rows(): v = lax.dynamic_update_slice_in_dim(wide, got, 1 - me, dim)]
  transfers between devices with their start and end apart: 12 -> 75, of which waited for: 10 -> 35; matrix products, arithmetic and copies ran while one was open for 33% -> 31% of each run, Pallas kernels for 0% -> 0%
where the time goes in v1:
time: 723 us; the launch traced here: 714 us
  waiting for transfers between devices  322 us (45%)
  local copies, waits for them, and re-layouts  120 us (17%)
  matrix products  114 us (16%)
  starting transfers between devices  80.1 us (11%)
  blocking collectives  38.1 us (5%)
  other arithmetic  37 us (5%)
    ppermute x64, waiting for transfers between devices, swap(): lax.ppermute(v, name, [(i, i ^ bit) for i in range(lax.axis_size(name))])  169 us
    ppermute x9, waiting for transfers between devices, across(): return lax.ppermute(v, 'fsdp', [(0, 1), (1, 0)])  153 us
    dot_general x24, matrix products, dot(): lax.dot_general(a, b, (((ca,), (cb,)), ((), ())), preferred_element_type=...  105 us
    ppermute x64, starting transfers between devices, swap(): lax.ppermute(v, name, [(i, i ^ bit) for i in range(lax.axis_size(name))])  60.3 us
    psum x1, blocking collectives, local(): gain_parts = lax.psum(jnp.stack([gain_one_part, gain_two_part]), EVERY)  38.1 us
    dynamic_update_slice x40, local copies, waits for them, and re-layouts, gather_rows(): v = lax.dynamic_update_slice_in_dim(wide, got, 1 - me, dim)  28.5 us
    dynamic_update_slice x34, local copies, waits for them, and re-layouts, gather_rows(): lax.dynamic_update_slice_in_dim(jnp.zeros(shape, v.dtype), v, me, dim)  25.7 us
    unnamed x140, local copies, waits for them, and re-layouts  24.1 us
  transfers between devices with their start and end apart: 75, of which 35 were waited for; matrix products, arithmetic and copies ran while one was open for 31% of the time, Pallas kernels for 0%

profile of v1, /device:TPU:0, one launch (start us, length us, event | category | flops | bytes accessed | tf_op | source)
XLA Modules:
  0.0 713.8 jit_solution(3592967877426458592)
XLA Ops:
  2.3 3.0 collective-permute-start.1
  5.5 6.7 convert_element_type.391
  12.1 4.1 multiply_reduce_fusion.3
  16.3 6.7 collective-permute-done.1
  24.9 2.6 collective-permute-start.2
  27.6 3.0 collective-permute-done.6
  32.0 6.3 collective-permute-done.2
  39.0 4.6 fusion.82
  44.8 3.4 collective-permute-start.8
  50.1 6.2 collective-permute-done.3
  61.7 9.7 %collective-permute-done.8 = bf16[1,1,2,1,128,1024]{5,4,3,2,1,0:T(8,128)(2,1)S(1)} collective-permute-done((bf16[1,1,2,1,128,1024]{5,4,3,2,1,0:T(8,128)(2,1)S(1)}, bf16[1,1,2,1,128,1024]{5,4,3,2,1,0:T(8,128)(2,1)S(1)}, u32[]{:S(2)}, u32[]{:S(2)}) %collective-permute-start.8) | collective-permute-done | bytes 524320 | tf_op jit(solution)/shard_map/ppermute | solution.py:33
  72.2 3.1 convert_element_type.404
  87.0 9.7 %collective-permute-done.9 = bf16[2,1,2,1,128,1024]{5,4,3,2,1,0:T(8,128)(2,1)} collective-permute-done((bf16[2,1,2,1,128,1024]{5,4,3,2,1,0:T(8,128)(2,1)}, bf16[2,1,2,1,128,1024]{5,4,3,2,1,0:T(8,128)(2,1)}, u32[]{:S(2)}, u32[]{:S(2)}) %collective-permute-start.9) | collective-permute-done | bytes 1048608 | tf_op jit(solution)/shard_map/ppermute | solution.py:33
  103.8 5.0 all-to-all-start
  111.8 2.7 constant_dynamic-update-slice_fusion.65
  116.5 7.7 %collective-permute-done.15 = bf16[1024,1024]{1,0:T(8,128)(2,1)} collective-permute-done((bf16[1024,1024]{1,0:T(8,128)(2,1)}, bf16[1024,1024]{1,0:T(8,128)(2,1)}, u32[]{:S(2)}, u32[]{:S(2)}) %collective-permute-start.15) | collective-permute-done | bytes 2097184 | tf_op jit(solution)/shard_map/ppermute | solution.py:78
  124.1 3.5 convert_element_type.405
  127.6 7.7 %reshape.416 = bf16[1024,2048]{1,0:T(8,128)(2,1)} reshape(bf16[1024,2,4,256]{3,2,1,0:T(4,128)(2,1)} %convert_element_type.405) | data formatting | bytes 8388608 | tf_op jit(solution)/shard_map/reshape | solution.py:156
  135.9 3.1 constant_dynamic-update-slice_fusion.72
  138.9 3.3 multiply_reduce_fusion.8
  147.5 2.7 collective-permute-start.11
  151.7 3.2 collective-permute-done.11
  158.9 5.4 collective-permute-done.12
  168.8 4.7 collective-permute-done.13
  173.8 4.7 collective-permute-done.18
  178.8 6.0 fusion.13
  185.8 40.6 %collective-permute-done.20 = bf16[1024,2048]{1,0:T(8,128)(2,1)} collective-permute-done((bf16[1024,2048]{1,0:T(8,128)(2,1)}, bf16[1024,2048]{1,0:T(8,128)(2,1)}, u32[]{:S(2)}, u32[]{:S(2)}) %collective-permute-start.20) | collective-permute-done | bytes 4194336 | tf_op jit(solution)/shard_map/ppermute | solution.py:78
  226.4 6.4 fusion.94
  232.9 7.0 convolution_add_fusion
  240.6 10.2 %multiply_convert_fusion.2 = (bf16[1024,1024]{1,0:T(8,128)(2,1)}, bf16[1024,1024]{1,0:T(8,128)(2,1)}, bf16[1024,1024]{1,0:T(8,128)(2,1)}) fusion(f32[1024,2048]{1,0:T(8,128)} %convolution_add_fusion, f32[1024,256]{1,0:T(8,128)S(1)} %broadcast_in_dim.34, f32[1024,256]{1,0:T(8,128)S(1)} %broadcast_in_dim.33, f32[1024,256]{1,0:T(8,128)S(1)} %broadcast_in_dim.32, ...), kind=kOutput, calls=%fused_computation.14 | convolution fusion | flops 2169503744 | bytes 27262980 | tf_op jit(solution)/shard_map/dot_general | solution.py:24
  250.8 4.6 convolution_convert_fusion.5
  257.0 4.1 convolution_convert_fusion.4
  262.7 6.4 convolution_convert_fusion
  269.1 7.3 %convolution_convert_fusion.2 = bf16[1024,1024]{1,0:T(8,128)(2,1)S(1)} fusion(bf16[1024,2048]{1,0:T(8,128)(2,1)} %collective-permute-done.20, bf16[1024,1024]{1,0:T(8,128)(2,1)S(1)} %copy-done.56, bf16[1024,1024]{1,0:T(8,128)(2,1)S(1)} %copy-done.54), kind=kOutput, calls=%fused_computation.39 | convolution fusion | flops 4304404480 | bytes 10485760 | tf_op jit(solution)/shard_map/dot_general | solution.py:24
  276.6 6.4 convolution_convert_fusion.3
  289.8 9.1 %collective-permute-done.22 = bf16[2,2,1,1,64,1024]{5,4,3,2,1,0:T(8,128)(2,1)S(1)} collective-permute-done((bf16[2,2,1,1,64,1024]{5,4,3,2,1,0:T(8,128)(2,1)S(1)}, bf16[2,2,1,1,64,1024]{5,4,3,2,1,0:T(8,128)(2,1)S(1)}, u32[]{:S(2)}, u32[]{:S(2)}) %collective-permute-start.22) | collective-permute-done | bytes 524320 | tf_op jit(solution)/shard_map/ppermute | solution.py:33
  303.6 14.2 %collective-permute-done.42 = bf16[2,1,2,1,64,1024]{5,4,3,2,1,0:T(8,128)(2,1)S(1)} collective-permute-done((bf16[2,1,2,1,64,1024]{5,4,3,2,1,0:T(8,128)(2,1)S(1)}, bf16[2,1,2,1,64,1024]{5,4,3,2,1,0:T(8,128)(2,1)S(1)}, u32[]{:S(2)}, u32[]{:S(2)}) %collective-permute-start.42) | collective-permute-done | bytes 524320 | tf_op jit(solution)/shard_map/ppermute | solution.py:33
  324.9 11.7 %collective-permute-done.43 = bf16[1,1,2,1,64,1024]{5,4,3,2,1,0:T(8,128)(2,1)S(1)} collective-permute-done((bf16[1,1,2,1,64,1024]{5,4,3,2,1,0:T(8,128)(2,1)S(1)}, bf16[1,1,2,1,64,1024]{5,4,3,2,1,0:T(8,128)(2,1)S(1)}, u32[]{:S(2)}, u32[]{:S(2)}) %collective-permute-start.43) | collective-permute-done | bytes 262176 | tf_op jit(solution)/shard_map/ppermute | solution.py:33
  337.5 3.8 convolution_convert_fusion.1
  351.5 3.7 all-to-all-start.1
  360.4 2.8 collective-permute-done.66
  364.5 9.2 %collective-permute-done.62 = bf16[1,1,1,1,64,1024]{5,4,3,2,1,0:T(8,128)(2,1)S(1)} collective-permute-done((bf16[1,1,1,1,64,1024]{5,4,3,2,1,0:T(8,128)(2,1)S(1)}, bf16[1,1,1,1,64,1024]{5,4,3,2,1,0:T(8,128)(2,1)S(1)}, u32[]{:S(2)}, u32[]{:S(2)}) %collective-permute-start.62) | collective-permute-done | bytes 131104 | tf_op jit(solution)/shard_map/ppermute | solution.py:33
  373.7 8.4 %collective-permute-done.29 = bf16[1,1,1,1,64,1024]{5,4,3,2,1,0:T(8,128)(2,1)S(1)} collective-permute-done((bf16[1,1,1,1,64,1024]{5,4,3,2,1,0:T(8,128)(2,1)S(1)}, bf16[1,1,1,1,64,1024]{5,4,3,2,1,0:T(8,128)(2,1)S(1)}, u32[]{:S(2)}, u32[]{:S(2)}) %collective-permute-start.29) | collective-permute-done | bytes 131104 | tf_op jit(solution)/shard_map/ppermute | solution.py:33
  385.8 91.9 %collective-permute-done.72 = bf16[1024,1024]{0,1:T(8,128)(2,1)} collective-permute-done((bf16[1024,1024]{0,1:T(8,128)(2,1)}, bf16[1024,1024]{0,1:T(8,128)(2,1)}, u32[]{:S(2)}, u32[]{:S(2)}) %collective-permute-start.72) | collective-permute-done | bytes 2097184 | tf_op jit(solution)/shard_map/ppermute | solution.py:78
  477.8 2.6 collective-permute-start.34
  480.4 6.6 convert_add_fusion.1
  491.8 5.2 copy.43
  514.3 3.3 multiply_reduce_fusion.2
  523.7 3.2 multiply_reduce_fusion.1
  526.9 38.1 %psum.7 = f32[2,2048]{1,0:T(2,128)S(1)} all-reduce(f32[2,2048]{1,0:T(2,128)S(1)} %pad_maximum_fusion.3), channel_id=1, replica_groups=mesh['fsdp'=2,'heads'=4,'tensor'=4] {'fsdp','heads','tensor'}, use_global_device_ids=true, to_apply=%region_21.22 | all-reduce | flops 4096 | bytes 32768 | tf_op jit(solution)/shard_map/psum | solution.py:245
  569.1 3.3 convolution_convert_fusion.6
  588.7 2.8 collective-permute-done.61
  593.8 3.0 copy.42
  608.6 4.8 collective-permute-done.46
  619.0 5.4 collective-permute-done.47
  626.4 11.0 %collective-permute-done.51 = bf16[1,1,2,1,64,1024]{5,4,3,2,1,0:T(8,128)(2,1)S(1)} collective-permute-done((bf16[1,1,2,1,64,1024]{5,4,3,2,1,0:T(8,128)(2,1)S(1)}, bf16[1,1,2,1,64,1024]{5,4,3,2,1,0:T(8,128)(2,1)S(1)}, u32[]{:S(2)}, u32[]{:S(2)}) %collective-permute-start.51) | collective-permute-done | bytes 262176 | tf_op jit(solution)/shard_map/ppermute | solution.py:33
  638.0 7.1 collective-permute-done.48
  646.5 7.7 %collective-permute-done.53 = bf16[1,1,1,1,64,1024]{5,4,3,2,1,0:T(8,128)(2,1)S(1)} collective-permute-done((bf16[1,1,1,1,64,1024]{5,4,3,2,1,0:T(8,128)(2,1)S(1)}, bf16[1,1,1,1,64,1024]{5,4,3,2,1,0:T(8,128)(2,1)S(1)}, u32[]{:S(2)}, u32[]{:S(2)}) %collective-permute-start.53) | collective-permute-done | bytes 131104 | tf_op jit(solution)/shard_map/ppermute | solution.py:33
  657.0 10.3 %collective-permute-done.54 = bf16[2,1,1,1,64,1024]{5,4,3,2,1,0:T(8,128)(2,1)S(1)} collective-permute-done((bf16[2,1,1,1,64,1024]{5,4,3,2,1,0:T(8,128)(2,1)S(1)}, bf16[2,1,1,1,64,1024]{5,4,3,2,1,0:T(8,128)(2,1)S(1)}, u32[]{:S(2)}, u32[]{:S(2)}) %collective-permute-start.54) | collective-permute-done | bytes 262176 | tf_op jit(solution)/shard_map/ppermute | solution.py:33
  675.4 5.0 collective-permute-done.55
  682.0 8.9 %convert_add_fusion = f32[1024,2048]{1,0:T(8,128)} fusion(bf16[1024,2048]{1,0:T(8,128)(2,1)} %collective-permute-done.71, bf16[1024,1024]{1,0:T(8,128)(2,1)S(1)} %bitcast.206, bf16[1024,1024]{1,0:T(8,128)(2,1)S(1)} %copy-done.57, bf16[1024,1024]{1,0:T(8,128)(2,1)S(1)} %copy-done.55), kind=kOutput, calls=%fused_computation | convolution fusion | flops 4307550208 | bytes 18874368 | tf_op jit(solution)/shard_map/dot_general | solution.py:24
  690.9 10.8 %reshape.439 = f32[1024,2,4,256]{3,2,1,0:T(4,128)} reshape(f32[1024,2048]{1,0:T(8,128)} %convert_add_fusion) | data formatting | bytes 16777216 | tf_op jit(solution)/shard_map/reshape | solution.py:267
  701.7 2.6 convolution_add_fusion.2
  708.9 4.4 maximum_convert_fusion
  (458 shorter events, 187.8 us)
Async XLA Ops:
  2.3 20.6 %collective-permute-start.1 = (bf16[1024,384]{0,1:T(8,128)(2,1)S(1)}, bf16[1024,384]{0,1:T(8,128)(2,1)S(1)}, u32[]{:S(2)}, u32[]{:S(2)}) collective-permute-start(bf16[1024,384]{0,1:T(8,128)(2,1)S(1)} %bitcast.190), channel_id=1, source_target_pairs={{0,16},{16,0},{1,17},{17,1},{2,18},{18,2},{3,19},{19,3},{4,20},{20... | collective-permute-start | bytes 2359304 | tf_op jit(solution)/shard_map/ppermute | solution.py:78
  5.4 66.8 %collective-permute-start = (bf16[2,1024]{1,0:T(2,128)(2,1)S(1)}, bf16[2,1024]{1,0:T(2,128)(2,1)S(1)}, u32[]{:S(2)}, u32[]{:S(2)}) collective-permute-start(bf16[2,1024]{1,0:T(2,128)(2,1)S(1)} %convert_element_type.392), channel_id=1, source_target_pairs={{0,16},{16,0},{1,17},{17,1},{2,18},{18,2},{3,19},{19,3},{4,20},{20... | collective-permute-start | bytes 12296 | tf_op jit(solution)/shard_map/ppermute | solution.py:78
  24.9 13.4 %collective-permute-start.2 = (bf16[1,1,1,1,128,1024]{5,4,3,2,1,0:T(8,128)(2,1)S(1)}, bf16[1,1,1,1,128,1024]{5,4,3,2,1,0:T(8,128)(2,1)S(1)}, u32[]{:S(2)}, u32[]{:S(2)}) collective-permute-start(bf16[1,1,1,1,128,1024]{5,4,3,2,1,0:T(8,128)(2,1)S(1)} %bitcast.217), channel_id=1, source_target_pairs={{0,8},{4,12},{8,0},{12,4},{1,9},{5,13},{9,1},{13,5},{2,10},{6,14},... | collective-permute-start | bytes 786440 | tf_op jit(solution)/shard_map/ppermute | solution.py:33
  30.6 13.1 %collective-permute-start.7 = (bf16[1,1,1,1,128,1024]{5,4,3,2,1,0:T(8,128)(2,1)S(1)}, bf16[1,1,1,1,128,1024]{5,4,3,2,1,0:T(8,128)(2,1)}, u32[]{:S(2)}, u32[]{:S(2)}) collective-permute-start(bf16[1,1,1,1,128,1024]{5,4,3,2,1,0:T(8,128)(2,1)S(1)} %bitcast.218), channel_id=1, source_target_pairs={{0,2},{1,3},{2,0},{3,1},{4,6},{5,7},{6,4},{7,5},{8,10},{9,11},{10,... | collective-permute-start | bytes 786440 | tf_op jit(solution)/shard_map/ppermute | solution.py:33
  38.3 18.1 %collective-permute-start.3 = (bf16[2,1,1,1,128,1024]{5,4,3,2,1,0:T(8,128)(2,1)S(1)}, bf16[2,1,1,1,128,1024]{5,4,3,2,1,0:T(8,128)(2,1)S(1)}, u32[]{:S(2)}, u32[]{:S(2)}) collective-permute-start(bf16[2,1,1,1,128,1024]{5,4,3,2,1,0:T(8,128)(2,1)S(1)} %constant_dynamic-update-slice_fusion.78), channel_id=1, source_target_pairs={{0,4},{4,0},{8,12},{12,8},{1,5},{5,1},{9,13},{13,9},{2,6},{6,2},{1... | collective-permute-start | bytes 1572872 | tf_op jit(solution)/shard_map/ppermute | solution.py:33
  44.8 26.6 %collective-permute-start.8 = (bf16[1,1,2,1,128,1024]{5,4,3,2,1,0:T(8,128)(2,1)S(1)}, bf16[1,1,2,1,128,1024]{5,4,3,2,1,0:T(8,128)(2,1)S(1)}, u32[]{:S(2)}, u32[]{:S(2)}) collective-permute-start(bf16[1,1,2,1,128,1024]{5,4,3,2,1,0:T(8,128)(2,1)S(1)} %constant_dynamic-update-slice_fusion.70), channel_id=1, source_target_pairs={{0,8},{4,12},{8,0},{12,4},{1,9},{5,13},{9,1},{13,5},{2,10},{6,14},... | collective-permute-start | bytes 1572872 | tf_op jit(solution)/shard_map/ppermute | solution.py:33
  57.2 22.9 %collective-permute-start.4 = (bf16[2,2,1,1,128,1024]{5,4,3,2,1,0:T(8,128)(2,1)}, bf16[2,2,1,1,128,1024]{5,4,3,2,1,0:T(8,128)(2,1)}, u32[]{:S(2)}, u32[]{:S(2)}) collective-permute-start(bf16[2,2,1,1,128,1024]{5,4,3,2,1,0:T(8,128)(2,1)} %constant_dynamic-update-slice_fusion.76), channel_id=1, source_target_pairs={{0,2},{1,3},{2,0},{3,1},{4,6},{5,7},{6,4},{7,5},{8,10},{9,11},{10,... | collective-permute-start | bytes 3145736 | tf_op jit(solution)/shard_map/ppermute | solution.py:33
  72.1 24.6 %collective-permute-start.9 = (bf16[2,1,2,1,128,1024]{5,4,3,2,1,0:T(8,128)(2,1)}, bf16[2,1,2,1,128,1024]{5,4,3,2,1,0:T(8,128)(2,1)}, u32[]{:S(2)}, u32[]{:S(2)}) collective-permute-start(bf16[2,1,2,1,128,1024]{5,4,3,2,1,0:T(8,128)(2,1)} %constant_dynamic-update-slice_fusion.68), channel_id=1, source_target_pairs={{0,4},{4,0},{8,12},{12,8},{1,5},{5,1},{9,13},{13,9},{2,6},{6,2},{1... | collective-permute-start | bytes 3145736 | tf_op jit(solution)/shard_map/ppermute | solution.py:33
  77.1 47.0 %collective-permute-start.15 = (bf16[1024,1024]{1,0:T(8,128)(2,1)}, bf16[1024,1024]{1,0:T(8,128)(2,1)}, u32[]{:S(2)}, u32[]{:S(2)}) collective-permute-start(bf16[1024,1024]{1,0:T(8,128)(2,1)} %bitcast.65), channel_id=1, source_target_pairs={{0,16},{16,0},{1,17},{17,1},{2,18},{18,2},{3,19},{19,3},{4,20},{20... | collective-permute-start | bytes 6291464 | tf_op jit(solution)/shard_map/ppermute | solution.py:78
  81.4 54.4 %collective-permute-start.5 = (bf16[2,2,2,1,128,1024]{5,4,3,2,1,0:T(8,128)(2,1)S(1)}, bf16[2,2,2,1,128,1024]{5,4,3,2,1,0:T(8,128)(2,1)}, u32[]{:S(2)}, u32[]{:S(2)}) collective-permute-start(bf16[2,2,2,1,128,1024]{5,4,3,2,1,0:T(8,128)(2,1)S(1)} %constant_dynamic-update-slice_fusion.74), channel_id=1, source_target_pairs={{0,1},{1,0},{2,3},{3,2},{4,5},{5,4},{6,7},{7,6},{8,9},{9,8},{10,11... | collective-permute-start | bytes 6291464 | tf_op jit(solution)/shard_map/ppermute | solution.py:33
  99.0 43.3 %collective-permute-start.10 = (bf16[2,2,2,1,128,1024]{5,4,3,2,1,0:T(8,128)(2,1)}, bf16[2,2,2,1,128,1024]{5,4,3,2,1,0:T(8,128)(2,1)}, u32[]{:S(2)}, u32[]{:S(2)}) collective-permute-start(bf16[2,2,2,1,128,1024]{5,4,3,2,1,0:T(8,128)(2,1)} %constant_dynamic-update-slice_fusion.66), channel_id=1, source_target_pairs={{0,1},{1,0},{2,3},{3,2},{4,5},{5,4},{6,7},{7,6},{8,9},{9,8},{10,11... | collective-permute-start | bytes 6291464 | tf_op jit(solution)/shard_map/ppermute | solution.py:33
  103.8 35.2 %all-to-all-start = ((bf16[16,64,128]{2,1,0:T(8,128)(2,1)}), bf16[16,64,128]{2,1,0:T(8,128)(2,1)S(1)}, u32[]{:S(2)}, u32[]{:S(2)}) async-start(bf16[16,64,128]{2,1,0:T(8,128)(2,1)} %bitcast.3), calls=%async_computation | async-start | bytes 524288 | tf_op jit(solution)/shard_map/all_to_all | solution.py:177
  135.3 91.0 %collective-permute-start.20 = (bf16[1024,2048]{1,0:T(8,128)(2,1)}, bf16[1024,2048]{1,0:T(8,128)(2,1)}, u32[]{:S(2)}, u32[]{:S(2)}) collective-permute-start(bf16[1024,2048]{1,0:T(8,128)(2,1)} %reshape.416), channel_id=1, source_target_pairs={{0,16},{16,0},{1,17},{17,1},{2,18},{18,2},{3,19},{19,3},{4,20},{20... | collective-permute-start | bytes 12582920 | tf_op jit(solution)/shard_map/ppermute | solution.py:78
  155.0 9.3 %collective-permute-start.12 = (bf16[2,1,1,1,64,1024]{5,4,3,2,1,0:T(8,128)(2,1)S(1)}, bf16[2,1,1,1,64,1024]{5,4,3,2,1,0:T(8,128)(2,1)S(1)}, u32[]{:S(2)}, u32[]{:S(2)}) collective-permute-start(bf16[2,1,1,1,64,1024]{5,4,3,2,1,0:T(8,128)(2,1)S(1)} %constant_dynamic-update-slice_fusion.62), channel_id=1, source_target_pairs={{0,4},{4,0},{8,12},{12,8},{1,5},{5,1},{9,13},{13,9},{2,6},{6,2},{1... | collective-permute-start | bytes 786440 | tf_op jit(solution)/shard_map/ppermute | solution.py:33
  156.5 11.4 %collective-permute-start.17 = (bf16[1,1,2,1,64,1024]{5,4,3,2,1,0:T(8,128)(2,1)S(1)}, bf16[1,1,2,1,64,1024]{5,4,3,2,1,0:T(8,128)(2,1)S(1)}, u32[]{:S(2)}, u32[]{:S(2)}) collective-permute-start(bf16[1,1,2,1,64,1024]{5,4,3,2,1,0:T(8,128)(2,1)S(1)} %constant_dynamic-update-slice_fusion.54), channel_id=1, source_target_pairs={{0,8},{4,12},{8,0},{12,4},{1,9},{5,13},{9,1},{13,5},{2,10},{6,14},... | collective-permute-start | bytes 786440 | tf_op jit(solution)/shard_map/ppermute | solution.py:33
  164.3 9.2 %collective-permute-start.13 = (bf16[2,2,1,1,64,1024]{5,4,3,2,1,0:T(8,128)(2,1)S(1)}, bf16[2,2,1,1,64,1024]{5,4,3,2,1,0:T(8,128)(2,1)S(1)}, u32[]{:S(2)}, u32[]{:S(2)}) collective-permute-start(bf16[2,2,1,1,64,1024]{5,4,3,2,1,0:T(8,128)(2,1)S(1)} %constant_dynamic-update-slice_fusion.60), channel_id=1, source_target_pairs={{0,2},{1,3},{2,0},{3,1},{4,6},{5,7},{6,4},{7,5},{8,10},{9,11},{10,... | collective-permute-start | bytes 1572872 | tf_op jit(solution)/shard_map/ppermute | solution.py:33
  168.0 10.6 %collective-permute-start.18 = (bf16[2,1,2,1,64,1024]{5,4,3,2,1,0:T(8,128)(2,1)S(1)}, bf16[2,1,2,1,64,1024]{5,4,3,2,1,0:T(8,128)(2,1)S(1)}, u32[]{:S(2)}, u32[]{:S(2)}) collective-permute-start(bf16[2,1,2,1,64,1024]{5,4,3,2,1,0:T(8,128)(2,1)S(1)} %constant_dynamic-update-slice_fusion.52), channel_id=1, source_target_pairs={{0,4},{4,0},{8,12},{12,8},{1,5},{5,1},{9,13},{13,9},{2,6},{6,2},{1... | collective-permute-start | bytes 1572872 | tf_op jit(solution)/shard_map/ppermute | solution.py:33
  173.6 11.9 %collective-permute-start.14 = (bf16[2,2,2,1,64,1024]{5,4,3,2,1,0:T(8,128)(2,1)S(1)}, bf16[2,2,2,1,64,1024]{5,4,3,2,1,0:T(8,128)(2,1)S(1)}, u32[]{:S(2)}, u32[]{:S(2)}) collective-permute-start(bf16[2,2,2,1,64,1024]{5,4,3,2,1,0:T(8,128)(2,1)S(1)} %constant_dynamic-update-slice_fusion.58), channel_id=1, source_target_pairs={{0,1},{1,0},{2,3},{3,2},{4,5},{5,4},{6,7},{7,6},{8,9},{9,8},{10,11... | collective-permute-start | bytes 3145736 | tf_op jit(solution)/shard_map/ppermute | solution.py:33
  255.5 28.1 %collective-permute-start.21 = (bf16[2,2,2,1,64,1024]{5,4,3,2,1,0:T(8,128)(2,1)S(1)}, bf16[2,2,2,1,64,1024]{5,4,3,2,1,0:T(8,128)(2,1)S(1)}, u32[]{:S(2)}, u32[]{:S(2)}) collective-permute-start(bf16[2,2,2,1,64,1024]{5,4,3,2,1,0:T(8,128)(2,1)S(1)} %constant_dynamic-slice_fusion.24), channel_id=1, source_target_pairs={{0,1},{1,0},{2,3},{3,2},{4,5},{5,4},{6,7},{7,6},{8,9},{9,8},{10,11... | collective-permute-start | bytes 3145736 | tf_op jit(solution)/shard_map/ppermute | solution.py:33
  261.2 24.4 %collective-permute-start.25 = (bf16[2,2,2,1,64,1024]{5,4,3,2,1,0:T(8,128)(2,1)S(1)}, bf16[2,2,2,1,64,1024]{5,4,3,2,1,0:T(8,128)(2,1)S(1)}, u32[]{:S(2)}, u32[]{:S(2)}) collective-permute-start(bf16[2,2,2,1,64,1024]{5,4,3,2,1,0:T(8,128)(2,1)S(1)} %constant_dynamic-slice_fusion.20), channel_id=1, source_target_pairs={{0,1},{1,0},{2,3},{3,2},{4,5},{5,4},{6,7},{7,6},{8,9},{9,8},{10,11... | collective-permute-start | bytes 3145736 | tf_op jit(solution)/shard_map/ppermute | solution.py:33
  276.5 11.1 %collective-permute-start.41 = (bf16[2,2,2,1,64,1024]{5,4,3,2,1,0:T(8,128)(2,1)S(1)}, bf16[2,2,2,1,64,1024]{5,4,3,2,1,0:T(8,128)(2,1)S(1)}, u32[]{:S(2)}, u32[]{:S(2)}) collective-permute-start(bf16[2,2,2,1,64,1024]{5,4,3,2,1,0:T(8,128)(2,1)S(1)} %constant_dynamic-slice_fusion.12), channel_id=1, source_target_pairs={{0,1},{1,0},{2,3},{3,2},{4,5},{5,4},{6,7},{7,6},{8,9},{9,8},{10,11... | collective-permute-start | bytes 3145736 | tf_op jit(solution)/shard_map/ppermute | solution.py:33
  284.1 14.9 %collective-permute-start.22 = (bf16[2,2,1,1,64,1024]{5,4,3,2,1,0:T(8,128)(2,1)S(1)}, bf16[2,2,1,1,64,1024]{5,4,3,2,1,0:T(8,128)(2,1)S(1)}, u32[]{:S(2)}, u32[]{:S(2)}) collective-permute-start(bf16[2,2,1,1,64,1024]{5,4,3,2,1,0:T(8,128)(2,1)S(1)} %constant_dynamic-slice_fusion.23), channel_id=1, source_target_pairs={{0,2},{1,3},{2,0},{3,1},{4,6},{5,7},{6,4},{7,5},{8,10},{9,11},{10,... | collective-permute-start | bytes 1572872 | tf_op jit(solution)/shard_map/ppermute | solution.py:33
  286.1 14.9 %collective-permute-start.26 = (bf16[2,1,2,1,64,1024]{5,4,3,2,1,0:T(8,128)(2,1)S(1)}, bf16[2,1,2,1,64,1024]{5,4,3,2,1,0:T(8,128)(2,1)S(1)}, u32[]{:S(2)}, u32[]{:S(2)}) collective-permute-start(bf16[2,1,2,1,64,1024]{5,4,3,2,1,0:T(8,128)(2,1)S(1)} %constant_dynamic-slice_fusion.19), channel_id=1, source_target_pairs={{0,4},{4,0},{8,12},{12,8},{1,5},{5,1},{9,13},{13,9},{2,6},{6,2},{1... | collective-permute-start | bytes 1572872 | tf_op jit(solution)/shard_map/ppermute | solution.py:33
  288.1 29.8 %collective-permute-start.42 = (bf16[2,1,2,1,64,1024]{5,4,3,2,1,0:T(8,128)(2,1)S(1)}, bf16[2,1,2,1,64,1024]{5,4,3,2,1,0:T(8,128)(2,1)S(1)}, u32[]{:S(2)}, u32[]{:S(2)}) collective-permute-start(bf16[2,1,2,1,64,1024]{5,4,3,2,1,0:T(8,128)(2,1)S(1)} %constant_dynamic-slice_fusion.11), channel_id=1, source_target_pairs={{0,4},{4,0},{8,12},{12,8},{1,5},{5,1},{9,13},{13,9},{2,6},{6,2},{1... | collective-permute-start | bytes 1572872 | tf_op jit(solution)/shard_map/ppermute | solution.py:33
  289.2 29.4 %collective-permute-start.38 = (bf16[2,2,1,1,64,1024]{5,4,3,2,1,0:T(8,128)(2,1)S(1)}, bf16[2,2,1,1,64,1024]{5,4,3,2,1,0:T(8,128)(2,1)S(1)}, u32[]{:S(2)}, u32[]{:S(2)}) collective-permute-start(bf16[2,2,1,1,64,1024]{5,4,3,2,1,0:T(8,128)(2,1)S(1)} %constant_dynamic-slice_fusion.15), channel_id=1, source_target_pairs={{0,2},{1,3},{2,0},{3,1},{4,6},{5,7},{6,4},{7,5},{8,10},{9,11},{10,... | collective-permute-start | bytes 1572872 | tf_op jit(solution)/shard_map/ppermute | solution.py:33
  299.2 24.6 %collective-permute-start.23 = (bf16[2,1,1,1,64,1024]{5,4,3,2,1,0:T(8,128)(2,1)S(1)}, bf16[2,1,1,1,64,1024]{5,4,3,2,1,0:T(8,128)(2,1)S(1)}, u32[]{:S(2)}, u32[]{:S(2)}) collective-permute-start(bf16[2,1,1,1,64,1024]{5,4,3,2,1,0:T(8,128)(2,1)S(1)} %constant_dynamic-slice_fusion.22), channel_id=1, source_target_pairs={{0,4},{4,0},{8,12},{12,8},{1,5},{5,1},{9,13},{13,9},{2,6},{6,2},{1... | collective-permute-start | bytes 786440 | tf_op jit(solution)/shard_map/ppermute | solution.py:33
  301.2 23.0 %collective-permute-start.27 = (bf16[1,1,2,1,64,1024]{5,4,3,2,1,0:T(8,128)(2,1)S(1)}, bf16[1,1,2,1,64,1024]{5,4,3,2,1,0:T(8,128)(2,1)S(1)}, u32[]{:S(2)}, u32[]{:S(2)}) collective-permute-start(bf16[1,1,2,1,64,1024]{5,4,3,2,1,0:T(8,128)(2,1)S(1)} %constant_dynamic-slice_fusion.18), channel_id=1, source_target_pairs={{0,8},{4,12},{8,0},{12,4},{1,9},{5,13},{9,1},{13,5},{2,10},{6,14},... | collective-permute-start | bytes 786440 | tf_op jit(solution)/shard_map/ppermute | solution.py:33
  318.1 18.5 %collective-permute-start.43 = (bf16[1,1,2,1,64,1024]{5,4,3,2,1,0:T(8,128)(2,1)S(1)}, bf16[1,1,2,1,64,1024]{5,4,3,2,1,0:T(8,128)(2,1)S(1)}, u32[]{:S(2)}, u32[]{:S(2)}) collective-permute-start(bf16[1,1,2,1,64,1024]{5,4,3,2,1,0:T(8,128)(2,1)S(1)} %constant_dynamic-slice_fusion.10), channel_id=1, source_target_pairs={{0,8},{4,12},{8,0},{12,4},{1,9},{5,13},{9,1},{13,5},{2,10},{6,14},... | collective-permute-start | bytes 786440 | tf_op jit(solution)/shard_map/ppermute | solution.py:33
  318.9 18.4 %collective-permute-start.39 = (bf16[2,1,1,1,64,1024]{5,4,3,2,1,0:T(8,128)(2,1)S(1)}, bf16[2,1,1,1,64,1024]{5,4,3,2,1,0:T(8,128)(2,1)S(1)}, u32[]{:S(2)}, u32[]{:S(2)}) collective-permute-start(bf16[2,1,1,1,64,1024]{5,4,3,2,1,0:T(8,128)(2,1)S(1)} %constant_dynamic-slice_fusion.14), channel_id=1, source_target_pairs={{0,4},{4,0},{8,12},{12,8},{1,5},{5,1},{9,13},{13,9},{2,6},{6,2},{1... | collective-permute-start | bytes 786440 | tf_op jit(solution)/shard_map/ppermute | solution.py:33
  323.8 19.9 %collective-permute-start.24 = (bf16[1,1,1,1,64,1024]{5,4,3,2,1,0:T(8,128)(2,1)S(1)}, bf16[1,1,1,1,64,1024]{5,4,3,2,1,0:T(8,128)(2,1)S(1)}, u32[]{:S(2)}, u32[]{:S(2)}) collective-permute-start(bf16[1,1,1,1,64,1024]{5,4,3,2,1,0:T(8,128)(2,1)S(1)} %constant_dynamic-slice_fusion.21), channel_id=1, source_target_pairs={{0,8},{4,12},{8,0},{12,4},{1,9},{5,13},{9,1},{13,5},{2,10},{6,14},... | collective-permute-start | bytes 393224 | tf_op jit(solution)/shard_map/ppermute | solution.py:33
  324.3 20.0 %collective-permute-start.28 = (bf16[1,1,1,1,64,1024]{5,4,3,2,1,0:T(8,128)(2,1)S(1)}, bf16[1,1,1,1,64,1024]{5,4,3,2,1,0:T(8,128)(2,1)S(1)}, u32[]{:S(2)}, u32[]{:S(2)}) collective-permute-start(bf16[1,1,1,1,64,1024]{5,4,3,2,1,0:T(8,128)(2,1)S(1)} %constant_dynamic-slice_fusion.17), channel_id=1, source_target_pairs={{0,2},{1,3},{2,0},{3,1},{4,6},{5,7},{6,4},{7,5},{8,10},{9,11},{10,... | collective-permute-start | bytes 393224 | tf_op jit(solution)/shard_map/ppermute | solution.py:33
  337.4 8.9 %collective-permute-start.40 = (bf16[1,1,1,1,64,1024]{5,4,3,2,1,0:T(8,128)(2,1)S(1)}, bf16[1,1,1,1,64,1024]{5,4,3,2,1,0:T(8,128)(2,1)S(1)}, u32[]{:S(2)}, u32[]{:S(2)}) collective-permute-start(bf16[1,1,1,1,64,1024]{5,4,3,2,1,0:T(8,128)(2,1)S(1)} %constant_dynamic-slice_fusion.13), channel_id=1, source_target_pairs={{0,8},{4,12},{8,0},{12,4},{1,9},{5,13},{9,1},{13,5},{2,10},{6,14},... | collective-permute-start | bytes 393224 | tf_op jit(solution)/shard_map/ppermute | solution.py:33
  341.2 340.7 %collective-permute-start.71 = (bf16[1024,2048]{1,0:T(8,128)(2,1)}, bf16[1024,2048]{1,0:T(8,128)(2,1)}, u32[]{:S(2)}, u32[]{:S(2)}) collective-permute-start(bf16[1024,2048]{1,0:T(8,128)(2,1)} %convolution_convert_fusion), channel_id=1, source_target_pairs={{0,16},{16,0},{1,17},{17,1},{2,18},{18,2},{3,19},{19,3},{4,20},{20... | collective-permute-start | bytes 12582920 | tf_op jit(solution)/shard_map/ppermute | solution.py:78
  343.8 134.0 %collective-permute-start.72 = (bf16[1024,1024]{0,1:T(8,128)(2,1)}, bf16[1024,1024]{0,1:T(8,128)(2,1)}, u32[]{:S(2)}, u32[]{:S(2)}) collective-permute-start(bf16[1024,1024]{0,1:T(8,128)(2,1)} %convolution_convert_fusion.1), channel_id=1, source_target_pairs={{0,16},{16,0},{1,17},{17,1},{2,18},{18,2},{3,19},{19,3},{4,20},{20... | collective-permute-start | bytes 6291464 | tf_op jit(solution)/shard_map/ppermute | solution.py:78
  351.5 162.8 %all-to-all-start.1 = ((bf16[64,16,128]{2,0,1:T(8,128)(2,1)}), bf16[64,16,128]{2,0,1:T(8,128)(2,1)S(1)}, u32[]{:S(2)}, u32[]{:S(2)}) async-start(bf16[64,16,128]{2,0,1:T(8,128)(2,1)} %bitcast.166), calls=%async_computation.1 | async-start | bytes 524288 | tf_op jit(solution)/shard_map/all_to_all | solution.py:226
  357.2 16.5 %collective-permute-start.62 = (bf16[1,1,1,1,64,1024]{5,4,3,2,1,0:T(8,128)(2,1)S(1)}, bf16[1,1,1,1,64,1024]{5,4,3,2,1,0:T(8,128)(2,1)S(1)}, u32[]{:S(2)}, u32[]{:S(2)}) collective-permute-start(bf16[1,1,1,1,64,1024]{5,4,3,2,1,0:T(8,128)(2,1)S(1)} %get-tuple-element.56), channel_id=1, source_target_pairs={{0,8},{4,12},{8,0},{12,4},{1,9},{5,13},{9,1},{13,5},{2,10},{6,14},... | collective-permute-start | bytes 393224 | tf_op jit(solution)/shard_map/ppermute | solution.py:33
  359.7 22.4 %collective-permute-start.29 = (bf16[1,1,1,1,64,1024]{5,4,3,2,1,0:T(8,128)(2,1)S(1)}, bf16[1,1,1,1,64,1024]{5,4,3,2,1,0:T(8,128)(2,1)S(1)}, u32[]{:S(2)}, u32[]{:S(2)}) collective-permute-start(bf16[1,1,1,1,64,1024]{5,4,3,2,1,0:T(8,128)(2,1)S(1)} %get-tuple-element.80), channel_id=1, source_target_pairs={{0,8},{4,12},{8,0},{12,4},{1,9},{5,13},{9,1},{13,5},{2,10},{6,14},... | collective-permute-start | bytes 393224 | tf_op jit(solution)/shard_map/ppermute | solution.py:33
  363.2 19.0 %collective-permute-start.33 = (bf16[1,1,1,1,64,1024]{5,4,3,2,1,0:T(8,128)(2,1)S(1)}, bf16[1,1,1,1,64,1024]{5,4,3,2,1,0:T(8,128)(2,1)S(1)}, u32[]{:S(2)}, u32[]{:S(2)}) collective-permute-start(bf16[1,1,1,1,64,1024]{5,4,3,2,1,0:T(8,128)(2,1)S(1)} %get-tuple-element.81), channel_id=1, source_target_pairs={{0,2},{1,3},{2,0},{3,1},{4,6},{5,7},{6,4},{7,5},{8,10},{9,11},{10,... | collective-permute-start | bytes 393224 | tf_op jit(solution)/shard_map/ppermute | solution.py:33
  373.7 123.3 %collective-permute-start.67 = (bf16[1,1,2,1,64,1024]{5,4,3,2,1,0:T(8,128)(2,1)S(1)}, bf16[1,1,2,1,64,1024]{5,4,3,2,1,0:T(8,128)(2,1)S(1)}, u32[]{:S(2)}, u32[]{:S(2)}) collective-permute-start(bf16[1,1,2,1,64,1024]{5,4,3,2,1,0:T(8,128)(2,1)S(1)} %constant_dynamic-update-slice_fusion.6), channel_id=1, source_target_pairs={{0,8},{4,12},{8,0},{12,4},{1,9},{5,13},{9,1},{13,5},{2,10},{6,14},... | collective-permute-start | bytes 786440 | tf_op jit(solution)/shard_map/ppermute | solution.py:33
  382.1 115.7 %collective-permute-start.63 = (bf16[2,1,1,1,64,1024]{5,4,3,2,1,0:T(8,128)(2,1)S(1)}, bf16[2,1,1,1,64,1024]{5,4,3,2,1,0:T(8,128)(2,1)S(1)}, u32[]{:S(2)}, u32[]{:S(2)}) collective-permute-start(bf16[2,1,1,1,64,1024]{5,4,3,2,1,0:T(8,128)(2,1)S(1)} %constant_dynamic-update-slice_fusion.14), channel_id=1, source_target_pairs={{0,4},{4,0},{8,12},{12,8},{1,5},{5,1},{9,13},{13,9},{2,6},{6,2},{1... | collective-permute-start | bytes 786440 | tf_op jit(solution)/shard_map/ppermute | solution.py:33
  382.1 117.9 %collective-permute-start.30 = (bf16[2,1,1,1,64,1024]{5,4,3,2,1,0:T(8,128)(2,1)S(1)}, bf16[2,1,1,1,64,1024]{5,4,3,2,1,0:T(8,128)(2,1)S(1)}, u32[]{:S(2)}, u32[]{:S(2)}) collective-permute-start(bf16[2,1,1,1,64,1024]{5,4,3,2,1,0:T(8,128)(2,1)S(1)} %constant_dynamic-update-slice_fusion.46), channel_id=1, source_target_pairs={{0,4},{4,0},{8,12},{12,8},{1,5},{5,1},{9,13},{13,9},{2,6},{6,2},{1... | collective-permute-start | bytes 786440 | tf_op jit(solution)/shard_map/ppermute | solution.py:33
  477.8 23.6 %collective-permute-start.34 = (bf16[1,1,2,1,64,1024]{5,4,3,2,1,0:T(8,128)(2,1)S(1)}, bf16[1,1,2,1,64,1024]{5,4,3,2,1,0:T(8,128)(2,1)S(1)}, u32[]{:S(2)}, u32[]{:S(2)}) collective-permute-start(bf16[1,1,2,1,64,1024]{5,4,3,2,1,0:T(8,128)(2,1)S(1)} %constant_dynamic-update-slice_fusion.38), channel_id=1, source_target_pairs={{0,8},{4,12},{8,0},{12,4},{1,9},{5,13},{9,1},{13,5},{2,10},{6,14},... | collective-permute-start | bytes 786440 | tf_op jit(solution)/shard_map/ppermute | solution.py:33
  497.8 74.6 %collective-permute-start.68 = (bf16[2,1,2,1,64,1024]{5,4,3,2,1,0:T(8,128)(2,1)}, bf16[2,1,2,1,64,1024]{5,4,3,2,1,0:T(8,128)(2,1)}, u32[]{:S(2)}, u32[]{:S(2)}) collective-permute-start(bf16[2,1,2,1,64,1024]{5,4,3,2,1,0:T(8,128)(2,1)} %constant_dynamic-update-slice_fusion.4), channel_id=1, source_target_pairs={{0,4},{4,0},{8,12},{12,8},{1,5},{5,1},{9,13},{13,9},{2,6},{6,2},{1... | collective-permute-start | bytes 1572872 | tf_op jit(solution)/shard_map/ppermute | solution.py:33
  498.6 77.3 %collective-permute-start.64 = (bf16[2,2,1,1,64,1024]{5,4,3,2,1,0:T(8,128)(2,1)}, bf16[2,2,1,1,64,1024]{5,4,3,2,1,0:T(8,128)(2,1)}, u32[]{:S(2)}, u32[]{:S(2)}) collective-permute-start(bf16[2,2,1,1,64,1024]{5,4,3,2,1,0:T(8,128)(2,1)} %constant_dynamic-update-slice_fusion.12), channel_id=1, source_target_pairs={{0,2},{1,3},{2,0},{3,1},{4,6},{5,7},{6,4},{7,5},{8,10},{9,11},{10,... | collective-permute-start | bytes 1572872 | tf_op jit(solution)/shard_map/ppermute | solution.py:33
  500.8 77.2 %collective-permute-start.31 = (bf16[2,2,1,1,64,1024]{5,4,3,2,1,0:T(8,128)(2,1)}, bf16[2,2,1,1,64,1024]{5,4,3,2,1,0:T(8,128)(2,1)}, u32[]{:S(2)}, u32[]{:S(2)}) collective-permute-start(bf16[2,2,1,1,64,1024]{5,4,3,2,1,0:T(8,128)(2,1)} %constant_dynamic-update-slice_fusion.44), channel_id=1, source_target_pairs={{0,2},{1,3},{2,0},{3,1},{4,6},{5,7},{6,4},{7,5},{8,10},{9,11},{10,... | collective-permute-start | bytes 1572872 | tf_op jit(solution)/shard_map/ppermute | solution.py:33
  502.1 80.5 %collective-permute-start.35 = (bf16[2,1,2,1,64,1024]{5,4,3,2,1,0:T(8,128)(2,1)}, bf16[2,1,2,1,64,1024]{5,4,3,2,1,0:T(8,128)(2,1)}, u32[]{:S(2)}, u32[]{:S(2)}) collective-permute-start(bf16[2,1,2,1,64,1024]{5,4,3,2,1,0:T(8,128)(2,1)} %constant_dynamic-update-slice_fusion.36), channel_id=1, source_target_pairs={{0,4},{4,0},{8,12},{12,8},{1,5},{5,1},{9,13},{13,9},{2,6},{6,2},{1... | collective-permute-start | bytes 1572872 | tf_op jit(solution)/shard_map/ppermute | solution.py:33
  572.4 19.1 %collective-permute-start.61 = (bf16[1024,384]{0,1:T(8,128)(2,1)S(1)}, bf16[1024,384]{0,1:T(8,128)(2,1)S(1)}, u32[]{:S(2)}, u32[]{:S(2)}) collective-permute-start(bf16[1024,384]{0,1:T(8,128)(2,1)S(1)} %convolution_convert_fusion.6), channel_id=1, source_target_pairs={{0,16},{16,0},{1,17},{17,1},{2,18},{18,2},{3,19},{19,3},{4,20},{20... | collective-permute-start | bytes 2359304 | tf_op jit(solution)/shard_map/ppermute | solution.py:78
  575.9 21.0 %collective-permute-start.45 = (bf16[2,2,2,1,64,1024]{5,4,3,2,1,0:T(8,128)(2,1)}, bf16[2,2,2,1,64,1024]{5,4,3,2,1,0:T(8,128)(2,1)}, u32[]{:S(2)}, u32[]{:S(2)}) collective-permute-start(bf16[2,2,2,1,64,1024]{5,4,3,2,1,0:T(8,128)(2,1)} %constant_dynamic-slice_fusion.8), channel_id=1, source_target_pairs={{0,1},{1,0},{2,3},{3,2},{4,5},{5,4},{6,7},{7,6},{8,9},{9,8},{10,11... | collective-permute-start | bytes 3145736 | tf_op jit(solution)/shard_map/ppermute | solution.py:33
  578.0 21.5 %collective-permute-start.49 = (bf16[2,2,2,1,64,1024]{5,4,3,2,1,0:T(8,128)(2,1)}, bf16[2,2,2,1,64,1024]{5,4,3,2,1,0:T(8,128)(2,1)}, u32[]{:S(2)}, u32[]{:S(2)}) collective-permute-start(bf16[2,2,2,1,64,1024]{5,4,3,2,1,0:T(8,128)(2,1)} %constant_dynamic-slice_fusion.4), channel_id=1, source_target_pairs={{0,1},{1,0},{2,3},{3,2},{4,5},{5,4},{6,7},{7,6},{8,9},{9,8},{10,11... | collective-permute-start | bytes 3145736 | tf_op jit(solution)/shard_map/ppermute | solution.py:33
  582.5 20.4 %collective-permute-start.69 = (bf16[2,2,2,1,64,1024]{5,4,3,2,1,0:T(8,128)(2,1)S(1)}, bf16[2,2,2,1,64,1024]{5,4,3,2,1,0:T(8,128)(2,1)}, u32[]{:S(2)}, u32[]{:S(2)}) collective-permute-start(bf16[2,2,2,1,64,1024]{5,4,3,2,1,0:T(8,128)(2,1)S(1)} %constant_dynamic-update-slice_fusion.2), channel_id=1, source_target_pairs={{0,1},{1,0},{2,3},{3,2},{4,5},{5,4},{6,7},{7,6},{8,9},{9,8},{10,11... | collective-permute-start | bytes 3145736 | tf_op jit(solution)/shard_map/ppermute | solution.py:33
  591.5 80.3 %collective-permute-start.65 = (bf16[2,2,2,1,64,1024]{5,4,3,2,1,0:T(8,128)(2,1)}, bf16[2,2,2,1,64,1024]{5,4,3,2,1,0:T(8,128)(2,1)}, u32[]{:S(2)}, u32[]{:S(2)}) collective-permute-start(bf16[2,2,2,1,64,1024]{5,4,3,2,1,0:T(8,128)(2,1)} %constant_dynamic-update-slice_fusion.10), channel_id=1, source_target_pairs={{0,1},{1,0},{2,3},{3,2},{4,5},{5,4},{6,7},{7,6},{8,9},{9,8},{10,11... | collective-permute-start | bytes 3145736 | tf_op jit(solution)/shard_map/ppermute | solution.py:33
  596.8 11.5 %collective-permute-start.32 = (bf16[2,2,2,1,64,1024]{5,4,3,2,1,0:T(8,128)(2,1)}, bf16[2,2,2,1,64,1024]{5,4,3,2,1,0:T(8,128)(2,1)S(1)}, u32[]{:S(2)}, u32[]{:S(2)}) collective-permute-start(bf16[2,2,2,1,64,1024]{5,4,3,2,1,0:T(8,128)(2,1)} %constant_dynamic-update-slice_fusion.42), channel_id=1, source_target_pairs={{0,1},{1,0},{2,3},{3,2},{4,5},{5,4},{6,7},{7,6},{8,9},{9,8},{10,11... | collective-permute-start | bytes 3145736 | tf_op jit(solution)/shard_map/ppermute | solution.py:33
  599.5 13.9 %collective-permute-start.46 = (bf16[2,2,1,1,64,1024]{5,4,3,2,1,0:T(8,128)(2,1)S(1)}, bf16[2,2,1,1,64,1024]{5,4,3,2,1,0:T(8,128)(2,1)S(1)}, u32[]{:S(2)}, u32[]{:S(2)}) collective-permute-start(bf16[2,2,1,1,64,1024]{5,4,3,2,1,0:T(8,128)(2,1)S(1)} %constant_dynamic-slice_fusion.7), channel_id=1, source_target_pairs={{0,2},{1,3},{2,0},{3,1},{4,6},{5,7},{6,4},{7,5},{8,10},{9,11},{10,... | collective-permute-start | bytes 1572872 | tf_op jit(solution)/shard_map/ppermute | solution.py:33
  603.0 14.0 %collective-permute-start.50 = (bf16[2,1,2,1,64,1024]{5,4,3,2,1,0:T(8,128)(2,1)S(1)}, bf16[2,1,2,1,64,1024]{5,4,3,2,1,0:T(8,128)(2,1)S(1)}, u32[]{:S(2)}, u32[]{:S(2)}) collective-permute-start(bf16[2,1,2,1,64,1024]{5,4,3,2,1,0:T(8,128)(2,1)S(1)} %constant_dynamic-slice_fusion.3), channel_id=1, source_target_pairs={{0,4},{4,0},{8,12},{12,8},{1,5},{5,1},{9,13},{13,9},{2,6},{6,2},{1... | collective-permute-start | bytes 1572872 | tf_op jit(solution)/shard_map/ppermute | solution.py:33
  608.3 29.1 %collective-permute-start.36 = (bf16[2,2,2,1,64,1024]{5,4,3,2,1,0:T(8,128)(2,1)}, bf16[2,2,2,1,64,1024]{5,4,3,2,1,0:T(8,128)(2,1)S(1)}, u32[]{:S(2)}, u32[]{:S(2)}) collective-permute-start(bf16[2,2,2,1,64,1024]{5,4,3,2,1,0:T(8,128)(2,1)} %constant_dynamic-update-slice_fusion.34), channel_id=1, source_target_pairs={{0,1},{1,0},{2,3},{3,2},{4,5},{5,4},{6,7},{7,6},{8,9},{9,8},{10,11... | collective-permute-start | bytes 3145736 | tf_op jit(solution)/shard_map/ppermute | solution.py:33
  613.4 88.3 %collective-permute-start.70 = (bf16[1024,128]{1,0:T(8,128)(2,1)S(1)}, bf16[1024,128]{1,0:T(8,128)(2,1)}, u32[]{:S(2)}, u32[]{:S(2)}) collective-permute-start(bf16[1024,128]{1,0:T(8,128)(2,1)S(1)} %convolution_convert_fusion.7), channel_id=1, source_target_pairs={{0,16},{16,0},{1,17},{17,1},{2,18},{18,2},{3,19},{19,3},{4,20},{20... | collective-permute-start | bytes 786440 | tf_op jit(solution)/shard_map/ppermute | solution.py:78
  624.4 13.0 %collective-permute-start.51 = (bf16[1,1,2,1,64,1024]{5,4,3,2,1,0:T(8,128)(2,1)S(1)}, bf16[1,1,2,1,64,1024]{5,4,3,2,1,0:T(8,128)(2,1)S(1)}, u32[]{:S(2)}, u32[]{:S(2)}) collective-permute-start(bf16[1,1,2,1,64,1024]{5,4,3,2,1,0:T(8,128)(2,1)S(1)} %constant_dynamic-slice_fusion.2), channel_id=1, source_target_pairs={{0,8},{4,12},{8,0},{12,4},{1,9},{5,13},{9,1},{13,5},{2,10},{6,14},... | collective-permute-start | bytes 786440 | tf_op jit(solution)/shard_map/ppermute | solution.py:33
  645.7 8.5 %collective-permute-start.53 = (bf16[1,1,1,1,64,1024]{5,4,3,2,1,0:T(8,128)(2,1)S(1)}, bf16[1,1,1,1,64,1024]{5,4,3,2,1,0:T(8,128)(2,1)S(1)}, u32[]{:S(2)}, u32[]{:S(2)}) collective-permute-start(bf16[1,1,1,1,64,1024]{5,4,3,2,1,0:T(8,128)(2,1)S(1)} %get-tuple-element.74), channel_id=1, source_target_pairs={{0,8},{4,12},{8,0},{12,4},{1,9},{5,13},{9,1},{13,5},{2,10},{6,14},... | collective-permute-start | bytes 393224 | tf_op jit(solution)/shard_map/ppermute | solution.py:33
  654.2 13.1 %collective-permute-start.54 = (bf16[2,1,1,1,64,1024]{5,4,3,2,1,0:T(8,128)(2,1)S(1)}, bf16[2,1,1,1,64,1024]{5,4,3,2,1,0:T(8,128)(2,1)S(1)}, u32[]{:S(2)}, u32[]{:S(2)}) collective-permute-start(bf16[2,1,1,1,64,1024]{5,4,3,2,1,0:T(8,128)(2,1)S(1)} %constant_dynamic-update-slice_fusion.30), channel_id=1, source_target_pairs={{0,4},{4,0},{8,12},{12,8},{1,5},{5,1},{9,13},{13,9},{2,6},{6,2},{1... | collective-permute-start | bytes 786440 | tf_op jit(solution)/shard_map/ppermute | solution.py:33
  654.3 14.9 %collective-permute-start.58 = (bf16[1,1,2,1,64,1024]{5,4,3,2,1,0:T(8,128)(2,1)S(1)}, bf16[1,1,2,1,64,1024]{5,4,3,2,1,0:T(8,128)(2,1)S(1)}, u32[]{:S(2)}, u32[]{:S(2)}) collective-permute-start(bf16[1,1,2,1,64,1024]{5,4,3,2,1,0:T(8,128)(2,1)S(1)} %constant_dynamic-update-slice_fusion.22), channel_id=1, source_target_pairs={{0,8},{4,12},{8,0},{12,4},{1,9},{5,13},{9,1},{13,5},{2,10},{6,14},... | collective-permute-start | bytes 786440 | tf_op jit(solution)/shard_map/ppermute | solution.py:33
  667.3 13.1 %collective-permute-start.55 = (bf16[2,2,1,1,64,1024]{5,4,3,2,1,0:T(8,128)(2,1)S(1)}, bf16[2,2,1,1,64,1024]{5,4,3,2,1,0:T(8,128)(2,1)S(1)}, u32[]{:S(2)}, u32[]{:S(2)}) collective-permute-start(bf16[2,2,1,1,64,1024]{5,4,3,2,1,0:T(8,128)(2,1)S(1)} %constant_dynamic-update-slice_fusion.28), channel_id=1, source_target_pairs={{0,2},{1,3},{2,0},{3,1},{4,6},{5,7},{6,4},{7,5},{8,10},{9,11},{10,... | collective-permute-start | bytes 1572872 | tf_op jit(solution)/shard_map/ppermute | solution.py:33
  669.2 11.3 %collective-permute-start.59 = (bf16[2,1,2,1,64,1024]{5,4,3,2,1,0:T(8,128)(2,1)S(1)}, bf16[2,1,2,1,64,1024]{5,4,3,2,1,0:T(8,128)(2,1)S(1)}, u32[]{:S(2)}, u32[]{:S(2)}) collective-permute-start(bf16[2,1,2,1,64,1024]{5,4,3,2,1,0:T(8,128)(2,1)S(1)} %constant_dynamic-update-slice_fusion.20), channel_id=1, source_target_pairs={{0,4},{4,0},{8,12},{12,8},{1,5},{5,1},{9,13},{13,9},{2,6},{6,2},{1... | collective-permute-start | bytes 1572872 | tf_op jit(solution)/shard_map/ppermute | solution.py:33
  680.4 25.8 %collective-permute-start.56 = (bf16[2,2,2,1,64,1024]{5,4,3,2,1,0:T(8,128)(2,1)S(1)}, bf16[2,2,2,1,64,1024]{5,4,3,2,1,0:T(8,128)(2,1)}, u32[]{:S(2)}, u32[]{:S(2)}) collective-permute-start(bf16[2,2,2,1,64,1024]{5,4,3,2,1,0:T(8,128)(2,1)S(1)} %constant_dynamic-update-slice_fusion.26), channel_id=1, source_target_pairs={{0,1},{1,0},{2,3},{3,2},{4,5},{5,4},{6,7},{7,6},{8,9},{9,8},{10,11... | collective-permute-start | bytes 3145736 | tf_op jit(solution)/shard_map/ppermute | solution.py:33
  681.4 26.1 %collective-permute-start.60 = (bf16[2,2,2,1,64,1024]{5,4,3,2,1,0:T(8,128)(2,1)}, bf16[2,2,2,1,64,1024]{5,4,3,2,1,0:T(8,128)(2,1)}, u32[]{:S(2)}, u32[]{:S(2)}) collective-permute-start(bf16[2,2,2,1,64,1024]{5,4,3,2,1,0:T(8,128)(2,1)} %constant_dynamic-update-slice_fusion.18), channel_id=1, source_target_pairs={{0,1},{1,0},{2,3},{3,2},{4,5},{5,4},{6,7},{7,6},{8,9},{9,8},{10,11... | collective-permute-start | bytes 3145736 | tf_op jit(solution)/shard_map/ppermute | solution.py:33
  (79 other events, 1021.4 us)

commit v2 on v1

v2 whole, which is shorter than its diff:
```python
import itertools

import jax
import jax.numpy as jnp
from jax import lax
from jax.experimental import pallas as pl
from jax.experimental.pallas import tpu as pltpu
from jax.sharding import PartitionSpec as P

SEQ_LEN = 1024
EPS = 1e-06
BF = jnp.bfloat16
F32 = jnp.float32
GROUP = ("heads", "tensor")
EVERY = ("fsdp", "heads", "tensor")

STEPS = {
    "core": ("tensor", 1, 0),
    "x": ("tensor", 2, 1),
    "z0": ("heads", 1, 2),
    "z1": ("heads", 2, 3),
}
BITS = (1, 2, 4, 8)
ORDER_A = ("core", "x", "z0", "z1")
ORDER_B = ("core", "z0", "z1", "x")


def dot(a, b, ca=1, cb=0):
    return lax.dot_general(a, b, (((ca,), (cb,)), ((), ())), preferred_element_type=F32)


def after(value, *others):
    return lax.optimization_barrier((value,) + others)[0]


def swap(v, step):
    name, bit, _ = STEPS[step]
    return lax.ppermute(v, name, [(i, i ^ bit) for i in range(lax.axis_size(name))])


def hold(values, *gates):
    return list(lax.optimization_barrier((*values, *gates))[: len(values)])


def reduce_rest(parts, gates=((), (), ()), orders=(ORDER_A, ORDER_B)):
    rows, cols = parts[0].shape
    now = [v.reshape(1, 2, 2, 2, rows // 8, cols) for v in parts]
    sent, after_step = [], []
    for i in range(3):
        now = hold(now, *gates[i])
        steps = [order[i + 1] for order in orders]
        send = [lax.slice_in_dim(v, 1, 2, axis=STEPS[s][2]) for v, s in zip(now, steps)]
        mine = [lax.slice_in_dim(v, 0, 1, axis=STEPS[s][2]) for v, s in zip(now, steps)]
        got = [swap(v, s) for v, s in zip(send, steps)]
        now = [(m.astype(F32) + g.astype(F32)).astype(BF) for m, g in zip(mine, got)]
        sent.append(send)
        after_step.append(now)
    return [v.reshape(rows // 8, cols) for v in now], sent, after_step


def reduce_first(left, rights, *gates):
    half = left.shape[0] // 2
    pair = []
    later = after(left, *gates) if gates else left
    for right in rights:
        got = swap(dot(left[half:], right, 1, 1).astype(BF), "core")
        pair.append((dot(later[:half], right, 1, 1) + got.astype(F32)).astype(BF))
    return pair


def gather_chain(parts, gates=((), (), (), ()), orders=(ORDER_A, ORDER_B), vector=None):
    rows, cols = parts[0].shape
    now = [v.reshape(1, 1, 1, 1, rows, cols) for v in parts]
    stages = []
    for i in range(4):
        now = hold(now, *gates[i], *([] if vector is None else [vector]))
        if vector is not None:
            vector = vector + swap(vector, ORDER_A[i])
        steps = [order[3 - i] for order in orders]
        got = [swap(v, step) for v, step in zip(now, steps)]
        if i < 3:
            now = [
                jnp.concatenate([v, g], axis=STEPS[step][2])
                for v, g, step in zip(now, got, steps)
            ]
            stages.append(now)
    flat_rows = [[v.reshape(8 * rows, cols) for v in pair] for pair in zip(now, got)]
    return flat_rows, stages, vector


def whole(pairs):
    return [jnp.concatenate(pair, axis=0) for pair in pairs]


def reversed_bits(p):
    return sum(((p >> i) & 1) << (3 - i) for i in range(4))


def group_index():
    return lax.axis_index("heads") * lax.axis_size("tensor") + lax.axis_index("tensor")


def reversed_index():
    me = group_index()
    return sum(((me >> i) & 1) << (3 - i) for i in range(4))


def reorder(parts, start, dtype, tile=256, shift=None):
    rows, cols = parts[0].shape
    tile = min(tile, cols)
    per = cols // tile
    count = len(parts)
    block = rows // 16

    def kernel(at, *refs):
        out = refs[-1]
        j = pl.program_id(0)
        for i, part in enumerate(refs[:-1]):

            @pl.when(j // per == i)
            def _(part=part):
                for p in range(16):
                    src = pl.multiple_of((at[0] ^ reversed_bits(p)) * block, block)
                    out[p * block : (p + 1) * block, :] = part[pl.ds(src, block), :].astype(dtype)

    def spec(i):
        def where(j, at):
            k = jnp.clip(j - i * per, 0, per - 1)
            return (0, lax.rem(k + at[1], per))

        return pl.BlockSpec((rows, tile), where)

    at = jnp.stack([start, jnp.int32(0) if shift is None else shift // tile]).astype(jnp.int32)
    return pl.pallas_call(
        kernel,
        grid_spec=pltpu.PrefetchScalarGridSpec(
            num_scalar_prefetch=1,
            grid=(per * count,),
            in_specs=[spec(i) for i in range(count)],
            out_specs=pl.BlockSpec((rows, tile), lambda j, at: (0, j)),
        ),
        out_shape=jax.ShapeDtypeStruct((rows, cols * count), dtype),
        cost_estimate=pl.CostEstimate(
            flops=0, bytes_accessed=rows * cols * count * 8, transcendentals=0
        ),
    )(at, *parts)


VMEM_LIMIT = 48 * 2**20


def indices(shape, order):
    lead = shape[1:-1]
    spots = itertools.product(*[range(lead[i]) for i in order])
    return [tuple(spot[order.index(i)] for i in range(len(lead))) for spot in spots]


def flat(weights, orders):
    rows = min(256, weights[0].shape[0])
    spots = [indices(v.shape, order) for v, order in zip(weights, orders)]
    wide = weights[0].shape[-1]
    columns = sum(len(s) for s in spots) * wide

    def kernel(*refs):
        out, at = refs[-1], 0
        for ref, some in zip(refs, spots):
            for spot in some:
                out[:, at : at + wide] = ref[(slice(None), *spot, slice(None))].astype(BF)
                at += wide

    def spec(v):
        zeros = (0,) * (v.ndim - 1)
        return pl.BlockSpec((rows, *v.shape[1:]), lambda i: (i, *zeros))

    count = weights[0].shape[0]
    return pl.pallas_call(
        kernel,
        grid=(count // rows,),
        in_specs=[spec(v) for v in weights],
        out_specs=pl.BlockSpec((rows, columns), lambda i: (i, 0)),
        out_shape=jax.ShapeDtypeStruct((count, columns), BF),
        compiler_params=pltpu.CompilerParams(vmem_limit_bytes=VMEM_LIMIT),
        cost_estimate=pl.CostEstimate(
            flops=0, bytes_accessed=count * columns * 6, transcendentals=0
        ),
    )(*weights)


def unflat_sum(own, got, shape, order):
    rows, wide = min(256, shape[0]), shape[-1]
    spots = indices(shape, order)

    def kernel(own_ref, got_ref, out):
        for j, spot in enumerate(spots):
            here = slice(j * wide, (j + 1) * wide)
            out[(slice(None), *spot, slice(None))] = own_ref[:, here] + got_ref[:, here].astype(F32)

    zeros = (0,) * (len(shape) - 1)
    return pl.pallas_call(
        kernel,
        grid=(shape[0] // rows,),
        in_specs=[
            pl.BlockSpec((rows, own.shape[1]), lambda i: (i, 0)),
            pl.BlockSpec((rows, own.shape[1]), lambda i: (i, 0)),
        ],
        out_specs=pl.BlockSpec((rows, *shape[1:]), lambda i: (i, *zeros)),
        out_shape=jax.ShapeDtypeStruct(shape, F32),
        compiler_params=pltpu.CompilerParams(vmem_limit_bytes=VMEM_LIMIT),
        cost_estimate=pl.CostEstimate(flops=0, bytes_accessed=own.size * 10, transcendentals=0),
    )(own, got)


def experts(first, named, top, h, grad_out, weights, count):
    tokens, half = h[0].shape
    wide = weights[0].shape[1] // (3 * count)
    rows = min(1024, tokens)

    def kernel(first_ref, named_ref, ha, hb, wa, wb, ga, gb, oa, ob, act_ref, grad_ref):
        mine = (first_ref[0] + pl.program_id(0)).astype(F32)
        named = named_ref[...]
        weight = jnp.sum(
            jnp.where(named[:, :top] == mine, named[:, top : 2 * top], 0.0), 1, keepdims=True
        )
        grad = weight * (dot(ga[...], oa[...]) + dot(gb[...], ob[...]))
        both = dot(ha[...], wa[...]) + dot(hb[...], wb[...])
        gate, up = both[:, :wide], both[:, wide:]
        sig = 1.0 / (1.0 + jnp.exp(-gate))
        silu = gate * sig
        act_ref[...] = (weight * (silu * up)).astype(BF)
        grad_ref[:, :wide] = (grad * up * sig * (1.0 + gate * (1.0 - sig))).astype(BF)
        grad_ref[:, wide:] = (grad * silu).astype(BF)

    def by_rows(columns):
        return pl.BlockSpec((rows, columns), lambda e, r: (r, 0))

    def by_expert(columns, skip):
        return pl.BlockSpec((half, columns), lambda e, r: (0, skip + e))

    def out(columns):
        return pl.BlockSpec((rows, columns), lambda e, r: (r, e))

    return pl.pallas_call(
        kernel,
        grid=(count, tokens // rows),
        in_specs=[
            pl.BlockSpec(memory_space=pltpu.SMEM),
            by_rows(128),
            by_rows(half),
            by_rows(half),
            by_expert(2 * wide, 0),
            by_expert(2 * wide, 0),
            by_rows(half),
            by_rows(half),
            by_expert(wide, 2 * count),
            by_expert(wide, 2 * count),
        ],
        out_specs=[out(wide), out(2 * wide)],
        out_shape=[
            jax.ShapeDtypeStruct((tokens, count * wide), BF),
            jax.ShapeDtypeStruct((tokens, 2 * count * wide), BF),
        ],
        compiler_params=pltpu.CompilerParams(vmem_limit_bytes=VMEM_LIMIT),
        cost_estimate=pl.CostEstimate(
            flops=12 * tokens * half * count * wide,
            bytes_accessed=16 * tokens * half + 12 * half * count * wide,
            transcendentals=tokens * count * wide,
        ),
    )(first.reshape(1), named, *h, *weights, *grad_out, *weights)


def ordered(pairs, start, dtype, tile=512):
    rows, cols = pairs[0][0].shape
    per, block = cols // tile, rows // 8

    def kernel(at, *refs):
        out, j = refs[-1], pl.program_id(0)
        for i in range(len(pairs)):
            for top in range(2):

                @pl.when((j // per == i) & (at[0] // 8 == top))
                def _(i=i, top=top):
                    for p in range(16):
                        part = refs[2 * i + (top ^ (p & 1))]
                        src = pl.multiple_of(((at[0] ^ reversed_bits(p)) & 7) * block, block)
                        out[p * block : (p + 1) * block, :] = part[pl.ds(src, block), :].astype(
                            dtype
                        )

    def spec(i):
        return pl.BlockSpec((rows, tile), lambda j, at: (0, jnp.clip(j - i * per, 0, per - 1)))

    return pl.pallas_call(
        kernel,
        grid_spec=pltpu.PrefetchScalarGridSpec(
            num_scalar_prefetch=1,
            grid=(per * len(pairs),),
            in_specs=[spec(i) for i in range(len(pairs)) for _ in range(2)],
            out_specs=pl.BlockSpec((2 * rows, tile), lambda j, at: (0, j)),
        ),
        out_shape=jax.ShapeDtypeStruct((2 * rows, cols * len(pairs)), dtype),
        compiler_params=pltpu.CompilerParams(vmem_limit_bytes=VMEM_LIMIT),
        cost_estimate=pl.CostEstimate(
            flops=0, bytes_accessed=rows * cols * len(pairs) * 12, transcendentals=0
        ),
    )(start.reshape(1).astype(jnp.int32), *[v for pair in pairs for v in pair])


def two_way():
    return lax.axis_size("fsdp") == 2


def across(v):
    return v if v is None else lax.ppermute(v, "fsdp", [(0, 1), (1, 0)])


def spread(v, axis=0):
    if two_way():
        return v, across(v)
    full = lax.all_gather(v, "fsdp", axis=axis, tiled=True)
    half = full.shape[axis] // 2
    return (
        lax.slice_in_dim(full, 0, half, axis=axis),
        lax.slice_in_dim(full, half, 2 * half, axis=axis),
    )


def halves(v):
    half = v.shape[-1] // 2
    start = lax.axis_index("fsdp") * half if two_way() else 0
    return (
        lax.dynamic_slice_in_dim(v, start, half, v.ndim - 1),
        lax.dynamic_slice_in_dim(v, half - start, half, v.ndim - 1),
    )


def join(first, second):
    straight = jnp.concatenate([first, second], axis=-1)
    if not two_way():
        return straight
    crossed = jnp.concatenate([second, first], axis=-1)
    return jnp.where(lax.axis_index("fsdp") == 0, straight, crossed)


def partner_part(left, right):
    return dot(left[1], right, 0, 0).astype(BF) if two_way() else None


def own_part(left, right):
    if two_way():
        return dot(left[0], right, 0, 0)
    whole = jnp.concatenate([dot(part, right, 0, 0) for part in left], axis=0)
    return lax.psum_scatter(whole, "fsdp", scatter_dimension=0, tiled=True)


def beside(*parts):
    return jnp.concatenate(parts, axis=1) if two_way() else None


def restore(own, got, shape, order):
    if two_way():
        return unflat_sum(own, got, shape, order)
    lead = [shape[1 + i] for i in order]
    turned = own.reshape(shape[0], *lead, shape[-1])
    back = [1 + order.index(i) for i in range(len(order))]
    return turned.transpose(0, *back, len(shape) - 1)


def rms(first, second):
    total = jnp.sum(first * first, -1, keepdims=True) + jnp.sum(second * second, -1, keepdims=True)
    return lax.rsqrt(total / (first.shape[-1] + second.shape[-1]) + EPS)


def norm_back(grads, normed, gains, scale):
    m = [g * d for g, d in zip(gains, grads)]
    mean = (
        jnp.sum(m[0] * normed[0], -1, keepdims=True) + jnp.sum(m[1] * normed[1], -1, keepdims=True)
    ) / (m[0].shape[-1] + m[1].shape[-1])
    return [scale * (a - n * mean) for a, n in zip(m, normed)]


def local(
    tokens,
    attn_qkv,
    attn_out,
    norm_gains,
    expert_in,
    expert_out,
    segment_ids,
    keep_mask,
    routes,
    gate_weights,
    cotangent,
):
    tok_count, width = tokens.shape
    head_width = attn_qkv.shape[2]
    seq_count = tok_count // SEQ_LEN
    own_experts, hidden_width = expert_in.shape[2:]
    columns = own_experts * hidden_width
    rank, rank_reversed = group_index(), reversed_index()
    shard = tok_count // 16
    half = width // 2

    gains = [g.astype(F32) for g in spread(norm_gains.astype(BF), 1)]
    gain_one, gain_two = [g[0] for g in gains], [g[1] for g in gains]
    w_qkv = spread(attn_qkv.astype(BF).reshape(-1, 3 * head_width))
    w_o_own = after(attn_out.astype(BF).T, w_qkv[0])
    w_o = spread(w_o_own, 1)
    w_experts = flat([expert_in, expert_out], [(1, 0), (0,)])
    w_qkv = w_qkv[0], after(w_qkv[1], w_experts)
    w_experts = spread(after(w_experts, w_qkv[1]))
    w_in = [w[:, : 2 * columns] for w in w_experts]
    w_out = [w[:, 2 * columns :] for w in w_experts]

    x = [v.astype(F32) for v in halves(tokens)]
    r_one = rms(*x)
    h_one = [(v * r_one * g).astype(BF) for v, g in zip(x, gain_one)]
    projected = (dot(h_one[0], w_qkv[0]) + dot(h_one[1], w_qkv[1])).astype(BF)
    w_o = w_o[0], after(w_o[1], projected)
    w_o_full = [lax.all_gather(w, GROUP, axis=0, tiled=True) for w in w_o]
    q, k, v = [
        projected[:, i * head_width : (i + 1) * head_width].reshape(seq_count, SEQ_LEN, head_width)
        for i in range(3)
    ]
    seg = segment_ids.reshape(seq_count, SEQ_LEN)
    keep = keep_mask.reshape(seq_count, SEQ_LEN)
    diagonal = jnp.arange(SEQ_LEN)[:, None] == jnp.arange(SEQ_LEN)[None, :]
    allowed = (seg[:, :, None] == seg[:, None, :]) & ((keep[:, None, :] == 1) | diagonal[None])
    score_scale = head_width ** (-0.5)
    scores = jnp.einsum("sqe,ske->sqk", q, k, preferred_element_type=F32) * score_scale
    probs = jax.nn.softmax(jnp.where(allowed, scores, -1e30), axis=-1)
    attended = jnp.einsum("sqk,ske->sqe", probs.astype(BF), v, preferred_element_type=F32)
    attended = attended.reshape(tok_count, head_width).astype(BF)

    attended_rows = lax.all_to_all(attended, GROUP, 0, 1, tiled=True)
    first_expert = lax.axis_index("heads") * own_experts
    named = jnp.concatenate([routes.astype(F32), gate_weights], axis=1)
    top = routes.shape[1]
    named = jnp.pad(named, ((0, 0), (0, 128 - 2 * top)))
    named = reorder([named], rank, F32)
    attended_rows = after(attended_rows, named)
    start = lax.axis_index("fsdp") * half if two_way() else jnp.int32(0)
    grad_out = reorder([cotangent], rank, BF, shift=start)
    attended_rows = after(attended_rows, grad_out)
    grad_out = grad_out[:, :half], grad_out[:, half:]
    x_rows = halves(lax.dynamic_slice_in_dim(tokens, rank * shard, shard, 0))
    x_rows = [v.astype(F32) for v in x_rows]
    middle = [v + dot(attended_rows, w) for v, w in zip(x_rows, w_o_full)]
    r_two = rms(*middle)
    n_two = [v * r_two for v in middle]
    h_two_rows = [(n * g).astype(BF) for n, g in zip(n_two, gain_two)]
    h_two = whole(gather_chain(h_two_rows)[0])

    act, grad_gate_up = experts(first_expert, named, top, h_two, grad_out, w_experts, own_experts)
    grad_two = reduce_first(grad_gate_up, w_in)
    act_late, grad_gate_up_late = hold([act, grad_gate_up], *grad_two)
    expert_in_part = partner_part(h_two, grad_gate_up_late)
    expert_in_got = across(expert_in_part)
    expert_out_part = partner_part(grad_out, after(act_late, expert_in_part))
    expert_out_got = across(expert_out_part)
    grad_two, _, steps_two = reduce_rest(
        grad_two, ((), [expert_in_part], [expert_out_part])
    )
    grad_two = [g.astype(F32) for g in grad_two]

    out_in_rows = halves(lax.dynamic_slice_in_dim(cotangent, rank * shard, shard, 0))
    out_in_rows = [v.astype(F32) for v in out_in_rows]
    grad_middle = [
        a + b for a, b in zip(out_in_rows, norm_back(grad_two, n_two, gain_two, r_two))
    ]
    gain_two_part = join(*[jnp.sum(g * n, axis=0) for g, n in zip(grad_two, n_two)])
    grad_branch_rows = [g.astype(BF) for g in grad_middle]
    grad_attended_rows = (
        dot(grad_branch_rows[0], w_o_full[0], 1, 1) + dot(grad_branch_rows[1], w_o_full[1], 1, 1)
    ).astype(BF)
    grad_attended = lax.all_to_all(grad_attended_rows, GROUP, 1, 0, tiled=True)
    grad_attended = grad_attended.reshape(seq_count, SEQ_LEN, head_width)

    grad_v = jnp.einsum("sqk,sqe->ske", probs.astype(BF), grad_attended, preferred_element_type=F32)
    grad_probs = jnp.einsum("sqe,ske->sqk", grad_attended, v, preferred_element_type=F32)
    grad_scores = probs * (grad_probs - jnp.sum(probs * grad_probs, axis=-1, keepdims=True))
    grad_scores = grad_scores.astype(BF)
    grad_q = jnp.einsum("sqk,ske->sqe", grad_scores, k, preferred_element_type=F32) * score_scale
    grad_k = jnp.einsum("sqk,sqe->ske", grad_scores, q, preferred_element_type=F32) * score_scale
    grad_projected = jnp.concatenate([grad_q, grad_k, grad_v], axis=-1)
    grad_projected = grad_projected.reshape(tok_count, 3 * head_width).astype(BF)
    grad_projected_blocks = reorder([grad_projected], rank, BF, tile=3 * head_width)
    grad_one = reduce_first(grad_projected_blocks, w_qkv)
    qkv_part = partner_part(h_one, after(grad_projected, *grad_one))

    mixture = reduce_first(after(act_late, *steps_two[1]), w_out, grad_attended_rows)
    mixture = reduce_rest(mixture, ((), [grad_projected_blocks], grad_one))[0]
    grad_branch = jnp.concatenate(hold(grad_branch_rows, grad_attended_rows), axis=1)
    grad_branch = lax.all_gather(grad_branch, GROUP, axis=0, tiled=True)
    out_rows = join(*[(a + b.astype(F32)).astype(BF) for a, b in zip(middle, mixture)])
    output = lax.all_gather(after(out_rows, grad_branch), GROUP, axis=0, tiled=True)
    grad_branch = grad_branch[:, :half], grad_branch[:, half:]
    out_part = partner_part(grad_branch, attended)
    attention_got = across(beside(qkv_part, out_part))
    grad_one, _, steps_one = reduce_rest(grad_one, ((), [qkv_part], [mixture[0], expert_in_got]))
    own_act, own_gate_up = hold([act, grad_gate_up], grad_attended_rows)
    expert_in_own = own_part(h_two, own_gate_up)
    expert_out_own = own_part(grad_out, after(own_act, *steps_one[0]))
    expert_in_grad = restore(
        expert_in_own, after(expert_in_got, *steps_one[1]), expert_in.shape, (1, 0)
    )
    grad_one = hold(grad_one, expert_in_grad, expert_out_own)
    grad_one = [g.astype(F32) for g in grad_one]

    r_rows = rms(*x_rows)
    n_rows = [v * r_rows for v in x_rows]
    gain_one_part = join(*[jnp.sum(g * n, axis=0) for g, n in zip(grad_one, n_rows)])
    gain_parts = jnp.stack([gain_one_part, gain_two_part])
    grad_rows = join(
        *[a + b for a, b in zip(grad_middle, norm_back(grad_one, n_rows, gain_one, r_rows))]
    ).astype(BF)
    expert_out_grad = restore(expert_out_own, expert_out_got, expert_out.shape, (0,))
    input_grad, stages, gain_parts = gather_chain(
        [grad_rows[:, :half], grad_rows[:, half:]],
        ((), (), [expert_out_got], [expert_out_grad, output, attention_got]),
        vector=gain_parts,
    )
    gain_parts = gain_parts + across(gain_parts) if two_way() else lax.psum(gain_parts, "fsdp")
    own_width = norm_gains.shape[1]
    gains_grad = lax.dynamic_slice_in_dim(
        gain_parts, lax.axis_index("fsdp") * own_width, own_width, 1
    )

    qkv_own, out_own = own_part(h_one, grad_projected), own_part(grad_branch, attended)
    if two_way():
        attention_got = attention_got.astype(F32)
        qkv_own = qkv_own + attention_got[:, : 3 * head_width]
        out_own = out_own + attention_got[:, 3 * head_width :]
    input_grad = ordered(input_grad, rank_reversed, F32)

    return (
        output,
        input_grad,
        qkv_own.reshape(attn_qkv.shape),
        out_own,
        gains_grad,
        expert_in_grad,
        expert_out_grad,
    )


def solution(mesh):
    placed = (
        P("fsdp", None),
        P("fsdp", None, ("heads", "tensor")),
        P("fsdp", ("heads", "tensor")),
        P(None, "fsdp"),
        P("fsdp", None, "heads", "tensor"),
        P("fsdp", "heads", "tensor"),
        P("fsdp"),
        P("fsdp"),
        P("fsdp", None),
        P("fsdp", None),
        P("fsdp", None),
    )
    return jax.shard_map(
        local,
        mesh=mesh,
        in_specs=placed,
        out_specs=(
            P("fsdp", None),
            P("fsdp", None),
            P("fsdp", None, ("heads", "tensor")),
            P("fsdp", ("heads", "tensor")),
            P(None, "fsdp"),
            P("fsdp", None, "heads", "tensor"),
            P("fsdp", "heads", "tensor"),
        ),
        check_vma=False,
    )
```

time: 723 us -> 509 us (0.70)
  waiting for transfers between devices: 322 us -> 213 us
  local copies, waits for them, and re-layouts: 120 us -> 21.5 us
  Pallas kernels: 0 us -> 69 us
  blocking collectives: 38.1 us -> 0 us
  matrix products: 114 us -> 89.2 us
  starting transfers between devices: 80.1 us -> 66.8 us
  between operations: 3.23 us -> 15.4 us
  other arithmetic: 37 us -> 25.2 us
    ppermute x9 -> x8, waiting for transfers between devices: 153 us -> 16.4 us  [across(): return v if v is None else lax.ppermute(v, 'fsdp', [(0, 1), (1, 0)])]
    pallas_call x0 -> x8, Pallas kernels: none -> 69 us  [the longest x1 21.4 us: experts(): pl.pallas_call(kernel, grid=(count, tokens // rows), in_specs=[pl.BlockSp...]
    all_gather x0 -> x4, waiting for transfers between devices: none -> 59.6 us  [the longest x2 59.6 us: local(): w_o_full = [lax.all_gather(w, GROUP, axis=0, tiled=True) for w in w_o]]
    dynamic_update_slice x74 -> x0, local copies, waits for them, and re-layouts: 54.2 us -> none  [the longest x40 28.5 us: gather_rows(): v = lax.dynamic_update_slice_in_dim(wide, got, 1 - me, dim)]
    psum x1 -> x0, blocking collectives: 38.1 us -> none  [local(): gain_parts = lax.psum(jnp.stack([gain_one_part, gain_two_part]), EVERY)]
    ppermute x64 -> x44, waiting for transfers between devices: 169 us -> 132 us  [swap(): lax.ppermute(v, name, [(i, i ^ bit) for i in range(lax.axis_size(name))])]
    dot_general x24 -> x26, matrix products: 105 us -> 79.5 us  [dot(): lax.dot_general(a, b, (((ca,), (cb,)), ((), ())), preferred_element_type=...]
    convert_element_type x24 -> x18, other arithmetic: 26.5 us -> 7.2 us  [the longest x12 2.6 us: reduce_rest(): (m.astype(F32) + g.astype(F32)).astype(BF)]
  transfers between devices with their start and end apart: 75 -> 58, of which waited for: 35 -> 33; matrix products, arithmetic and copies ran while one was open for 31% -> 23% of each run, Pallas kernels for 0% -> 8%
where the time goes in v2:
time: 509 us; the launch traced here: 500 us
  waiting for transfers between devices  213 us (42%)
  matrix products  89.2 us (18%)
  Pallas kernels  69 us (14%)
  starting transfers between devices  66.8 us (13%)
  other arithmetic  25.2 us (5%)
  local copies, waits for them, and re-layouts  21.5 us (4%)
  between operations  15.4 us (3%)
    ppermute x44, waiting for transfers between devices, swap(): lax.ppermute(v, name, [(i, i ^ bit) for i in range(lax.axis_size(name))])  132 us
    dot_general x26, matrix products, dot(): lax.dot_general(a, b, (((ca,), (cb,)), ((), ())), preferred_element_type=...  79.5 us
    all_gather x2, waiting for transfers between devices, local(): w_o_full = [lax.all_gather(w, GROUP, axis=0, tiled=True) for w in w_o]  59.6 us
    ppermute x44, starting transfers between devices, swap(): lax.ppermute(v, name, [(i, i ^ bit) for i in range(lax.axis_size(name))])  43.4 us
    pallas_call x1, Pallas kernels, experts(): pl.pallas_call(kernel, grid=(count, tokens // rows), in_specs=[pl.BlockSp...  21.4 us
    ppermute x8, waiting for transfers between devices, across(): return v if v is None else lax.ppermute(v, 'fsdp', [(0, 1), (1, 0)])  16.4 us
    pallas_call x1, Pallas kernels, flat(): pl.pallas_call(kernel, grid=(count // rows,), in_specs=[spec(v) for v in...  15.1 us
    pallas_call x2, Pallas kernels, unflat_sum(): pl.pallas_call(kernel, grid=(shape[0] // rows,), in_specs=[pl.BlockSpec((...  14.3 us
  transfers between devices with their start and end apart: 58, of which 33 were waited for; matrix products, arithmetic and copies ran while one was open for 23% of the time, Pallas kernels for 8%

profile of v2, /device:TPU:0, one launch (start us, length us, event | category | flops | bytes accessed | tf_op | source)
XLA Modules:
  0.0 499.9 jit_solution(4070535197842521613)
XLA Ops:
  10.7 3.0 collective-permute-start.1
  16.5 3.3 fusion.3
  22.2 15.1 %shard_map.162.wa.oa = bf16[1024,3072]{1,0:T(8,128)(2,1)} custom-call(f32[1024,2,4,256]{3,2,1,0:T(4,128)} %refs_0_.2, f32[1024,4,256]{2,1,0:T(4,128)S(1)} %copy-done), custom_call_target="tpu_custom_call" | custom-call | bytes 18874368 | tf_op jit(solution)/shard_map/pallas_call | solution.py:176
  44.5 5.9 %all-to-all-start = ((bf16[16,64,128]{2,1,0:T(8,128)(2,1)}), bf16[16,64,128]{2,1,0:T(8,128)(2,1)S(1)}, u32[]{:S(2)}, u32[]{:S(2)}) async-start(bf16[16,64,128]{2,1,0:T(8,128)(2,1)} %bitcast.3), calls=%async_computation | async-start | bytes 524288 | tf_op jit(solution)/shard_map/all_to_all | solution.py:434
  52.3 2.5 shard_map.163.named_ref
  55.5 7.3 %shard_map.164 = bf16[1024,2048]{1,0:T(8,128)(2,1)} custom-call(s32[2]{0:T(128)} %pad_add_fusion.1.at, bf16[1024,2048]{1,0:T(8,128)(2,1)} %refs_0_.3), custom_call_target="tpu_custom_call" | custom-call | bytes 16777216 | tf_op jit(solution)/shard_map/pallas_call | solution.py:134
  63.1 7.6 %all-gather.5.cloned.1.call-done = bf16[2048,1024]{0,1:T(8,128)(2,1)} async-done(((bf16[128,1024]{0,1:T(8,128)(2,1)}), bf16[2048,1024]{0,1:T(8,128)(2,1)}) %all-gather.5.cloned.1.call-update) | async-done | bytes 4194320 | tf_op jit(solution)/shard_map/all_gather | solution.py:419
  70.7 3.7 multiply_reduce_fusion.2
  74.4 52.0 %all-gather.7.cloned.1.call-done = bf16[2048,1024]{0,1:T(8,128)(2,1)} async-done(((bf16[128,1024]{0,1:T(8,128)(2,1)}), bf16[2048,1024]{0,1:T(8,128)(2,1)}) %all-gather.7.cloned.1.call-update) | async-done | bytes 4194320 | tf_op jit(solution)/shard_map/all_gather | solution.py:419
  126.4 3.7 multiply_reduce_fusion.1
  132.4 3.6 collective-permute-done.4
  136.0 3.1 collective-permute-done.3
  139.2 3.0 collective-permute-start.5
  142.2 10.8 %collective-permute-done.6 = bf16[1,2,1,1,64,1024]{5,4,3,2,1,0:T(8,128)(2,1)S(1)} collective-permute-done((bf16[1,2,1,1,64,1024]{5,4,3,2,1,0:T(8,128)(2,1)S(1)}, bf16[1,2,1,1,64,1024]{5,4,3,2,1,0:T(8,128)(2,1)S(1)}, u32[]{:S(2)}, u32[]{:S(2)}) %collective-permute-start.6) | collective-permute-done | bytes 262176 | tf_op jit(solution)/shard_map/ppermute | solution.py:38
  154.9 12.1 %collective-permute-done.8 = bf16[1,2,1,2,64,1024]{5,4,3,2,1,0:T(8,128)(2,1)S(1)} collective-permute-done((bf16[1,2,1,2,64,1024]{5,4,3,2,1,0:T(8,128)(2,1)S(1)}, bf16[1,2,1,2,64,1024]{5,4,3,2,1,0:T(8,128)(2,1)S(1)}, u32[]{:S(2)}, u32[]{:S(2)}) %collective-permute-start.8) | collective-permute-done | bytes 524320 | tf_op jit(solution)/shard_map/ppermute | solution.py:38
  167.8 2.6 fusion.155
  172.2 4.1 collective-permute-done.11.wb.ob
  176.4 21.4 %shard_map.165 = (bf16[1024,1024]{1,0:T(8,128)(2,1)S(1)}, bf16[1024,2048]{1,0:T(8,128)(2,1)}) custom-call(s32[1]{0:T(128)} %bitcast.8.first_ref, f32[1024,128]{1,0:T(8,128)S(1)} %copy-done.1, bf16[1024,1024]{1,0:T(8,128)(2,1)S(1)} %pad_maximum_fusion.ha, bf16[1024,1024]{1,0:T(8,128)(2,1)} %pad_maximum_fusion.1.hb, bf16[1024,3072]{1,0:T(8,128)(2,1)} %shard_map.162.wa.oa, ...), custom_call_target="tpu_custom_call" | custom-call | flops 12884901888 | bytes 29360128 | tf_op jit(solution)/shard_map/pallas_call | solution.py:242
  197.8 5.3 %fusion.46 = bf16[512,1024]{1,0:T(8,128)(2,1)S(1)} fusion(bf16[1024,3072]{1,0:T(8,128)(2,1)} %collective-permute-done.11.wb.ob, bf16[1024,2048]{1,0:T(8,128)(2,1)} %get-tuple-element.107), kind=kOutput, calls=%fused_computation.62 | convolution fusion | flops 2148007936 | bytes 7340032 | tf_op jit(solution)/shard_map/dot_general | solution.py:29
  203.2 2.4 fusion.41
  206.2 4.6 add_convert_fusion.4
  210.8 2.4 add_convert_fusion.5
  216.3 6.2 %convolution_convert_fusion = bf16[1024,2048]{1,0:T(8,128)(2,1)} fusion(bf16[1024,2048]{1,0:T(8,128)(2,1)S(1)} %copy-done.38, bf16[512,1024]{1,0:T(8,128)(2,1)S(1)} %bitcast.148, bf16[512,1024]{1,0:T(8,128)(2,1)S(1)} %bitcast.135), kind=kOutput, calls=%fused_computation.17 | convolution fusion | flops 4301258752 | bytes 10485760 | tf_op jit(solution)/shard_map/dot_general | solution.py:29
  222.6 4.7 collective-permute-done.15
  228.7 2.6 collective-permute-start.17
  231.9 3.7 convolution_convert_fusion.1
  235.6 6.9 %collective-permute-done.17 = bf16[1,2,1,1,64,1024]{5,4,3,2,1,0:T(8,128)(2,1)S(1)} collective-permute-done((bf16[1,2,1,1,64,1024]{5,4,3,2,1,0:T(8,128)(2,1)S(1)}, bf16[1,2,1,1,64,1024]{5,4,3,2,1,0:T(8,128)(2,1)S(1)}, u32[]{:S(2)}, u32[]{:S(2)}) %collective-permute-start.17) | collective-permute-done | bytes 262176 | tf_op jit(solution)/shard_map/ppermute | solution.py:38
  245.4 5.6 %collective-permute-done.18 = bf16[1,1,1,1,64,1024]{5,4,3,2,1,0:T(8,128)(2,1)S(1)} collective-permute-done((bf16[1,1,1,1,64,1024]{5,4,3,2,1,0:T(8,128)(2,1)S(1)}, bf16[1,1,1,1,64,1024]{5,4,3,2,1,0:T(8,128)(2,1)S(1)}, u32[]{:S(2)}, u32[]{:S(2)}) %collective-permute-start.18) | collective-permute-done | bytes 131104 | tf_op jit(solution)/shard_map/ppermute | solution.py:38
  258.2 4.2 all-to-all-start.1
  262.7 3.9 fusion.38
  266.9 3.9 fusion.35
  271.0 4.8 all-to-all-done.1
  275.7 3.5 multiply_reduce_fusion
  285.6 2.9 shard_map.166
  288.6 3.1 add_convert_fusion.2
  291.7 3.3 add_convert_fusion.3
  301.7 15.6 %collective-permute-done.23 = bf16[1,2,1,2,64,1024]{5,4,3,2,1,0:T(8,128)(2,1)S(1)} collective-permute-done((bf16[1,2,1,2,64,1024]{5,4,3,2,1,0:T(8,128)(2,1)S(1)}, bf16[1,2,1,2,64,1024]{5,4,3,2,1,0:T(8,128)(2,1)S(1)}, u32[]{:S(2)}, u32[]{:S(2)}) %collective-permute-start.23) | collective-permute-done | bytes 524320 | tf_op jit(solution)/shard_map/ppermute | solution.py:38
  317.7 2.2 collective-permute-start.25
  324.0 8.5 %collective-permute-done.25 = bf16[1,2,1,1,64,1024]{5,4,3,2,1,0:T(8,128)(2,1)S(1)} collective-permute-done((bf16[1,2,1,1,64,1024]{5,4,3,2,1,0:T(8,128)(2,1)S(1)}, bf16[1,2,1,1,64,1024]{5,4,3,2,1,0:T(8,128)(2,1)S(1)}, u32[]{:S(2)}, u32[]{:S(2)}) %collective-permute-start.25) | collective-permute-done | bytes 262176 | tf_op jit(solution)/shard_map/ppermute | solution.py:38
  333.0 2.1 collective-permute-start.29
  340.3 11.9 %collective-permute-done.28 = bf16[1,1,1,1,64,1024]{5,4,3,2,1,0:T(8,128)(2,1)S(1)} collective-permute-done((bf16[1,1,1,1,64,1024]{5,4,3,2,1,0:T(8,128)(2,1)S(1)}, bf16[1,1,1,1,64,1024]{5,4,3,2,1,0:T(8,128)(2,1)S(1)}, u32[]{:S(2)}, u32[]{:S(2)}) %collective-permute-start.28) | collective-permute-done | bytes 131104 | tf_op jit(solution)/shard_map/ppermute | solution.py:38
  356.1 3.1 convolution_convert_fusion.4
  360.5 9.9 %collective-permute-done.30 = bf16[1,1,2,2,64,1024]{5,4,3,2,1,0:T(8,128)(2,1)S(1)} collective-permute-done((bf16[1,1,2,2,64,1024]{5,4,3,2,1,0:T(8,128)(2,1)S(1)}, bf16[1,1,2,2,64,1024]{5,4,3,2,1,0:T(8,128)(2,1)S(1)}, u32[]{:S(2)}, u32[]{:S(2)}) %collective-permute-start.30) | collective-permute-done | bytes 524320 | tf_op jit(solution)/shard_map/ppermute | solution.py:38
  370.6 3.1 collective-permute-start.33
  373.8 6.8 %fusion.147.own_ref = f32[1024,2048]{1,0:T(8,128)} fusion(bf16[1024,2048]{1,0:T(8,128)(2,1)S(1)} %copy-done.39, bf16[512,1024]{1,0:T(8,128)(2,1)S(1)} %bitcast.146, bf16[512,1024]{1,0:T(8,128)(2,1)S(1)} %bitcast.133), kind=kOutput, calls=%fused_computation.214 | convolution fusion | flops 4299161600 | bytes 14680064 | tf_op jit(solution)/shard_map/dot_general | solution.py:29
  380.7 5.6 %collective-permute-done.33 = bf16[1,2,1,1,64,1024]{5,4,3,2,1,0:T(8,128)(2,1)S(1)} collective-permute-done((bf16[1,2,1,1,64,1024]{5,4,3,2,1,0:T(8,128)(2,1)S(1)}, bf16[1,2,1,1,64,1024]{5,4,3,2,1,0:T(8,128)(2,1)S(1)}, u32[]{:S(2)}, u32[]{:S(2)}) %collective-permute-start.33) | collective-permute-done | bytes 262176 | tf_op jit(solution)/shard_map/ppermute | solution.py:38
  386.4 2.6 collective-permute-done.32
  389.1 4.7 collective-permute-done.34.got_ref
  394.3 4.4 fusion.145.own_ref
  398.8 2.5 collective-permute-start.35
  401.3 9.1 %shard_map.167 = f32[1024,2,4,256]{3,2,1,0:T(4,128)} custom-call(f32[1024,2048]{1,0:T(8,128)} %fusion.147.own_ref, bf16[1024,2048]{1,0:T(8,128)(2,1)} %collective-permute-done.34.got_ref), custom_call_target="tpu_custom_call" | custom-call | bytes 20971520 | tf_op jit(solution)/shard_map/pallas_call | solution.py:199
  415.3 2.7 collective-permute-start.43
  419.7 3.9 collective-permute-done.38
  423.7 3.8 collective-permute-done.37
  432.1 8.6 %collective-permute-done.41 = bf16[1,2,1,1,64,1024]{5,4,3,2,1,0:T(8,128)(2,1)S(1)} collective-permute-done((bf16[1,2,1,1,64,1024]{5,4,3,2,1,0:T(8,128)(2,1)S(1)}, bf16[1,2,1,1,64,1024]{5,4,3,2,1,0:T(8,128)(2,1)S(1)}, u32[]{:S(2)}, u32[]{:S(2)}) %collective-permute-start.41) | collective-permute-done | bytes 262176 | tf_op jit(solution)/shard_map/ppermute | solution.py:38
  444.9 5.3 %shard_map.168 = f32[1024,4,256]{2,1,0:T(4,128)} custom-call(f32[1024,1024]{1,0:T(8,128)} %fusion.145.own_ref, bf16[1024,1024]{1,0:T(8,128)(2,1)S(1)} %collective-permute-done.42.got_ref), custom_call_target="tpu_custom_call" | custom-call | bytes 10485760 | tf_op jit(solution)/shard_map/pallas_call | solution.py:199
  450.2 4.9 collective-permute-done.47
  455.3 5.4 %collective-permute-done.46 = bf16[1024,512]{0,1:T(8,128)(2,1)} collective-permute-done((bf16[1024,512]{0,1:T(8,128)(2,1)S(1)}, bf16[1024,512]{0,1:T(8,128)(2,1)}, u32[]{:S(2)}, u32[]{:S(2)}) %collective-permute-start.46) | collective-permute-done | bytes 1048608 | tf_op jit(solution)/shard_map/ppermute | solution.py:313
  462.3 3.6 collective-permute-done.50
  467.5 2.2 collective-permute-done.51
  473.1 2.9 slice_add_fusion.1
  478.0 4.5 slice_add_fusion
  482.5 3.0 copy.45
  485.5 5.4 %shard_map.169 = f32[1024,2048]{1,0:T(8,128)} custom-call(s32[1]{0:T(128)} %bitcast.32.at, bf16[512,1024]{1,0:T(8,128)(2,1)S(1)} %bitcast.120, bf16[512,1024]{1,0:T(8,128)(2,1)S(1)} %bitcast.121, bf16[512,1024]{1,0:T(8,128)(2,1)S(1)} %bitcast.119, bf16[512,1024]{1,0:T(8,128)(2,1)} %bitcast.48.refs_3_), custom_call_target="tpu_custom_call" | custom-call | bytes 12582912 | tf_op jit(solution)/shard_map/pallas_call | solution.py:292
  (276 shorter events, 97.5 us)
Async XLA Ops:
  7.2 63.6 %all-gather.5.cloned.1.call-start = ((), (), s32[]{:S(2)}) async-start(), calls=%async_computation.2 | async-start | bytes 4456448 | tf_op jit(solution)/shard_map/all_gather | solution.py:419
  10.7 115.7 %all-gather.7.cloned.1.call-start = ((), (), s32[]{:S(2)}) async-start(), calls=%async_computation.3 | async-start | bytes 4456448 | tf_op jit(solution)/shard_map/all_gather | solution.py:419
  10.7 26.6 %collective-permute-start.1 = (bf16[1024,384]{0,1:T(8,128)(2,1)S(1)}, bf16[1024,384]{0,1:T(8,128)(2,1)S(1)}, u32[]{:S(2)}, u32[]{:S(2)}) collective-permute-start(bf16[1024,384]{0,1:T(8,128)(2,1)S(1)} %bitcast.122), channel_id=1, source_target_pairs={{0,16},{16,0},{1,17},{17,1},{2,18},{18,2},{3,19},{19,3},{4,20},{20... | collective-permute-start | bytes 2359304 | tf_op jit(solution)/shard_map/ppermute | solution.py:313
  13.8 24.9 %collective-permute-start.2 = (bf16[128,1024]{0,1:T(8,128)(2,1)}, bf16[128,1024]{0,1:T(8,128)(2,1)S(1)}, u32[]{:S(2)}, u32[]{:S(2)}) collective-permute-start(bf16[128,1024]{0,1:T(8,128)(2,1)} %convert_bitcast_fusion), channel_id=1, source_target_pairs={{0,16},{16,0},{1,17},{17,1},{2,18},{18,2},{3,19},{19,3},{4,20},{20... | collective-permute-start | bytes 786440 | tf_op jit(solution)/shard_map/ppermute | solution.py:313
  14.6 22.8 %collective-permute-start = (bf16[2,1024]{1,0:T(2,128)(2,1)S(1)}, bf16[2,1024]{1,0:T(2,128)(2,1)S(1)}, u32[]{:S(2)}, u32[]{:S(2)}) collective-permute-start(bf16[2,1024]{1,0:T(2,128)(2,1)S(1)} %convert_element_type.351), channel_id=1, source_target_pairs={{0,16},{16,0},{1,17},{17,1},{2,18},{18,2},{3,19},{19,3},{4,20},{20... | collective-permute-start | bytes 12296 | tf_op jit(solution)/shard_map/ppermute | solution.py:313
  39.5 136.9 %collective-permute-start.11 = (bf16[1024,3072]{1,0:T(8,128)(2,1)}, bf16[1024,3072]{1,0:T(8,128)(2,1)}, u32[]{:S(2)}, u32[]{:S(2)}) collective-permute-start(bf16[1024,3072]{1,0:T(8,128)(2,1)} %shard_map.162.wa.oa), channel_id=1, source_target_pairs={{0,16},{16,0},{1,17},{17,1},{2,18},{18,2},{3,19},{19,3},{4,20},{20... | collective-permute-start | bytes 18874376 | tf_op jit(solution)/shard_map/ppermute | solution.py:313
  44.5 18.6 %all-to-all-start = ((bf16[16,64,128]{2,1,0:T(8,128)(2,1)}), bf16[16,64,128]{2,1,0:T(8,128)(2,1)S(1)}, u32[]{:S(2)}, u32[]{:S(2)}) async-start(bf16[16,64,128]{2,1,0:T(8,128)(2,1)} %bitcast.3), calls=%async_computation | async-start | bytes 524288 | tf_op jit(solution)/shard_map/all_to_all | solution.py:434
  50.4 302.6 %all-gather.9.cloned.1.call-start = ((), (), s32[]{:S(2)}) async-start(), calls=%async_computation.4 | async-start | bytes 4456448 | tf_op jit(solution)/shard_map/all_gather | solution.py:493
  130.1 37.7 %copy-start.2 = (bf16[1024,2048]{1,0:T(8,128)(2,1)S(1)}, bf16[1024,2048]{1,0:T(8,128)(2,1)}, u32[]{:S(2)}) copy-start(bf16[1024,2048]{1,0:T(8,128)(2,1)} %shard_map.164) | copy-start | bytes 12582916
  130.2 5.7 %collective-permute-start.4 = (bf16[1,1,1,1,64,1024]{5,4,3,2,1,0:T(8,128)(2,1)S(1)}, bf16[1,1,1,1,64,1024]{5,4,3,2,1,0:T(8,128)(2,1)S(1)}, u32[]{:S(2)}, u32[]{:S(2)}) collective-permute-start(bf16[1,1,1,1,64,1024]{5,4,3,2,1,0:T(8,128)(2,1)S(1)} %get-tuple-element.70), channel_id=1, source_target_pairs={{0,2},{1,3},{2,0},{3,1},{4,6},{5,7},{6,4},{7,5},{8,10},{9,11},{10,... | collective-permute-start | bytes 393224 | tf_op jit(solution)/shard_map/ppermute | solution.py:38
  131.7 7.4 %collective-permute-start.3 = (bf16[1,1,1,1,64,1024]{5,4,3,2,1,0:T(8,128)(2,1)S(1)}, bf16[1,1,1,1,64,1024]{5,4,3,2,1,0:T(8,128)(2,1)S(1)}, u32[]{:S(2)}, u32[]{:S(2)}) collective-permute-start(bf16[1,1,1,1,64,1024]{5,4,3,2,1,0:T(8,128)(2,1)S(1)} %get-tuple-element.69), channel_id=1, source_target_pairs={{0,8},{4,12},{8,0},{12,4},{1,9},{5,13},{9,1},{13,5},{2,10},{6,14},... | collective-permute-start | bytes 393224 | tf_op jit(solution)/shard_map/ppermute | solution.py:38
  139.1 13.9 %collective-permute-start.6 = (bf16[1,2,1,1,64,1024]{5,4,3,2,1,0:T(8,128)(2,1)S(1)}, bf16[1,2,1,1,64,1024]{5,4,3,2,1,0:T(8,128)(2,1)S(1)}, u32[]{:S(2)}, u32[]{:S(2)}) collective-permute-start(bf16[1,2,1,1,64,1024]{5,4,3,2,1,0:T(8,128)(2,1)S(1)} %pad_maximum_fusion.12), channel_id=1, source_target_pairs={{0,8},{4,12},{8,0},{12,4},{1,9},{5,13},{9,1},{13,5},{2,10},{6,14},... | collective-permute-start | bytes 786440 | tf_op jit(solution)/shard_map/ppermute | solution.py:38
  139.2 14.0 %collective-permute-start.5 = (bf16[1,1,1,2,64,1024]{5,4,3,2,1,0:T(8,128)(2,1)S(1)}, bf16[1,1,1,2,64,1024]{5,4,3,2,1,0:T(8,128)(2,1)S(1)}, u32[]{:S(2)}, u32[]{:S(2)}) collective-permute-start(bf16[1,1,1,2,64,1024]{5,4,3,2,1,0:T(8,128)(2,1)S(1)} %pad_maximum_fusion.11), channel_id=1, source_target_pairs={{0,4},{4,0},{8,12},{12,8},{1,5},{5,1},{9,13},{13,9},{2,6},{6,2},{1... | collective-permute-start | bytes 786440 | tf_op jit(solution)/shard_map/ppermute | solution.py:38
  153.3 13.7 %collective-permute-start.8 = (bf16[1,2,1,2,64,1024]{5,4,3,2,1,0:T(8,128)(2,1)S(1)}, bf16[1,2,1,2,64,1024]{5,4,3,2,1,0:T(8,128)(2,1)S(1)}, u32[]{:S(2)}, u32[]{:S(2)}) collective-permute-start(bf16[1,2,1,2,64,1024]{5,4,3,2,1,0:T(8,128)(2,1)S(1)} %pad_maximum_fusion.8), channel_id=1, source_target_pairs={{0,4},{4,0},{8,12},{12,8},{1,5},{5,1},{9,13},{13,9},{2,6},{6,2},{1... | collective-permute-start | bytes 1572872 | tf_op jit(solution)/shard_map/ppermute | solution.py:38
  153.5 13.6 %collective-permute-start.7 = (bf16[1,1,2,2,64,1024]{5,4,3,2,1,0:T(8,128)(2,1)S(1)}, bf16[1,1,2,2,64,1024]{5,4,3,2,1,0:T(8,128)(2,1)S(1)}, u32[]{:S(2)}, u32[]{:S(2)}) collective-permute-start(bf16[1,1,2,2,64,1024]{5,4,3,2,1,0:T(8,128)(2,1)S(1)} %pad_maximum_fusion.7), channel_id=1, source_target_pairs={{0,2},{1,3},{2,0},{3,1},{4,6},{5,7},{6,4},{7,5},{8,10},{9,11},{10,... | collective-permute-start | bytes 1572872 | tf_op jit(solution)/shard_map/ppermute | solution.py:38
  167.2 3.1 collective-permute-start.10
  167.3 4.7 collective-permute-start.9
  172.0 31.2 %slice-start = ((s8[6291456]{0:T(1024)(128)(4,1)}), s8[4194304]{0:T(1024)(128)(4,1)S(1)}, s32[]{:S(2)}) async-start(s8[6291456]{0:T(1024)(128)(4,1)} %bitcast.126), calls=%async_computation.6 | async-start | bytes 8388608
  176.4 26.8 %slice-start.1 = ((s8[6291456]{0:T(1024)(128)(4,1)}), s8[2097152]{0:T(1024)(128)(4,1)S(1)}, s32[]{:S(2)}) async-start(s8[6291456]{0:T(1024)(128)(4,1)} %bitcast.126), calls=%async_computation.7 | async-start | bytes 4194304
  203.1 3.1 collective-permute-start.13
  205.7 5.1 %collective-permute-start.12 = (bf16[512,1024]{1,0:T(8,128)(2,1)S(1)}, bf16[512,1024]{1,0:T(8,128)(2,1)S(1)}, u32[]{:S(2)}, u32[]{:S(2)}) collective-permute-start(bf16[512,1024]{1,0:T(8,128)(2,1)S(1)} %fusion.41), channel_id=1, source_target_pairs={{0,1},{1,0},{2,3},{3,2},{4,5},{5,4},{6,7},{7,6},{8,9},{9,8},{10,11... | collective-permute-start | bytes 3145736 | tf_op jit(solution)/shard_map/ppermute | solution.py:38
  213.3 13.9 %collective-permute-start.15 = (bf16[1,2,1,2,64,1024]{5,4,3,2,1,0:T(8,128)(2,1)S(1)}, bf16[1,2,1,2,64,1024]{5,4,3,2,1,0:T(8,128)(2,1)S(1)}, u32[]{:S(2)}, u32[]{:S(2)}) collective-permute-start(bf16[1,2,1,2,64,1024]{5,4,3,2,1,0:T(8,128)(2,1)S(1)} %slice.205), channel_id=1, source_target_pairs={{0,4},{4,0},{8,12},{12,8},{1,5},{5,1},{9,13},{13,9},{2,6},{6,2},{1... | collective-permute-start | bytes 1572872 | tf_op jit(solution)/shard_map/ppermute | solution.py:38
  214.9 13.7 %collective-permute-start.14 = (bf16[1,1,2,2,64,1024]{5,4,3,2,1,0:T(8,128)(2,1)S(1)}, bf16[1,1,2,2,64,1024]{5,4,3,2,1,0:T(8,128)(2,1)S(1)}, u32[]{:S(2)}, u32[]{:S(2)}) collective-permute-start(bf16[1,1,2,2,64,1024]{5,4,3,2,1,0:T(8,128)(2,1)S(1)} %slice.203), channel_id=1, source_target_pairs={{0,2},{1,3},{2,0},{3,1},{4,6},{5,7},{6,4},{7,5},{8,10},{9,11},{10,... | collective-permute-start | bytes 1572872 | tf_op jit(solution)/shard_map/ppermute | solution.py:38
  228.7 13.8 %collective-permute-start.17 = (bf16[1,2,1,1,64,1024]{5,4,3,2,1,0:T(8,128)(2,1)S(1)}, bf16[1,2,1,1,64,1024]{5,4,3,2,1,0:T(8,128)(2,1)S(1)}, u32[]{:S(2)}, u32[]{:S(2)}) collective-permute-start(bf16[1,2,1,1,64,1024]{5,4,3,2,1,0:T(8,128)(2,1)S(1)} %slice.209), channel_id=1, source_target_pairs={{0,8},{4,12},{8,0},{12,4},{1,9},{5,13},{9,1},{13,5},{2,10},{6,14},... | collective-permute-start | bytes 786440 | tf_op jit(solution)/shard_map/ppermute | solution.py:38
  231.3 12.3 %collective-permute-start.16 = (bf16[1,1,1,2,64,1024]{5,4,3,2,1,0:T(8,128)(2,1)S(1)}, bf16[1,1,1,2,64,1024]{5,4,3,2,1,0:T(8,128)(2,1)S(1)}, u32[]{:S(2)}, u32[]{:S(2)}) collective-permute-start(bf16[1,1,1,2,64,1024]{5,4,3,2,1,0:T(8,128)(2,1)S(1)} %slice.207), channel_id=1, source_target_pairs={{0,4},{4,0},{8,12},{12,8},{1,5},{5,1},{9,13},{13,9},{2,6},{6,2},{1... | collective-permute-start | bytes 786440 | tf_op jit(solution)/shard_map/ppermute | solution.py:38
  243.7 7.3 %collective-permute-start.18 = (bf16[1,1,1,1,64,1024]{5,4,3,2,1,0:T(8,128)(2,1)S(1)}, bf16[1,1,1,1,64,1024]{5,4,3,2,1,0:T(8,128)(2,1)S(1)}, u32[]{:S(2)}, u32[]{:S(2)}) collective-permute-start(bf16[1,1,1,1,64,1024]{5,4,3,2,1,0:T(8,128)(2,1)S(1)} %slice.211), channel_id=1, source_target_pairs={{0,8},{4,12},{8,0},{12,4},{1,9},{5,13},{9,1},{13,5},{2,10},{6,14},... | collective-permute-start | bytes 393224 | tf_op jit(solution)/shard_map/ppermute | solution.py:38
  243.8 7.2 %collective-permute-start.19 = (bf16[1,1,1,1,64,1024]{5,4,3,2,1,0:T(8,128)(2,1)S(1)}, bf16[1,1,1,1,64,1024]{5,4,3,2,1,0:T(8,128)(2,1)S(1)}, u32[]{:S(2)}, u32[]{:S(2)}) collective-permute-start(bf16[1,1,1,1,64,1024]{5,4,3,2,1,0:T(8,128)(2,1)S(1)} %slice.213), channel_id=1, source_target_pairs={{0,2},{1,3},{2,0},{3,1},{4,6},{5,7},{6,4},{7,5},{8,10},{9,11},{10,... | collective-permute-start | bytes 393224 | tf_op jit(solution)/shard_map/ppermute | solution.py:38
  258.2 17.5 %all-to-all-start.1 = ((bf16[64,16,128]{2,0,1:T(8,128)(2,1)}), bf16[64,16,128]{2,0,1:T(8,128)(2,1)}, u32[]{:S(2)}, u32[]{:S(2)}) async-start(bf16[64,16,128]{2,0,1:T(8,128)(2,1)} %copy_bitcast_fusion.1), calls=%async_computation.1 | async-start | bytes 524288 | tf_op jit(solution)/shard_map/all_to_all | solution.py:475
  262.4 198.3 %all-gather.11.cloned.1.call-start = ((), (), s32[]{:S(2)}) async-start(), calls=%async_computation.5 | async-start | bytes 4456448 | tf_op jit(solution)/shard_map/all_gather | solution.py:495
  266.6 22.0 %collective-permute-start.21 = (bf16[512,1024]{1,0:T(8,128)(2,1)}, bf16[512,1024]{1,0:T(8,128)(2,1)}, u32[]{:S(2)}, u32[]{:S(2)}) collective-permute-start(bf16[512,1024]{1,0:T(8,128)(2,1)} %fusion.38), channel_id=1, source_target_pairs={{0,1},{1,0},{2,3},{3,2},{4,5},{5,4},{6,7},{7,6},{8,9},{9,8},{10,11... | collective-permute-start | bytes 3145736 | tf_op jit(solution)/shard_map/ppermute | solution.py:38
  270.8 21.0 %collective-permute-start.20 = (bf16[512,1024]{1,0:T(8,128)(2,1)}, bf16[512,1024]{1,0:T(8,128)(2,1)}, u32[]{:S(2)}, u32[]{:S(2)}) collective-permute-start(bf16[512,1024]{1,0:T(8,128)(2,1)} %fusion.35), channel_id=1, source_target_pairs={{0,1},{1,0},{2,3},{3,2},{4,5},{5,4},{6,7},{7,6},{8,9},{9,8},{10,11... | collective-permute-start | bytes 3145736 | tf_op jit(solution)/shard_map/ppermute | solution.py:38
  295.1 22.1 %collective-permute-start.23 = (bf16[1,2,1,2,64,1024]{5,4,3,2,1,0:T(8,128)(2,1)S(1)}, bf16[1,2,1,2,64,1024]{5,4,3,2,1,0:T(8,128)(2,1)S(1)}, u32[]{:S(2)}, u32[]{:S(2)}) collective-permute-start(bf16[1,2,1,2,64,1024]{5,4,3,2,1,0:T(8,128)(2,1)S(1)} %slice.221), channel_id=1, source_target_pairs={{0,4},{4,0},{8,12},{12,8},{1,5},{5,1},{9,13},{13,9},{2,6},{6,2},{1... | collective-permute-start | bytes 1572872 | tf_op jit(solution)/shard_map/ppermute | solution.py:38
  295.9 24.6 %collective-permute-start.27 = (bf16[512,1024]{1,0:T(8,128)(2,1)S(1)}, bf16[512,1024]{1,0:T(8,128)(2,1)S(1)}, u32[]{:S(2)}, u32[]{:S(2)}) collective-permute-start(bf16[512,1024]{1,0:T(8,128)(2,1)S(1)} %convolution_convert_fusion.2), channel_id=1, source_target_pairs={{0,1},{1,0},{2,3},{3,2},{4,5},{5,4},{6,7},{7,6},{8,9},{9,8},{10,11... | collective-permute-start | bytes 3145736 | tf_op jit(solution)/shard_map/ppermute | solution.py:38
  297.6 19.8 %collective-permute-start.22 = (bf16[1,1,2,2,64,1024]{5,4,3,2,1,0:T(8,128)(2,1)S(1)}, bf16[1,1,2,2,64,1024]{5,4,3,2,1,0:T(8,128)(2,1)S(1)}, u32[]{:S(2)}, u32[]{:S(2)}) collective-permute-start(bf16[1,1,2,2,64,1024]{5,4,3,2,1,0:T(8,128)(2,1)S(1)} %slice.219), channel_id=1, source_target_pairs={{0,2},{1,3},{2,0},{3,1},{4,6},{5,7},{6,4},{7,5},{8,10},{9,11},{10,... | collective-permute-start | bytes 1572872 | tf_op jit(solution)/shard_map/ppermute | solution.py:38
  299.9 22.2 %collective-permute-start.26 = (bf16[512,1024]{1,0:T(8,128)(2,1)S(1)}, bf16[512,1024]{1,0:T(8,128)(2,1)S(1)}, u32[]{:S(2)}, u32[]{:S(2)}) collective-permute-start(bf16[512,1024]{1,0:T(8,128)(2,1)S(1)} %convolution_convert_fusion.3), channel_id=1, source_target_pairs={{0,1},{1,0},{2,3},{3,2},{4,5},{5,4},{6,7},{7,6},{8,9},{9,8},{10,11... | collective-permute-start | bytes 3145736 | tf_op jit(solution)/shard_map/ppermute | solution.py:38
  300.0 93.8 %collective-permute-start.34 = (bf16[1024,2048]{1,0:T(8,128)(2,1)}, bf16[1024,2048]{1,0:T(8,128)(2,1)}, u32[]{:S(2)}, u32[]{:S(2)}) collective-permute-start(bf16[1024,2048]{1,0:T(8,128)(2,1)} %convolution_convert_fusion), channel_id=1, source_target_pairs={{0,16},{16,0},{1,17},{17,1},{2,18},{18,2},{3,19},{19,3},{4,20},{20... | collective-permute-start | bytes 12582920 | tf_op jit(solution)/shard_map/ppermute | solution.py:313
  317.7 14.9 %collective-permute-start.25 = (bf16[1,2,1,1,64,1024]{5,4,3,2,1,0:T(8,128)(2,1)S(1)}, bf16[1,2,1,1,64,1024]{5,4,3,2,1,0:T(8,128)(2,1)S(1)}, u32[]{:S(2)}, u32[]{:S(2)}) collective-permute-start(bf16[1,2,1,1,64,1024]{5,4,3,2,1,0:T(8,128)(2,1)S(1)} %slice.225), channel_id=1, source_target_pairs={{0,8},{4,12},{8,0},{12,4},{1,9},{5,13},{9,1},{13,5},{2,10},{6,14},... | collective-permute-start | bytes 786440 | tf_op jit(solution)/shard_map/ppermute | solution.py:38
  319.8 13.1 %collective-permute-start.24 = (bf16[1,1,1,2,64,1024]{5,4,3,2,1,0:T(8,128)(2,1)S(1)}, bf16[1,1,1,2,64,1024]{5,4,3,2,1,0:T(8,128)(2,1)S(1)}, u32[]{:S(2)}, u32[]{:S(2)}) collective-permute-start(bf16[1,1,1,2,64,1024]{5,4,3,2,1,0:T(8,128)(2,1)S(1)} %slice.223), channel_id=1, source_target_pairs={{0,4},{4,0},{8,12},{12,8},{1,5},{5,1},{9,13},{13,9},{2,6},{6,2},{1... | collective-permute-start | bytes 786440 | tf_op jit(solution)/shard_map/ppermute | solution.py:38
  333.0 7.2 %collective-permute-start.29 = (bf16[1,1,1,1,64,1024]{5,4,3,2,1,0:T(8,128)(2,1)S(1)}, bf16[1,1,1,1,64,1024]{5,4,3,2,1,0:T(8,128)(2,1)S(1)}, u32[]{:S(2)}, u32[]{:S(2)}) collective-permute-start(bf16[1,1,1,1,64,1024]{5,4,3,2,1,0:T(8,128)(2,1)S(1)} %slice.231), channel_id=1, source_target_pairs={{0,2},{1,3},{2,0},{3,1},{4,6},{5,7},{6,4},{7,5},{8,10},{9,11},{10,... | collective-permute-start | bytes 393224 | tf_op jit(solution)/shard_map/ppermute | solution.py:38
  338.3 21.0 %collective-permute-start.31 = (bf16[1,2,1,2,64,1024]{5,4,3,2,1,0:T(8,128)(2,1)}, bf16[1,2,1,2,64,1024]{5,4,3,2,1,0:T(8,128)(2,1)}, u32[]{:S(2)}, u32[]{:S(2)}) collective-permute-start(bf16[1,2,1,2,64,1024]{5,4,3,2,1,0:T(8,128)(2,1)} %slice.235), channel_id=1, source_target_pairs={{0,4},{4,0},{8,12},{12,8},{1,5},{5,1},{9,13},{13,9},{2,6},{6,2},{1... | collective-permute-start | bytes 1572872 | tf_op jit(solution)/shard_map/ppermute | solution.py:38
  338.6 13.5 %collective-permute-start.28 = (bf16[1,1,1,1,64,1024]{5,4,3,2,1,0:T(8,128)(2,1)S(1)}, bf16[1,1,1,1,64,1024]{5,4,3,2,1,0:T(8,128)(2,1)S(1)}, u32[]{:S(2)}, u32[]{:S(2)}) collective-permute-start(bf16[1,1,1,1,64,1024]{5,4,3,2,1,0:T(8,128)(2,1)S(1)} %slice.229), channel_id=1, source_target_pairs={{0,8},{4,12},{8,0},{12,4},{1,9},{5,13},{9,1},{13,5},{2,10},{6,14},... | collective-permute-start | bytes 393224 | tf_op jit(solution)/shard_map/ppermute | solution.py:38
  353.0 87.9 %collective-permute-start.42 = (bf16[1024,1024]{1,0:T(8,128)(2,1)}, bf16[1024,1024]{1,0:T(8,128)(2,1)S(1)}, u32[]{:S(2)}, u32[]{:S(2)}) collective-permute-start(bf16[1024,1024]{1,0:T(8,128)(2,1)} %convolution_convert_fusion.1), channel_id=1, source_target_pairs={{0,16},{16,0},{1,17},{17,1},{2,18},{18,2},{3,19},{19,3},{4,20},{20... | collective-permute-start | bytes 6291464 | tf_op jit(solution)/shard_map/ppermute | solution.py:313
  355.7 14.7 %collective-permute-start.30 = (bf16[1,1,2,2,64,1024]{5,4,3,2,1,0:T(8,128)(2,1)S(1)}, bf16[1,1,2,2,64,1024]{5,4,3,2,1,0:T(8,128)(2,1)S(1)}, u32[]{:S(2)}, u32[]{:S(2)}) collective-permute-start(bf16[1,1,2,2,64,1024]{5,4,3,2,1,0:T(8,128)(2,1)S(1)} %slice.233), channel_id=1, source_target_pairs={{0,2},{1,3},{2,0},{3,1},{4,6},{5,7},{6,4},{7,5},{8,10},{9,11},{10,... | collective-permute-start | bytes 1572872 | tf_op jit(solution)/shard_map/ppermute | solution.py:38
  370.6 23.7 %copy-start.3 = (bf16[1024,2048]{1,0:T(8,128)(2,1)S(1)}, bf16[1024,2048]{1,0:T(8,128)(2,1)}, u32[]{:S(2)}) copy-start(bf16[1024,2048]{1,0:T(8,128)(2,1)} %shard_map.164) | copy-start | bytes 12582916
  370.6 15.7 %collective-permute-start.33 = (bf16[1,2,1,1,64,1024]{5,4,3,2,1,0:T(8,128)(2,1)S(1)}, bf16[1,2,1,1,64,1024]{5,4,3,2,1,0:T(8,128)(2,1)S(1)}, u32[]{:S(2)}, u32[]{:S(2)}) collective-permute-start(bf16[1,2,1,1,64,1024]{5,4,3,2,1,0:T(8,128)(2,1)S(1)} %slice.239), channel_id=1, source_target_pairs={{0,8},{4,12},{8,0},{12,4},{1,9},{5,13},{9,1},{13,5},{2,10},{6,14},... | collective-permute-start | bytes 786440 | tf_op jit(solution)/shard_map/ppermute | solution.py:38
  380.6 8.4 %collective-permute-start.32 = (bf16[1,1,1,2,64,1024]{5,4,3,2,1,0:T(8,128)(2,1)S(1)}, bf16[1,1,1,2,64,1024]{5,4,3,2,1,0:T(8,128)(2,1)S(1)}, u32[]{:S(2)}, u32[]{:S(2)}) collective-permute-start(bf16[1,1,1,2,64,1024]{5,4,3,2,1,0:T(8,128)(2,1)S(1)} %slice.237), channel_id=1, source_target_pairs={{0,4},{4,0},{8,12},{12,8},{1,5},{5,1},{9,13},{13,9},{2,6},{6,2},{1... | collective-permute-start | bytes 786440 | tf_op jit(solution)/shard_map/ppermute | solution.py:38
  393.8 16.6 %collective-permute-start.36 = (bf16[1,1,1,1,64,1024]{5,4,3,2,1,0:T(8,128)(2,1)S(1)}, bf16[1,1,1,1,64,1024]{5,4,3,2,1,0:T(8,128)(2,1)S(1)}, u32[]{:S(2)}, u32[]{:S(2)}) collective-permute-start(bf16[1,1,1,1,64,1024]{5,4,3,2,1,0:T(8,128)(2,1)S(1)} %slice.243), channel_id=1, source_target_pairs={{0,2},{1,3},{2,0},{3,1},{4,6},{5,7},{6,4},{7,5},{8,10},{9,11},{10,... | collective-permute-start | bytes 393224 | tf_op jit(solution)/shard_map/ppermute | solution.py:38
  398.8 13.6 %collective-permute-start.35 = (bf16[1,1,1,1,64,1024]{5,4,3,2,1,0:T(8,128)(2,1)S(1)}, bf16[1,1,1,1,64,1024]{5,4,3,2,1,0:T(8,128)(2,1)S(1)}, u32[]{:S(2)}, u32[]{:S(2)}) collective-permute-start(bf16[1,1,1,1,64,1024]{5,4,3,2,1,0:T(8,128)(2,1)S(1)} %slice.241), channel_id=1, source_target_pairs={{0,8},{4,12},{8,0},{12,4},{1,9},{5,13},{9,1},{13,5},{2,10},{6,14},... | collective-permute-start | bytes 393224 | tf_op jit(solution)/shard_map/ppermute | solution.py:38
  410.3 19.0 %copy-start.34 = (bf16[1024,2048]{1,0:T(8,128)(2,1)S(1)}, bf16[1024,2048]{1,0:T(8,128)(2,1)}, u32[]{:S(2)}) copy-start(bf16[1024,2048]{1,0:T(8,128)(2,1)} %all-gather.9.cloned.1.call-done) | copy-start | bytes 12582916
  413.8 1.4 collective-permute-start.39
  415.3 4.4 collective-permute-start.43
  418.0 5.7 %collective-permute-start.38 = (bf16[1,1,1,1,64,1024]{5,4,3,2,1,0:T(8,128)(2,1)S(1)}, bf16[1,1,1,1,64,1024]{5,4,3,2,1,0:T(8,128)(2,1)S(1)}, u32[]{:S(2)}, u32[]{:S(2)}) collective-permute-start(bf16[1,1,1,1,64,1024]{5,4,3,2,1,0:T(8,128)(2,1)S(1)} %get-tuple-element.114), channel_id=1, source_target_pairs={{0,2},{1,3},{2,0},{3,1},{4,6},{5,7},{6,4},{7,5},{8,10},{9,11},{10,... | collective-permute-start | bytes 393224 | tf_op jit(solution)/shard_map/ppermute | solution.py:38
  418.1 9.4 %collective-permute-start.37 = (bf16[1,1,1,1,64,1024]{5,4,3,2,1,0:T(8,128)(2,1)S(1)}, bf16[1,1,1,1,64,1024]{5,4,3,2,1,0:T(8,128)(2,1)S(1)}, u32[]{:S(2)}, u32[]{:S(2)}) collective-permute-start(bf16[1,1,1,1,64,1024]{5,4,3,2,1,0:T(8,128)(2,1)S(1)} %get-tuple-element.113), channel_id=1, source_target_pairs={{0,8},{4,12},{8,0},{12,4},{1,9},{5,13},{9,1},{13,5},{2,10},{6,14},... | collective-permute-start | bytes 393224 | tf_op jit(solution)/shard_map/ppermute | solution.py:38
  427.5 13.2 %collective-permute-start.41 = (bf16[1,2,1,1,64,1024]{5,4,3,2,1,0:T(8,128)(2,1)S(1)}, bf16[1,2,1,1,64,1024]{5,4,3,2,1,0:T(8,128)(2,1)S(1)}, u32[]{:S(2)}, u32[]{:S(2)}) collective-permute-start(bf16[1,2,1,1,64,1024]{5,4,3,2,1,0:T(8,128)(2,1)S(1)} %pad_maximum_fusion.15), channel_id=1, source_target_pairs={{0,8},{4,12},{8,0},{12,4},{1,9},{5,13},{9,1},{13,5},{2,10},{6,14},... | collective-permute-start | bytes 786440 | tf_op jit(solution)/shard_map/ppermute | solution.py:38
  427.6 13.3 %collective-permute-start.40 = (bf16[1,1,1,2,64,1024]{5,4,3,2,1,0:T(8,128)(2,1)S(1)}, bf16[1,1,1,2,64,1024]{5,4,3,2,1,0:T(8,128)(2,1)S(1)}, u32[]{:S(2)}, u32[]{:S(2)}) collective-permute-start(bf16[1,1,1,2,64,1024]{5,4,3,2,1,0:T(8,128)(2,1)S(1)} %pad_maximum_fusion.14), channel_id=1, source_target_pairs={{0,4},{4,0},{8,12},{12,8},{1,5},{5,1},{9,13},{13,9},{2,6},{6,2},{1... | collective-permute-start | bytes 786440 | tf_op jit(solution)/shard_map/ppermute | solution.py:38
  430.8 29.9 %collective-permute-start.46 = (bf16[1024,512]{0,1:T(8,128)(2,1)S(1)}, bf16[1024,512]{0,1:T(8,128)(2,1)}, u32[]{:S(2)}, u32[]{:S(2)}) collective-permute-start(bf16[1024,512]{0,1:T(8,128)(2,1)S(1)} %pad_maximum_fusion.6), channel_id=1, source_target_pairs={{0,16},{16,0},{1,17},{17,1},{2,18},{18,2},{3,19},{19,3},{4,20},{20... | collective-permute-start | bytes 3145736 | tf_op jit(solution)/shard_map/ppermute | solution.py:313
  441.0 14.1 %collective-permute-start.45 = (bf16[1,2,1,2,64,1024]{5,4,3,2,1,0:T(8,128)(2,1)S(1)}, bf16[1,2,1,2,64,1024]{5,4,3,2,1,0:T(8,128)(2,1)S(1)}, u32[]{:S(2)}, u32[]{:S(2)}) collective-permute-start(bf16[1,2,1,2,64,1024]{5,4,3,2,1,0:T(8,128)(2,1)S(1)} %pad_maximum_fusion.10), channel_id=1, source_target_pairs={{0,4},{4,0},{8,12},{12,8},{1,5},{5,1},{9,13},{13,9},{2,6},{6,2},{1... | collective-permute-start | bytes 1572872 | tf_op jit(solution)/shard_map/ppermute | solution.py:38
  441.3 13.9 %collective-permute-start.44 = (bf16[1,1,2,2,64,1024]{5,4,3,2,1,0:T(8,128)(2,1)S(1)}, bf16[1,1,2,2,64,1024]{5,4,3,2,1,0:T(8,128)(2,1)S(1)}, u32[]{:S(2)}, u32[]{:S(2)}) collective-permute-start(bf16[1,1,2,2,64,1024]{5,4,3,2,1,0:T(8,128)(2,1)S(1)} %pad_maximum_fusion.9), channel_id=1, source_target_pairs={{0,2},{1,3},{2,0},{3,1},{4,6},{5,7},{6,4},{7,5},{8,10},{9,11},{10,... | collective-permute-start | bytes 1572872 | tf_op jit(solution)/shard_map/ppermute | solution.py:38
  443.0 12.1 %collective-permute-start.47 = (f32[2,2048]{1,0:T(2,128)S(1)}, f32[2,2048]{1,0:T(2,128)S(1)}, u32[]{:S(2)}, u32[]{:S(2)}) collective-permute-start(f32[2,2048]{1,0:T(2,128)S(1)} %fusion.185), channel_id=1, source_target_pairs={{0,4},{4,0},{8,12},{12,8},{1,5},{5,1},{9,13},{13,9},{2,6},{6,2},{1... | collective-permute-start | bytes 49160 | tf_op jit(solution)/shard_map/ppermute | solution.py:38
  455.3 22.7 %copy-start.28 = (bf16[1,1024,128]{2,1,0:T(8,128)(2,1)S(1)}, bf16[1,1024,128]{2,1,0:T(8,128)(2,1)}, u32[]{:S(2)}) copy-start(bf16[1,1024,128]{2,1,0:T(8,128)(2,1)} %copy-done.27) | copy-start | bytes 786436
  460.7 24.8 %collective-permute-start.48 = (bf16[1,2,2,2,64,1024]{5,4,3,2,1,0:T(8,128)(2,1)S(1)}, bf16[1,2,2,2,64,1024]{5,4,3,2,1,0:T(8,128)(2,1)S(1)}, u32[]{:S(2)}, u32[]{:S(2)}) collective-permute-start(bf16[1,2,2,2,64,1024]{5,4,3,2,1,0:T(8,128)(2,1)S(1)} %pad_maximum_fusion.4), channel_id=1, source_target_pairs={{0,1},{1,0},{2,3},{3,2},{4,5},{5,4},{6,7},{7,6},{8,9},{9,8},{10,11... | collective-permute-start | bytes 3145736 | tf_op jit(solution)/shard_map/ppermute | solution.py:38
  460.7 24.8 %collective-permute-start.49 = (bf16[1,2,2,2,64,1024]{5,4,3,2,1,0:T(8,128)(2,1)S(1)}, bf16[1,2,2,2,64,1024]{5,4,3,2,1,0:T(8,128)(2,1)}, u32[]{:S(2)}, u32[]{:S(2)}) collective-permute-start(bf16[1,2,2,2,64,1024]{5,4,3,2,1,0:T(8,128)(2,1)S(1)} %pad_maximum_fusion.5), channel_id=1, source_target_pairs={{0,1},{1,0},{2,3},{3,2},{4,5},{5,4},{6,7},{7,6},{8,9},{9,8},{10,11... | collective-permute-start | bytes 3145736 | tf_op jit(solution)/shard_map/ppermute | solution.py:38
  461.3 4.6 collective-permute-start.50
  465.9 3.8 collective-permute-start.51
  (36 other events, 232.5 us)
Sparse Core Ops, SparseCore 0:
  10.8 59.8 all-gather.4
  72.9 53.4 all-gather.6
  256.6 56.9 all-gather.8
  353.1 62.7 all-gather.10

commit v3 on v2

--- a/solution.py
+++ b/solution.py
@@ -25,6 +25,31 @@
 ORDER_B = ("core", "z0", "z1", "x")
 
 
+PLAN = {
+    "make": {
+        "core2": ("in0", "in0_got"),
+        "two1": ("in1", "in1_got", "out", "out_got"),
+        "two2": ("mix_send",),
+        "do": ("branch", "mix0", "mix1"),
+        "blocks": ("mix2",),
+        "core1": ("qkv",),
+        "one1": ("mix3",),
+        "one2": ("in_whole", "attention", "attention_got"),
+        "one3": ("output",),
+        "stage1": ("out_whole",),
+    },
+    "wait": {
+        "two1": ("in0",),
+        "two2": ("out",),
+        "one1": ("qkv",),
+        "one2": ("in0_got",),
+        "one3": ("in_whole", "mix3"),
+        "stage1": ("out_got",),
+        "stage2": ("output", "out_whole", "attention_got"),
+    },
+}
+
+
 def dot(a, b, ca=1, cb=0):
     return lax.dot_general(a, b, (((ca,), (cb,)), ((), ())), preferred_element_type=F32)
 
@@ -42,39 +67,33 @@
     return list(lax.optimization_barrier((*values, *gates))[: len(values)])
 
 
-def reduce_rest(parts, gates=((), (), ()), orders=(ORDER_A, ORDER_B)):
-    rows, cols = parts[0].shape
-    now = [v.reshape(1, 2, 2, 2, rows // 8, cols) for v in parts]
-    sent, after_step = [], []
-    for i in range(3):
-        now = hold(now, *gates[i])
-        steps = [order[i + 1] for order in orders]
-        send = [lax.slice_in_dim(v, 1, 2, axis=STEPS[s][2]) for v, s in zip(now, steps)]
-        mine = [lax.slice_in_dim(v, 0, 1, axis=STEPS[s][2]) for v, s in zip(now, steps)]
-        got = [swap(v, s) for v, s in zip(send, steps)]
-        now = [(m.astype(F32) + g.astype(F32)).astype(BF) for m, g in zip(mine, got)]
-        sent.append(send)
-        after_step.append(now)
-    return [v.reshape(rows // 8, cols) for v in now], sent, after_step
+def reduce_step(v, step):
+    dim = STEPS[step][2]
+    got = swap(lax.slice_in_dim(v, 1, 2, axis=dim), step)
+    return (lax.slice_in_dim(v, 0, 1, axis=dim).astype(F32) + got.astype(F32)).astype(BF)
+
+
+def chain_step(parts, i):
+    return [reduce_step(v, order[i]) for v, order in zip(parts, (ORDER_A, ORDER_B))]
 
 
 def reduce_first(left, rights, *gates):
     half = left.shape[0] // 2
-    pair = []
+    pair, sends = [], []
     later = after(left, *gates) if gates else left
     for right in rights:
-        got = swap(dot(left[half:], right, 1, 1).astype(BF), "core")
+        sends.append(dot(left[half:], right, 1, 1).astype(BF))
+        got = swap(sends[-1], "core")
         pair.append((dot(later[:half], right, 1, 1) + got.astype(F32)).astype(BF))
-    return pair
-
-
-def gather_chain(parts, gates=((), (), (), ()), orders=(ORDER_A, ORDER_B), vector=None):
+    return pair, sends
+
+
+def gather_chain(parts, orders=(ORDER_A, ORDER_B), vector=None, event=None):
     rows, cols = parts[0].shape
     now = [v.reshape(1, 1, 1, 1, rows, cols) for v in parts]
-    stages = []
     for i in range(4):
-        now = hold(now, *gates[i], *([] if vector is None else [vector]))
         if vector is not None:
+            now = hold(now, vector)
             vector = vector + swap(vector, ORDER_A[i])
         steps = [order[3 - i] for order in orders]
         got = [swap(v, step) for v, step in zip(now, steps)]
@@ -83,9 +102,10 @@
                 jnp.concatenate([v, g], axis=STEPS[step][2])
                 for v, g, step in zip(now, got, steps)
             ]
-            stages.append(now)
+            if event is not None:
+                now = event("stage%d" % i, now)
     flat_rows = [[v.reshape(8 * rows, cols) for v in pair] for pair in zip(now, got)]
-    return flat_rows, stages, vector
+    return flat_rows, vector
 
 
 def whole(pairs):
@@ -186,42 +206,58 @@
     )(*weights)
 
 
-def unflat_sum(own, got, shape, order):
+def weight_sum(left, right, got, column, shape, order, planes=False):
     rows, wide = min(256, shape[0]), shape[-1]
+    tokens, columns = right.shape
     spots = indices(shape, order)
-
-    def kernel(own_ref, got_ref, out):
+    widths = [columns] if column or len(got) == 1 else [v.shape[1] for v in got]
+    homes = [(k, at) for k, w in enumerate(widths) for at in range(0, w, wide)]
+
+    def kernel(left_ref, right_ref, *refs):
+        out = refs[-1]
+        total = dot(left_ref[...], right_ref[...], 0, 0)
         for j, spot in enumerate(spots):
-            here = slice(j * wide, (j + 1) * wide)
-            out[(slice(None), *spot, slice(None))] = own_ref[:, here] + got_ref[:, here].astype(F32)
+            k, at = homes[j]
+            here = refs[k][:, at : at + wide].astype(F32)
+            at = (*spot, slice(None)) if planes else (slice(None), *spot)
+            out[(*at, slice(None))] = total[:, j * wide : (j + 1) * wide] + here
 
     zeros = (0,) * (len(shape) - 1)
+    block, where = (rows, *shape[1:]), lambda i: (i, *zeros)
+    if planes:
+        block, where = (shape[1], rows, wide), lambda i: (0, i, 0)
+        shape = (shape[1], shape[0], wide)
     return pl.pallas_call(
         kernel,
-        grid=(shape[0] // rows,),
+        grid=(left.shape[1] // rows,),
         in_specs=[
-            pl.BlockSpec((rows, own.shape[1]), lambda i: (i, 0)),
-            pl.BlockSpec((rows, own.shape[1]), lambda i: (i, 0)),
-        ],
-        out_specs=pl.BlockSpec((rows, *shape[1:]), lambda i: (i, *zeros)),
+            pl.BlockSpec((tokens, rows), lambda i: (0, i)),
+            pl.BlockSpec((tokens, columns), lambda i: (0, 0)),
+        ]
+        + [pl.BlockSpec((rows, w), lambda i: (i, column)) for w in widths],
+        out_specs=pl.BlockSpec(block, where),
         out_shape=jax.ShapeDtypeStruct(shape, F32),
         compiler_params=pltpu.CompilerParams(vmem_limit_bytes=VMEM_LIMIT),
-        cost_estimate=pl.CostEstimate(flops=0, bytes_accessed=own.size * 10, transcendentals=0),
-    )(own, got)
-
-
-def experts(first, named, top, h, grad_out, weights, count):
+        cost_estimate=pl.CostEstimate(
+            flops=2 * tokens * left.shape[1] * columns,
+            bytes_accessed=2 * left.size + 2 * right.size + 6 * left.shape[1] * columns,
+            transcendentals=0,
+        ),
+    )(left, right, *got)
+
+
+def experts(first, named, top, h, grad_part, grad_rest, weights, count):
     tokens, half = h[0].shape
     wide = weights[0].shape[1] // (3 * count)
     rows = min(1024, tokens)
 
-    def kernel(first_ref, named_ref, ha, hb, wa, wb, ga, gb, oa, ob, act_ref, grad_ref):
+    def kernel(first_ref, named_ref, ha, hb, wa, wb, part, gb, ob, act_ref, grad_ref):
         mine = (first_ref[0] + pl.program_id(0)).astype(F32)
         named = named_ref[...]
         weight = jnp.sum(
             jnp.where(named[:, :top] == mine, named[:, top : 2 * top], 0.0), 1, keepdims=True
         )
-        grad = weight * (dot(ga[...], oa[...]) + dot(gb[...], ob[...]))
+        grad = weight * (part[...] + dot(gb[...], ob[...]))
         both = dot(ha[...], wa[...]) + dot(hb[...], wb[...])
         gate, up = both[:, :wide], both[:, wide:]
         sig = 1.0 / (1.0 + jnp.exp(-gate))
@@ -249,9 +285,8 @@
             by_rows(half),
             by_expert(2 * wide, 0),
             by_expert(2 * wide, 0),
+            out(wide),
             by_rows(half),
-            by_rows(half),
-            by_expert(wide, 2 * count),
             by_expert(wide, 2 * count),
         ],
         out_specs=[out(wide), out(2 * wide)],
@@ -261,11 +296,11 @@
         ],
         compiler_params=pltpu.CompilerParams(vmem_limit_bytes=VMEM_LIMIT),
         cost_estimate=pl.CostEstimate(
-            flops=12 * tokens * half * count * wide,
+            flops=10 * tokens * half * count * wide,
             bytes_accessed=16 * tokens * half + 12 * half * count * wide,
             transcendentals=tokens * count * wide,
         ),
-    )(first.reshape(1), named, *h, *weights, *grad_out, *weights)
+    )(first.reshape(1), named, *h, *weights, grad_part, grad_rest, weights[1])
 
 
 def ordered(pairs, start, dtype, tile=512):
@@ -342,23 +377,19 @@
 
 
 def partner_part(left, right):
-    return dot(left[1], right, 0, 0).astype(BF) if two_way() else None
-
-
-def own_part(left, right):
-    if two_way():
-        return dot(left[0], right, 0, 0)
-    whole = jnp.concatenate([dot(part, right, 0, 0) for part in left], axis=0)
-    return lax.psum_scatter(whole, "fsdp", scatter_dimension=0, tiled=True)
+    return dot(left[1], right, 0, 0).astype(BF)
 
 
 def beside(*parts):
     return jnp.concatenate(parts, axis=1) if two_way() else None
 
 
-def restore(own, got, shape, order):
+def weight_grad(left, right, got, column, shape, order, planes=False):
     if two_way():
-        return unflat_sum(own, got, shape, order)
+        total = weight_sum(left[0], right, got, column, shape, order, planes)
+        return total.transpose(1, 0, 2) if planes else total
+    both = jnp.concatenate([dot(part, right, 0, 0) for part in left], axis=0)
+    own = lax.psum_scatter(both, "fsdp", scatter_dimension=0, tiled=True)
     lead = [shape[1 + i] for i in order]
     turned = own.reshape(shape[0], *lead, shape[-1])
     back = [1 + order.index(i) for i in range(len(order))]
@@ -405,13 +436,12 @@
     w_qkv = spread(attn_qkv.astype(BF).reshape(-1, 3 * head_width))
     w_o_own = after(attn_out.astype(BF).T, w_qkv[0])
     w_o = spread(w_o_own, 1)
-    w_experts = flat([expert_in, expert_out], [(1, 0), (0,)])
-    w_qkv = w_qkv[0], after(w_qkv[1], w_experts)
-    w_experts = spread(after(w_experts, w_qkv[1]))
+    w_experts_own = flat([expert_in, expert_out], [(1, 0), (0,)])
+    w_experts = spread(after(w_experts_own, w_o_own))
     w_in = [w[:, : 2 * columns] for w in w_experts]
     w_out = [w[:, 2 * columns :] for w in w_experts]
 
-    x = [v.astype(F32) for v in halves(tokens)]
+    x = [v.astype(F32) for v in halves(after(tokens, w_experts_own))]
     r_one = rms(*x)
     h_one = [(v * r_one * g).astype(BF) for v, g in zip(x, gain_one)]
     projected = (dot(h_one[0], w_qkv[0]) + dot(h_one[1], w_qkv[1])).astype(BF)
@@ -442,6 +472,8 @@
     grad_out = reorder([cotangent], rank, BF, shift=start)
     attended_rows = after(attended_rows, grad_out)
     grad_out = grad_out[:, :half], grad_out[:, half:]
+    grad_act_own = dot(grad_out[0], w_out[0])
+    attended_rows = after(attended_rows, grad_act_own)
     x_rows = halves(lax.dynamic_slice_in_dim(tokens, rank * shard, shard, 0))
     x_rows = [v.astype(F32) for v in x_rows]
     middle = [v + dot(attended_rows, w) for v, w in zip(x_rows, w_o_full)]
@@ -450,17 +482,98 @@
     h_two_rows = [(n * g).astype(BF) for n, g in zip(n_two, gain_two)]
     h_two = whole(gather_chain(h_two_rows)[0])
 
-    act, grad_gate_up = experts(first_expert, named, top, h_two, grad_out, w_experts, own_experts)
-    grad_two = reduce_first(grad_gate_up, w_in)
-    act_late, grad_gate_up_late = hold([act, grad_gate_up], *grad_two)
-    expert_in_part = partner_part(h_two, grad_gate_up_late)
-    expert_in_got = across(expert_in_part)
-    expert_out_part = partner_part(grad_out, after(act_late, expert_in_part))
-    expert_out_got = across(expert_out_part)
-    grad_two, _, steps_two = reduce_rest(
-        grad_two, ((), [expert_in_part], [expert_out_part])
-    )
-    grad_two = [g.astype(F32) for g in grad_two]
+    act, grad_gate_up = experts(
+        first_expert, named, top, h_two, grad_act_own, grad_out[1], w_experts, own_experts
+    )
+    done = {}
+
+    def weight_part(left, right, begin, end):
+        def make(gates):
+            if not two_way() or begin == end:
+                return ()
+            return partner_part(left, after(right, *gates)[:, begin:end])
+
+        return make
+
+    def moved(name):
+        return lambda gates: jax.tree.map(across, done[name])
+
+    def mixture_step(before, i):
+        return lambda gates: chain_step(hold(done[before], *gates), i)
+
+    def mixture_sends(gates):
+        left = after(act, *gates)[tok_count // 2 :]
+        return [dot(left, w, 1, 1).astype(BF) for w in w_out]
+
+    def mixture_core(gates):
+        left = after(act, *gates)[: tok_count // 2]
+        pair = [
+            (dot(left, w, 1, 1) + swap(v, "core").astype(F32)).astype(BF)
+            for w, v in zip(w_out, done["mix_send"])
+        ]
+        return [v.reshape(1, 2, 2, 2, shard, half) for v in pair]
+
+    def gather_branch(gates):
+        rows = jnp.concatenate(hold(grad_branch_rows, *gates), axis=1)
+        return lax.all_gather(rows, GROUP, axis=0, tiled=True)
+
+    def gather_output(gates):
+        pair = [v.reshape(shard, half) for v in done["mix3"]]
+        rows = join(*[(a + b.astype(F32)).astype(BF) for a, b in zip(middle, pair)])
+        return lax.all_gather(after(rows, done["branch"]), GROUP, axis=0, tiled=True)
+
+    def branch_halves():
+        return done["branch"][:, :half], done["branch"][:, half:]
+
+    def attention_parts(gates):
+        if not two_way():
+            return ()
+        return beside(done["qkv"], partner_part(branch_halves(), attended))
+
+    def expert_in_whole(gates):
+        moves = jax.tree.leaves((done["in0_got"], done["in1_got"]))
+        right = after(grad_gate_up, *gates)
+        return weight_grad(h_two, right, moves, 0, expert_in.shape, (1, 0))
+
+    def expert_out_whole(gates):
+        right = after(act, *gates)
+        return weight_grad(grad_out, right, [done["out_got"]], 0, expert_out.shape, (0,))
+
+    split = 2 * columns
+    make = {
+        "in0": weight_part(h_two, grad_gate_up, 0, split),
+        "in0_got": moved("in0"),
+        "in1": weight_part(h_two, grad_gate_up, split, 2 * columns),
+        "in1_got": moved("in1"),
+        "out": weight_part(grad_out, act, 0, columns),
+        "out_got": moved("out"),
+        "mix_send": mixture_sends,
+        "mix0": mixture_core,
+        "mix1": mixture_step("mix0", 1),
+        "mix2": mixture_step("mix1", 2),
+        "mix3": mixture_step("mix2", 3),
+        "branch": gather_branch,
+        "output": gather_output,
+        "qkv": lambda gates: partner_part(h_one, after(grad_projected, *gates)),
+        "attention": attention_parts,
+        "attention_got": moved("attention"),
+        "in_whole": expert_in_whole,
+        "out_whole": expert_out_whole,
+    }
+
+    def event(name, values):
+        waits = [v for piece in PLAN["wait"].get(name, ()) for v in jax.tree.leaves(done[piece])]
+        values = hold(values, *waits)
+        for piece in PLAN["make"].get(name, ()):
+            done[piece] = make[piece](values)
+        return values
+
+    grad_two, _ = reduce_first(grad_gate_up, w_in)
+    event("core2", grad_two)
+    chain = [v.reshape(1, 2, 2, 2, shard, half) for v in grad_two]
+    for i, name in ((1, "two1"), (2, "two2"), (3, "two3")):
+        chain = event(name, chain_step(chain, i))
+    grad_two = [v.reshape(shard, half).astype(F32) for v in chain]
 
     out_in_rows = halves(lax.dynamic_slice_in_dim(cotangent, rank * shard, shard, 0))
     out_in_rows = [v.astype(F32) for v in out_in_rows]
@@ -472,7 +585,9 @@
     grad_attended_rows = (
         dot(grad_branch_rows[0], w_o_full[0], 1, 1) + dot(grad_branch_rows[1], w_o_full[1], 1, 1)
     ).astype(BF)
+    event("do", [grad_attended_rows])
     grad_attended = lax.all_to_all(grad_attended_rows, GROUP, 1, 0, tiled=True)
+    grad_attended = event("a2a", [grad_attended])[0]
     grad_attended = grad_attended.reshape(seq_count, SEQ_LEN, head_width)
 
     grad_v = jnp.einsum("sqk,sqe->ske", probs.astype(BF), grad_attended, preferred_element_type=F32)
@@ -481,30 +596,17 @@
     grad_scores = grad_scores.astype(BF)
     grad_q = jnp.einsum("sqk,ske->sqe", grad_scores, k, preferred_element_type=F32) * score_scale
     grad_k = jnp.einsum("sqk,sqe->ske", grad_scores, q, preferred_element_type=F32) * score_scale
+    grad_q, grad_k = event("qk", [grad_q, grad_k])
     grad_projected = jnp.concatenate([grad_q, grad_k, grad_v], axis=-1)
     grad_projected = grad_projected.reshape(tok_count, 3 * head_width).astype(BF)
     grad_projected_blocks = reorder([grad_projected], rank, BF, tile=3 * head_width)
-    grad_one = reduce_first(grad_projected_blocks, w_qkv)
-    qkv_part = partner_part(h_one, after(grad_projected, *grad_one))
-
-    mixture = reduce_first(after(act_late, *steps_two[1]), w_out, grad_attended_rows)
-    mixture = reduce_rest(mixture, ((), [grad_projected_blocks], grad_one))[0]
-    grad_branch = jnp.concatenate(hold(grad_branch_rows, grad_attended_rows), axis=1)
-    grad_branch = lax.all_gather(grad_branch, GROUP, axis=0, tiled=True)
-    out_rows = join(*[(a + b.astype(F32)).astype(BF) for a, b in zip(middle, mixture)])
-    output = lax.all_gather(after(out_rows, grad_branch), GROUP, axis=0, tiled=True)
-    grad_branch = grad_branch[:, :half], grad_branch[:, half:]
-    out_part = partner_part(grad_branch, attended)
-    attention_got = across(beside(qkv_part, out_part))
-    grad_one, _, steps_one = reduce_rest(grad_one, ((), [qkv_part], [mixture[0], expert_in_got]))
-    own_act, own_gate_up = hold([act, grad_gate_up], grad_attended_rows)
-    expert_in_own = own_part(h_two, own_gate_up)
-    expert_out_own = own_part(grad_out, after(own_act, *steps_one[0]))
-    expert_in_grad = restore(
-        expert_in_own, after(expert_in_got, *steps_one[1]), expert_in.shape, (1, 0)
-    )
-    grad_one = hold(grad_one, expert_in_grad, expert_out_own)
-    grad_one = [g.astype(F32) for g in grad_one]
+    event("blocks", [grad_projected_blocks])
+    grad_one, _ = reduce_first(grad_projected_blocks, w_qkv)
+    chain = event("core1", grad_one)
+    chain = [v.reshape(1, 2, 2, 2, shard, half) for v in chain]
+    for i, name in ((1, "one1"), (2, "one2"), (3, "one3")):
+        chain = event(name, chain_step(chain, i))
+    grad_one = [v.reshape(shard, half).astype(F32) for v in chain]
 
     r_rows = rms(*x_rows)
     n_rows = [v * r_rows for v in x_rows]
@@ -513,30 +615,32 @@
     grad_rows = join(
         *[a + b for a, b in zip(grad_middle, norm_back(grad_one, n_rows, gain_one, r_rows))]
     ).astype(BF)
-    expert_out_grad = restore(expert_out_own, expert_out_got, expert_out.shape, (0,))
-    input_grad, stages, gain_parts = gather_chain(
-        [grad_rows[:, :half], grad_rows[:, half:]],
-        ((), (), [expert_out_got], [expert_out_grad, output, attention_got]),
-        vector=gain_parts,
-    )
-    gain_parts = gain_parts + across(gain_parts) if two_way() else lax.psum(gain_parts, "fsdp")
+    grad_rows = event("rows", [grad_rows])[0]
+    input_grad, gain_parts = gather_chain(
+        [grad_rows[:, :half], grad_rows[:, half:]], vector=gain_parts, event=event
+    )
+    event("end", [gain_parts])
+
+    output, expert_in_grad, expert_out_grad = done["output"], done["in_whole"], done["out_whole"]
+    attention_got = [done["attention_got"]]
+    qkv_grad = weight_grad(h_one, grad_projected, attention_got, 0, attn_qkv.shape, (0,), True)
+    out_grad = weight_grad(branch_halves(), attended, attention_got, 3, attn_out.shape, ())
+    input_grad = ordered(input_grad, rank_reversed, F32)
+    if two_way():
+        got = after(across(gain_parts), input_grad, qkv_grad, out_grad, expert_out_grad)
+        gain_parts = gain_parts + got
+    else:
+        gain_parts = lax.psum(gain_parts, "fsdp")
     own_width = norm_gains.shape[1]
     gains_grad = lax.dynamic_slice_in_dim(
         gain_parts, lax.axis_index("fsdp") * own_width, own_width, 1
     )
 
-    qkv_own, out_own = own_part(h_one, grad_projected), own_part(grad_branch, attended)
-    if two_way():
-        attention_got = attention_got.astype(F32)
-        qkv_own = qkv_own + attention_got[:, : 3 * head_width]
-        out_own = out_own + attention_got[:, 3 * head_width :]
-    input_grad = ordered(input_grad, rank_reversed, F32)
-
     return (
         output,
         input_grad,
-        qkv_own.reshape(attn_qkv.shape),
-        out_own,
+        qkv_grad,
+        out_grad,
         gains_grad,
         expert_in_grad,
         expert_out_grad,

time: 509 us -> 499 us (0.980)
  matrix products: 89.2 us -> 75.2 us
  other arithmetic: 25.2 us -> 33.5 us
  Pallas kernels: 69 us -> 77.2 us
    all_gather x2, waiting for transfers between devices: 59.6 us -> 41.3 us  [local(): w_o_full = [lax.all_gather(w, GROUP, axis=0, tiled=True) for w in w_o]]
    ppermute x44, waiting for transfers between devices: 132 us -> 149 us  [swap(): lax.ppermute(v, name, [(i, i ^ bit) for i in range(lax.axis_size(name))])]
    dot_general x26 -> x23, matrix products: 79.5 us -> 65.6 us  [dot(): lax.dot_general(a, b, (((ca,), (cb,)), ((), ())), preferred_element_type=...]
    pallas_call x2 -> x4, Pallas kernels: 14.3 us -> 24.8 us  [weight_sum(): pl.pallas_call(kernel, grid=(left.shape[1] // rows,), in_specs=[pl.BlockS...]
    ppermute x8, waiting for transfers between devices: 16.4 us -> 11 us  [across(): return v if v is None else lax.ppermute(v, 'fsdp', [(0, 1), (1, 0)])]
    unnamed x88 -> x118, local copies, waits for them, and re-layouts: 12.8 us -> 8.3 us
  transfers between devices with their start and end apart: 58 -> 58, of which waited for: 33 -> 30; matrix products, arithmetic and copies ran while one was open for 23% -> 21% of each run, Pallas kernels for 8% -> 12%
where the time goes in v3:
time: 499 us; the launch traced here: 489 us
  waiting for transfers between devices  208 us (42%)
  Pallas kernels  77.2 us (15%)
  matrix products  75.2 us (15%)
  starting transfers between devices  62.1 us (12%)
  other arithmetic  33.5 us (7%)
  local copies, waits for them, and re-layouts  18.3 us (4%)
  between operations  15.5 us (3%)
    ppermute x44, waiting for transfers between devices, swap(): lax.ppermute(v, name, [(i, i ^ bit) for i in range(lax.axis_size(name))])  149 us
    dot_general x23, matrix products, dot(): lax.dot_general(a, b, (((ca,), (cb,)), ((), ())), preferred_element_type=...  65.6 us
    ppermute x44, starting transfers between devices, swap(): lax.ppermute(v, name, [(i, i ^ bit) for i in range(lax.axis_size(name))])  42.9 us
    all_gather x2, waiting for transfers between devices, local(): w_o_full = [lax.all_gather(w, GROUP, axis=0, tiled=True) for w in w_o]  41.3 us
    pallas_call x4, Pallas kernels, weight_sum(): pl.pallas_call(kernel, grid=(left.shape[1] // rows,), in_specs=[pl.BlockS...  24.8 us
    pallas_call x1, Pallas kernels, experts(): pl.pallas_call(kernel, grid=(count, tokens // rows), in_specs=[pl.BlockSp...  18.6 us
    pallas_call x1, Pallas kernels, flat(): pl.pallas_call(kernel, grid=(count // rows,), in_specs=[spec(v) for v in...  15.1 us
    pallas_call x3, Pallas kernels, reorder(): pl.pallas_call(kernel, grid_spec=pltpu.PrefetchScalarGridSpec(num_scalar_...  12.7 us
  transfers between devices with their start and end apart: 58, of which 30 were waited for; matrix products, arithmetic and copies ran while one was open for 21% of the time, Pallas kernels for 12%

profile of v3, /device:TPU:0, one launch (start us, length us, event | category | flops | bytes accessed | tf_op | source)
XLA Modules:
  0.0 489.4 jit_solution(5359067626756765669)
XLA Ops:
  8.9 2.1 convert_bitcast_fusion
  11.0 3.0 collective-permute-start.1
  16.8 2.2 copy-done.6
  19.0 15.1 %shard_map.162.wa = bf16[1024,3072]{1,0:T(8,128)(2,1)} custom-call(f32[1024,2,4,256]{3,2,1,0:T(4,128)} %refs_0_.2, f32[1024,4,256]{2,1,0:T(4,128)S(1)} %copy-done.6), custom_call_target="tpu_custom_call" | custom-call | bytes 18874368 | tf_op jit(solution)/shard_map/pallas_call | solution.py:196
  34.1 3.3 fusion.3
  39.5 2.3 add_convert_fusion.6
  44.4 2.5 shard_map.163.named_ref
  47.5 7.4 %shard_map.164 = bf16[1024,2048]{1,0:T(8,128)(2,1)} custom-call(s32[2]{0:T(128)} %pad_add_fusion.1.at, bf16[1024,2048]{1,0:T(8,128)(2,1)} %refs_0_.3), custom_call_target="tpu_custom_call" | custom-call | bytes 16777216 | tf_op jit(solution)/shard_map/pallas_call | solution.py:154
  58.5 6.5 %all-to-all-start = ((bf16[16,64,128]{2,1,0:T(8,128)(2,1)}), bf16[16,64,128]{2,1,0:T(8,128)(2,1)S(1)}, u32[]{:S(2)}, u32[]{:S(2)}) async-start(bf16[16,64,128]{2,1,0:T(8,128)(2,1)} %bitcast.3), calls=%async_computation | async-start | bytes 524288 | tf_op jit(solution)/shard_map/all_to_all | solution.py:464
  65.0 6.7 %fusion.33.part = f32[1024,1024]{1,0:T(8,128)} fusion(bf16[1024,3072]{1,0:T(8,128)(2,1)} %shard_map.162.wa, bf16[1024,2048]{1,0:T(8,128)(2,1)} %shard_map.164), kind=kOutput, calls=%fused_computation.53 | convolution fusion | flops 2147483648 | bytes 8388608 | tf_op jit(solution)/shard_map/dot_general | solution.py:54
  71.7 3.3 all-to-all-done
  75.1 3.8 multiply_reduce_fusion.2
  78.9 41.2 %all-gather.7.cloned.1.call-done = bf16[2048,1024]{0,1:T(8,128)(2,1)} async-done(((bf16[128,1024]{0,1:T(8,128)(2,1)}), bf16[2048,1024]{0,1:T(8,128)(2,1)}) %all-gather.7.cloned.1.call-update) | async-done | bytes 4194320 | tf_op jit(solution)/shard_map/all_gather | solution.py:449
  120.1 3.7 multiply_reduce_fusion.1
  126.1 3.6 collective-permute-done.7
  131.3 7.3 %collective-permute-done.3 = bf16[1,1,1,1,64,1024]{5,4,3,2,1,0:T(8,128)(2,1)S(1)} collective-permute-done((bf16[1,1,1,1,64,1024]{5,4,3,2,1,0:T(8,128)(2,1)S(1)}, bf16[1,1,1,1,64,1024]{5,4,3,2,1,0:T(8,128)(2,1)S(1)}, u32[]{:S(2)}, u32[]{:S(2)}) %collective-permute-start.3) | collective-permute-done | bytes 131104 | tf_op jit(solution)/shard_map/ppermute | solution.py:63
  139.1 5.1 %collective-permute-done.8 = bf16[1,2,1,1,64,1024]{5,4,3,2,1,0:T(8,128)(2,1)S(1)} collective-permute-done((bf16[1,2,1,1,64,1024]{5,4,3,2,1,0:T(8,128)(2,1)S(1)}, bf16[1,2,1,1,64,1024]{5,4,3,2,1,0:T(8,128)(2,1)S(1)}, u32[]{:S(2)}, u32[]{:S(2)}) %collective-permute-start.8) | collective-permute-done | bytes 262176 | tf_op jit(solution)/shard_map/ppermute | solution.py:63
  144.3 5.5 %collective-permute-done.4 = bf16[1,1,1,2,64,1024]{5,4,3,2,1,0:T(8,128)(2,1)S(1)} collective-permute-done((bf16[1,1,1,2,64,1024]{5,4,3,2,1,0:T(8,128)(2,1)S(1)}, bf16[1,1,1,2,64,1024]{5,4,3,2,1,0:T(8,128)(2,1)S(1)}, u32[]{:S(2)}, u32[]{:S(2)}) %collective-permute-start.4) | collective-permute-done | bytes 262176 | tf_op jit(solution)/shard_map/ppermute | solution.py:63
  151.3 9.6 %collective-permute-done.9 = bf16[1,2,1,2,64,1024]{5,4,3,2,1,0:T(8,128)(2,1)S(1)} collective-permute-done((bf16[1,2,1,2,64,1024]{5,4,3,2,1,0:T(8,128)(2,1)S(1)}, bf16[1,2,1,2,64,1024]{5,4,3,2,1,0:T(8,128)(2,1)S(1)}, u32[]{:S(2)}, u32[]{:S(2)}) %collective-permute-start.9) | collective-permute-done | bytes 524320 | tf_op jit(solution)/shard_map/ppermute | solution.py:63
  161.2 2.5 collective-permute-done.5
  164.0 2.5 fusion.135
  168.3 11.0 %collective-permute-done.11.wb.ob = bf16[1024,3072]{1,0:T(8,128)(2,1)} collective-permute-done((bf16[1024,3072]{1,0:T(8,128)(2,1)}, bf16[1024,3072]{1,0:T(8,128)(2,1)}, u32[]{:S(2)}, u32[]{:S(2)}) %collective-permute-start.11) | collective-permute-done | bytes 6291488 | tf_op jit(solution)/shard_map/ppermute | solution.py:348
  179.3 18.6 %shard_map.165 = (bf16[1024,1024]{1,0:T(8,128)(2,1)S(1)}, bf16[1024,2048]{1,0:T(8,128)(2,1)}) custom-call(s32[1]{0:T(128)} %bitcast.8.first_ref, f32[1024,128]{1,0:T(8,128)S(1)} %copy-done.12, bf16[1024,1024]{1,0:T(8,128)(2,1)S(1)} %pad_maximum_fusion.ha.left_ref, bf16[1024,1024]{1,0:T(8,128)(2,1)} %pad_maximum_fusion.1.hb, ...), custom_call_target="tpu_custom_call" | custom-call | flops 10737418240 | bytes 29360128 | tf_op jit(solution)/shard_map/pallas_call | solution.py:278
  198.0 6.0 %fusion.46 = bf16[512,1024]{1,0:T(8,128)(2,1)S(1)} fusion(bf16[1024,3072]{1,0:T(8,128)(2,1)} %collective-permute-done.11.wb.ob, bf16[1024,2048]{1,0:T(8,128)(2,1)} %get-tuple-element.98.right_ref), kind=kOutput, calls=%fused_computation.61 | convolution fusion | flops 2148007936 | bytes 7340032 | tf_op jit(solution)/shard_map/dot_general | solution.py:54
  204.1 2.4 fusion.41
  207.1 4.6 add_convert_fusion.4
  213.3 2.4 add_convert_fusion.5
  217.4 6.4 %convolution_convert_fusion = bf16[1024,2048]{1,0:T(8,128)(2,1)} fusion(bf16[1024,2048]{1,0:T(8,128)(2,1)S(1)} %copy-done.26, bf16[512,1024]{1,0:T(8,128)(2,1)S(1)} %bitcast.143, bf16[512,1024]{1,0:T(8,128)(2,1)S(1)} %bitcast.131), kind=kOutput, calls=%fused_computation.17 | convolution fusion | flops 4301258752 | bytes 10485760 | tf_op jit(solution)/shard_map/dot_general | solution.py:54
  225.8 3.6 collective-permute-done.13
  229.7 2.7 collective-permute-start.17
  232.8 3.8 convolution_convert_fusion.1
  236.6 6.8 %collective-permute-done.17 = bf16[1,2,1,1,64,1024]{5,4,3,2,1,0:T(8,128)(2,1)S(1)} collective-permute-done((bf16[1,2,1,1,64,1024]{5,4,3,2,1,0:T(8,128)(2,1)S(1)}, bf16[1,2,1,1,64,1024]{5,4,3,2,1,0:T(8,128)(2,1)S(1)}, u32[]{:S(2)}, u32[]{:S(2)}) %collective-permute-start.17) | collective-permute-done | bytes 262176 | tf_op jit(solution)/shard_map/ppermute | solution.py:63
  246.4 2.4 fusion.35
  249.9 3.6 collective-permute-done.18
  258.2 4.2 all-to-all-start.1
  264.4 4.2 fusion.38
  269.1 3.3 all-to-all-done.1
  272.4 3.6 multiply_reduce_fusion
  281.6 2.8 shard_map.166
  284.4 3.6 add_convert_fusion.2
  288.1 3.3 add_convert_fusion.3
  294.8 21.6 %collective-permute-done.23 = bf16[1,2,1,2,64,1024]{5,4,3,2,1,0:T(8,128)(2,1)S(1)} collective-permute-done((bf16[1,2,1,2,64,1024]{5,4,3,2,1,0:T(8,128)(2,1)S(1)}, bf16[1,2,1,2,64,1024]{5,4,3,2,1,0:T(8,128)(2,1)S(1)}, u32[]{:S(2)}, u32[]{:S(2)}) %collective-permute-start.23) | collective-permute-done | bytes 524320 | tf_op jit(solution)/shard_map/ppermute | solution.py:63
  317.1 2.5 collective-permute-start.25
  323.3 2.6 convolution_convert_fusion.4
  326.6 11.0 %collective-permute-done.25 = bf16[1,2,1,1,64,1024]{5,4,3,2,1,0:T(8,128)(2,1)S(1)} collective-permute-done((bf16[1,2,1,1,64,1024]{5,4,3,2,1,0:T(8,128)(2,1)S(1)}, bf16[1,2,1,1,64,1024]{5,4,3,2,1,0:T(8,128)(2,1)S(1)}, u32[]{:S(2)}, u32[]{:S(2)}) %collective-permute-start.25) | collective-permute-done | bytes 262176 | tf_op jit(solution)/shard_map/ppermute | solution.py:63
  338.4 8.1 %collective-permute-done.29 = bf16[1,2,1,2,64,1024]{5,4,3,2,1,0:T(8,128)(2,1)S(1)} collective-permute-done((bf16[1,2,1,2,64,1024]{5,4,3,2,1,0:T(8,128)(2,1)S(1)}, bf16[1,2,1,2,64,1024]{5,4,3,2,1,0:T(8,128)(2,1)S(1)}, u32[]{:S(2)}, u32[]{:S(2)}) %collective-permute-start.29) | collective-permute-done | bytes 524320 | tf_op jit(solution)/shard_map/ppermute | solution.py:63
  349.1 3.7 collective-permute-start.30
  354.4 4.1 collective-permute-done.30
  366.7 2.8 collective-permute-start.32
  370.2 9.6 %collective-permute-done.33 = bf16[1,2,1,1,64,1024]{5,4,3,2,1,0:T(8,128)(2,1)S(1)} collective-permute-done((bf16[1,2,1,1,64,1024]{5,4,3,2,1,0:T(8,128)(2,1)S(1)}, bf16[1,2,1,1,64,1024]{5,4,3,2,1,0:T(8,128)(2,1)S(1)}, u32[]{:S(2)}, u32[]{:S(2)}) %collective-permute-start.33) | collective-permute-done | bytes 262176 | tf_op jit(solution)/shard_map/ppermute | solution.py:63
  380.9 6.8 %collective-permute-done.32 = bf16[1,1,1,2,64,1024]{5,4,3,2,1,0:T(8,128)(2,1)S(1)} collective-permute-done((bf16[1,1,1,2,64,1024]{5,4,3,2,1,0:T(8,128)(2,1)S(1)}, bf16[1,1,1,2,64,1024]{5,4,3,2,1,0:T(8,128)(2,1)S(1)}, u32[]{:S(2)}, u32[]{:S(2)}) %collective-permute-start.32) | collective-permute-done | bytes 262176 | tf_op jit(solution)/shard_map/ppermute | solution.py:63
  388.7 2.1 collective-permute-start.36
  390.8 11.5 %shard_map.167 = f32[1024,2,4,256]{3,2,1,0:T(4,128)} custom-call(bf16[1024,1024]{1,0:T(8,128)(2,1)S(1)} %pad_maximum_fusion.ha.left_ref, bf16[1024,2048]{1,0:T(8,128)(2,1)} %get-tuple-element.98.right_ref, bf16[1024,2048]{1,0:T(8,128)(2,1)} %collective-permute-done.34.refs_0_), custom_call_target="tpu_custom_call" | custom-call | flops 4294967296 | bytes 18874368 | tf_op jit(solution)/shard_map/pallas_call | solution.py:230
  407.0 2.1 collective-permute-start.38
  411.0 2.2 collective-permute-done.38
  413.3 9.1 %collective-permute-done.37 = bf16[1,1,1,1,64,1024]{5,4,3,2,1,0:T(8,128)(2,1)S(1)} collective-permute-done((bf16[1,1,1,1,64,1024]{5,4,3,2,1,0:T(8,128)(2,1)S(1)}, bf16[1,1,1,1,64,1024]{5,4,3,2,1,0:T(8,128)(2,1)S(1)}, u32[]{:S(2)}, u32[]{:S(2)}) %collective-permute-start.37) | collective-permute-done | bytes 131104 | tf_op jit(solution)/shard_map/ppermute | solution.py:63
  427.8 8.2 %collective-permute-done.41 = bf16[1,2,1,1,64,1024]{5,4,3,2,1,0:T(8,128)(2,1)S(1)} collective-permute-done((bf16[1,2,1,1,64,1024]{5,4,3,2,1,0:T(8,128)(2,1)S(1)}, bf16[1,2,1,1,64,1024]{5,4,3,2,1,0:T(8,128)(2,1)S(1)}, u32[]{:S(2)}, u32[]{:S(2)}) %collective-permute-start.41) | collective-permute-done | bytes 262176 | tf_op jit(solution)/shard_map/ppermute | solution.py:63
  439.4 11.0 %collective-permute-done.47 = f32[2,2048]{1,0:T(2,128)S(1)} collective-permute-done((f32[2,2048]{1,0:T(2,128)S(1)}, f32[2,2048]{1,0:T(2,128)S(1)}, u32[]{:S(2)}, u32[]{:S(2)}) %collective-permute-start.47) | collective-permute-done | bytes 16416 | tf_op jit(solution)/shard_map/ppermute | solution.py:63
  450.4 6.7 %shard_map.168 = f32[1024,4,256]{2,1,0:T(4,128)} custom-call(bf16[1024,1024]{1,0:T(8,128)(2,1)S(1)} %copy-done.2, bf16[1024,1024]{1,0:T(8,128)(2,1)S(1)} %copy-done.11, bf16[1024,1024]{1,0:T(8,128)(2,1)} %copy-done.29), custom_call_target="tpu_custom_call" | custom-call | flops 2147483648 | bytes 10485760 | tf_op jit(solution)/shard_map/pallas_call | solution.py:230
  462.1 3.2 collective-permute-done.50
  467.2 3.2 shard_map.170
  470.5 3.5 shard_map.171
  474.0 5.8 %shard_map.169 = f32[1024,2048]{1,0:T(8,128)} custom-call(s32[1]{0:T(128)} %bitcast.33.at, bf16[512,1024]{1,0:T(8,128)(2,1)S(1)} %bitcast.119, bf16[512,1024]{1,0:T(8,128)(2,1)} %bitcast.47.refs_1_, bf16[512,1024]{1,0:T(8,128)(2,1)S(1)} %bitcast.118, bf16[512,1024]{1,0:T(8,128)(2,1)} %bitcast.49.refs_3_), custom_call_target="tpu_custom_call" | custom-call | bytes 12582912 | tf_op jit(solution)/shard_map/pallas_call | solution.py:327
  480.4 2.0 copy.46
  (308 shorter events, 92.1 us)
Async XLA Ops:
  7.2 67.9 %all-gather.5.cloned.1.call-start = ((), (), s32[]{:S(2)}) async-start(), calls=%async_computation.2 | async-start | bytes 4456448 | tf_op jit(solution)/shard_map/all_gather | solution.py:449
  8.9 284.6 %copy-start.20 = (bf16[1024,3,128]{0,2,1:T(8,128)(2,1)}, bf16[1024,3,128]{0,2,1:T(8,128)(2,1)S(1)}, u32[]{:S(2)}) copy-start(bf16[1024,3,128]{0,2,1:T(8,128)(2,1)S(1)} %copy.31) | copy-start | bytes 2359300
  11.0 109.1 %all-gather.7.cloned.1.call-start = ((), (), s32[]{:S(2)}) async-start(), calls=%async_computation.3 | async-start | bytes 4456448 | tf_op jit(solution)/shard_map/all_gather | solution.py:449
  11.0 28.5 %collective-permute-start.1 = (bf16[1024,384]{0,1:T(8,128)(2,1)S(1)}, bf16[1024,384]{0,1:T(8,128)(2,1)S(1)}, u32[]{:S(2)}, u32[]{:S(2)}) collective-permute-start(bf16[1024,384]{0,1:T(8,128)(2,1)S(1)} %bitcast.120), channel_id=1, source_target_pairs={{0,16},{16,0},{1,17},{17,1},{2,18},{18,2},{3,19},{19,3},{4,20},{20... | collective-permute-start | bytes 2359304 | tf_op jit(solution)/shard_map/ppermute | solution.py:348
  14.1 27.7 %collective-permute-start.2 = (bf16[128,1024]{0,1:T(8,128)(2,1)}, bf16[128,1024]{0,1:T(8,128)(2,1)S(1)}, u32[]{:S(2)}, u32[]{:S(2)}) collective-permute-start(bf16[128,1024]{0,1:T(8,128)(2,1)} %convert_bitcast_fusion), channel_id=1, source_target_pairs={{0,16},{16,0},{1,17},{17,1},{2,18},{18,2},{3,19},{19,3},{4,20},{20... | collective-permute-start | bytes 786440 | tf_op jit(solution)/shard_map/ppermute | solution.py:348
  14.8 24.6 %collective-permute-start = (bf16[2,1024]{1,0:T(2,128)(2,1)S(1)}, bf16[2,1024]{1,0:T(2,128)(2,1)S(1)}, u32[]{:S(2)}, u32[]{:S(2)}) collective-permute-start(bf16[2,1024]{1,0:T(2,128)(2,1)S(1)} %convert_element_type.355), channel_id=1, source_target_pairs={{0,16},{16,0},{1,17},{17,1},{2,18},{18,2},{3,19},{19,3},{4,20},{20... | collective-permute-start | bytes 12296 | tf_op jit(solution)/shard_map/ppermute | solution.py:348
  42.5 136.8 %collective-permute-start.11 = (bf16[1024,3072]{1,0:T(8,128)(2,1)}, bf16[1024,3072]{1,0:T(8,128)(2,1)}, u32[]{:S(2)}, u32[]{:S(2)}) collective-permute-start(bf16[1024,3072]{1,0:T(8,128)(2,1)} %shard_map.162.wa), channel_id=1, source_target_pairs={{0,16},{16,0},{1,17},{17,1},{2,18},{18,2},{3,19},{19,3},{4,20},{20... | collective-permute-start | bytes 18874376 | tf_op jit(solution)/shard_map/ppermute | solution.py:348
  58.5 16.6 %all-to-all-start = ((bf16[16,64,128]{2,1,0:T(8,128)(2,1)}), bf16[16,64,128]{2,1,0:T(8,128)(2,1)S(1)}, u32[]{:S(2)}, u32[]{:S(2)}) async-start(bf16[16,64,128]{2,1,0:T(8,128)(2,1)} %bitcast.3), calls=%async_computation | async-start | bytes 524288 | tf_op jit(solution)/shard_map/all_to_all | solution.py:464
  123.8 40.1 %copy-start.17 = (bf16[1024,2048]{1,0:T(8,128)(2,1)S(1)}, bf16[1024,2048]{1,0:T(8,128)(2,1)}, u32[]{:S(2)}) copy-start(bf16[1024,2048]{1,0:T(8,128)(2,1)} %shard_map.164) | copy-start | bytes 12582916
  123.8 130.5 %copy-start.48 = (f32[64]{0:T(128)}, f32[64]{0:T(128)S(1)}, u32[]{:S(2)}) copy-start(f32[64]{0:T(128)S(1)} %add_rsqrt_fusion.2) | copy-start | bytes 772
  124.0 5.7 %collective-permute-start.7 = (bf16[1,1,1,1,64,1024]{5,4,3,2,1,0:T(8,128)(2,1)S(1)}, bf16[1,1,1,1,64,1024]{5,4,3,2,1,0:T(8,128)(2,1)S(1)}, u32[]{:S(2)}, u32[]{:S(2)}) collective-permute-start(bf16[1,1,1,1,64,1024]{5,4,3,2,1,0:T(8,128)(2,1)S(1)} %get-tuple-element.149), channel_id=1, source_target_pairs={{0,2},{1,3},{2,0},{3,1},{4,6},{5,7},{6,4},{7,5},{8,10},{9,11},{10,... | collective-permute-start | bytes 393224 | tf_op jit(solution)/shard_map/ppermute | solution.py:63
  125.4 13.1 %collective-permute-start.3 = (bf16[1,1,1,1,64,1024]{5,4,3,2,1,0:T(8,128)(2,1)S(1)}, bf16[1,1,1,1,64,1024]{5,4,3,2,1,0:T(8,128)(2,1)S(1)}, u32[]{:S(2)}, u32[]{:S(2)}) collective-permute-start(bf16[1,1,1,1,64,1024]{5,4,3,2,1,0:T(8,128)(2,1)S(1)} %get-tuple-element.150), channel_id=1, source_target_pairs={{0,8},{4,12},{8,0},{12,4},{1,9},{5,13},{9,1},{13,5},{2,10},{6,14},... | collective-permute-start | bytes 393224 | tf_op jit(solution)/shard_map/ppermute | solution.py:63
  129.7 14.5 %collective-permute-start.8 = (bf16[1,2,1,1,64,1024]{5,4,3,2,1,0:T(8,128)(2,1)S(1)}, bf16[1,2,1,1,64,1024]{5,4,3,2,1,0:T(8,128)(2,1)S(1)}, u32[]{:S(2)}, u32[]{:S(2)}) collective-permute-start(bf16[1,2,1,1,64,1024]{5,4,3,2,1,0:T(8,128)(2,1)S(1)} %pad_maximum_fusion.12), channel_id=1, source_target_pairs={{0,8},{4,12},{8,0},{12,4},{1,9},{5,13},{9,1},{13,5},{2,10},{6,14},... | collective-permute-start | bytes 786440 | tf_op jit(solution)/shard_map/ppermute | solution.py:63
  138.6 11.2 %collective-permute-start.4 = (bf16[1,1,1,2,64,1024]{5,4,3,2,1,0:T(8,128)(2,1)S(1)}, bf16[1,1,1,2,64,1024]{5,4,3,2,1,0:T(8,128)(2,1)S(1)}, u32[]{:S(2)}, u32[]{:S(2)}) collective-permute-start(bf16[1,1,1,2,64,1024]{5,4,3,2,1,0:T(8,128)(2,1)S(1)} %pad_maximum_fusion.11), channel_id=1, source_target_pairs={{0,4},{4,0},{8,12},{12,8},{1,5},{5,1},{9,13},{13,9},{2,6},{6,2},{1... | collective-permute-start | bytes 786440 | tf_op jit(solution)/shard_map/ppermute | solution.py:63
  144.2 16.7 %collective-permute-start.9 = (bf16[1,2,1,2,64,1024]{5,4,3,2,1,0:T(8,128)(2,1)S(1)}, bf16[1,2,1,2,64,1024]{5,4,3,2,1,0:T(8,128)(2,1)S(1)}, u32[]{:S(2)}, u32[]{:S(2)}) collective-permute-start(bf16[1,2,1,2,64,1024]{5,4,3,2,1,0:T(8,128)(2,1)S(1)} %pad_maximum_fusion.8), channel_id=1, source_target_pairs={{0,4},{4,0},{8,12},{12,8},{1,5},{5,1},{9,13},{13,9},{2,6},{6,2},{1... | collective-permute-start | bytes 1572872 | tf_op jit(solution)/shard_map/ppermute | solution.py:63
  149.8 13.9 %collective-permute-start.5 = (bf16[1,1,2,2,64,1024]{5,4,3,2,1,0:T(8,128)(2,1)S(1)}, bf16[1,1,2,2,64,1024]{5,4,3,2,1,0:T(8,128)(2,1)S(1)}, u32[]{:S(2)}, u32[]{:S(2)}) collective-permute-start(bf16[1,1,2,2,64,1024]{5,4,3,2,1,0:T(8,128)(2,1)S(1)} %pad_maximum_fusion.7), channel_id=1, source_target_pairs={{0,2},{1,3},{2,0},{3,1},{4,6},{5,7},{6,4},{7,5},{8,10},{9,11},{10,... | collective-permute-start | bytes 1572872 | tf_op jit(solution)/shard_map/ppermute | solution.py:63
  161.0 5.4 %collective-permute-start.10 = (bf16[1,2,2,2,64,1024]{5,4,3,2,1,0:T(8,128)(2,1)S(1)}, bf16[1,2,2,2,64,1024]{5,4,3,2,1,0:T(8,128)(2,1)S(1)}, u32[]{:S(2)}, u32[]{:S(2)}) collective-permute-start(bf16[1,2,2,2,64,1024]{5,4,3,2,1,0:T(8,128)(2,1)S(1)} %pad_maximum_fusion.3), channel_id=1, source_target_pairs={{0,1},{1,0},{2,3},{3,2},{4,5},{5,4},{6,7},{7,6},{8,9},{9,8},{10,11... | collective-permute-start | bytes 3145736 | tf_op jit(solution)/shard_map/ppermute | solution.py:63
  163.9 4.1 collective-permute-start.6
  198.0 48.4 %copy-start.9 = (bf16[1024,1024]{1,0:T(8,128)(2,1)}, bf16[1024,1024]{1,0:T(8,128)(2,1)S(1)}, u32[]{:S(2)}) copy-start(bf16[1024,1024]{1,0:T(8,128)(2,1)S(1)} %get-tuple-element.111.right_ref) | copy-start | bytes 6291460
  204.0 3.1 collective-permute-start.14
  206.5 6.8 %collective-permute-start.12 = (bf16[512,1024]{1,0:T(8,128)(2,1)S(1)}, bf16[512,1024]{1,0:T(8,128)(2,1)S(1)}, u32[]{:S(2)}, u32[]{:S(2)}) collective-permute-start(bf16[512,1024]{1,0:T(8,128)(2,1)S(1)} %fusion.41), channel_id=1, source_target_pairs={{0,1},{1,0},{2,3},{3,2},{4,5},{5,4},{6,7},{7,6},{8,9},{9,8},{10,11... | collective-permute-start | bytes 3145736 | tf_op jit(solution)/shard_map/ppermute | solution.py:63
  211.7 13.9 %collective-permute-start.15 = (bf16[1,2,1,2,64,1024]{5,4,3,2,1,0:T(8,128)(2,1)S(1)}, bf16[1,2,1,2,64,1024]{5,4,3,2,1,0:T(8,128)(2,1)S(1)}, u32[]{:S(2)}, u32[]{:S(2)}) collective-permute-start(bf16[1,2,1,2,64,1024]{5,4,3,2,1,0:T(8,128)(2,1)S(1)} %slice.253), channel_id=1, source_target_pairs={{0,4},{4,0},{8,12},{12,8},{1,5},{5,1},{9,13},{13,9},{2,6},{6,2},{1... | collective-permute-start | bytes 1572872 | tf_op jit(solution)/shard_map/ppermute | solution.py:63
  215.8 13.7 %collective-permute-start.13 = (bf16[1,1,2,2,64,1024]{5,4,3,2,1,0:T(8,128)(2,1)S(1)}, bf16[1,1,2,2,64,1024]{5,4,3,2,1,0:T(8,128)(2,1)S(1)}, u32[]{:S(2)}, u32[]{:S(2)}) collective-permute-start(bf16[1,1,2,2,64,1024]{5,4,3,2,1,0:T(8,128)(2,1)S(1)} %slice.250), channel_id=1, source_target_pairs={{0,2},{1,3},{2,0},{3,1},{4,6},{5,7},{6,4},{7,5},{8,10},{9,11},{10,... | collective-permute-start | bytes 1572872 | tf_op jit(solution)/shard_map/ppermute | solution.py:63
  229.7 13.7 %collective-permute-start.17 = (bf16[1,2,1,1,64,1024]{5,4,3,2,1,0:T(8,128)(2,1)S(1)}, bf16[1,2,1,1,64,1024]{5,4,3,2,1,0:T(8,128)(2,1)S(1)}, u32[]{:S(2)}, u32[]{:S(2)}) collective-permute-start(bf16[1,2,1,1,64,1024]{5,4,3,2,1,0:T(8,128)(2,1)S(1)} %slice.202), channel_id=1, source_target_pairs={{0,8},{4,12},{8,0},{12,4},{1,9},{5,13},{9,1},{13,5},{2,10},{6,14},... | collective-permute-start | bytes 786440 | tf_op jit(solution)/shard_map/ppermute | solution.py:63
  232.4 12.3 %collective-permute-start.16 = (bf16[1,1,1,2,64,1024]{5,4,3,2,1,0:T(8,128)(2,1)S(1)}, bf16[1,1,1,2,64,1024]{5,4,3,2,1,0:T(8,128)(2,1)S(1)}, u32[]{:S(2)}, u32[]{:S(2)}) collective-permute-start(bf16[1,1,1,2,64,1024]{5,4,3,2,1,0:T(8,128)(2,1)S(1)} %slice.200), channel_id=1, source_target_pairs={{0,4},{4,0},{8,12},{12,8},{1,5},{5,1},{9,13},{13,9},{2,6},{6,2},{1... | collective-permute-start | bytes 786440 | tf_op jit(solution)/shard_map/ppermute | solution.py:63
  244.8 5.0 %collective-permute-start.19 = (bf16[1,1,1,1,64,1024]{5,4,3,2,1,0:T(8,128)(2,1)S(1)}, bf16[1,1,1,1,64,1024]{5,4,3,2,1,0:T(8,128)(2,1)S(1)}, u32[]{:S(2)}, u32[]{:S(2)}) collective-permute-start(bf16[1,1,1,1,64,1024]{5,4,3,2,1,0:T(8,128)(2,1)S(1)} %slice.206), channel_id=1, source_target_pairs={{0,2},{1,3},{2,0},{3,1},{4,6},{5,7},{6,4},{7,5},{8,10},{9,11},{10,... | collective-permute-start | bytes 393224 | tf_op jit(solution)/shard_map/ppermute | solution.py:63
  246.4 7.1 %collective-permute-start.18 = (bf16[1,1,1,1,64,1024]{5,4,3,2,1,0:T(8,128)(2,1)S(1)}, bf16[1,1,1,1,64,1024]{5,4,3,2,1,0:T(8,128)(2,1)S(1)}, u32[]{:S(2)}, u32[]{:S(2)}) collective-permute-start(bf16[1,1,1,1,64,1024]{5,4,3,2,1,0:T(8,128)(2,1)S(1)} %slice.204), channel_id=1, source_target_pairs={{0,8},{4,12},{8,0},{12,4},{1,9},{5,13},{9,1},{13,5},{2,10},{6,14},... | collective-permute-start | bytes 393224 | tf_op jit(solution)/shard_map/ppermute | solution.py:63
  258.2 14.2 %all-to-all-start.1 = ((bf16[64,16,128]{2,0,1:T(8,128)(2,1)}), bf16[64,16,128]{2,0,1:T(8,128)(2,1)}, u32[]{:S(2)}, u32[]{:S(2)}) async-start(bf16[64,16,128]{2,0,1:T(8,128)(2,1)} %copy_bitcast_fusion.1), calls=%async_computation.1 | async-start | bytes 524288 | tf_op jit(solution)/shard_map/all_to_all | solution.py:589
  262.4 99.0 %all-gather.9.cloned.1.call-start = ((), (), s32[]{:S(2)}) async-start(), calls=%async_computation.4 | async-start | bytes 4456448 | tf_op jit(solution)/shard_map/all_gather | solution.py:518
  264.1 196.1 %all-gather.11.cloned.1.call-start = ((), (), s32[]{:S(2)}) async-start(), calls=%async_computation.5 | async-start | bytes 4456448 | tf_op jit(solution)/shard_map/all_gather | solution.py:523
  268.6 15.8 %collective-permute-start.21 = (bf16[512,1024]{1,0:T(8,128)(2,1)}, bf16[512,1024]{1,0:T(8,128)(2,1)}, u32[]{:S(2)}, u32[]{:S(2)}) collective-permute-start(bf16[512,1024]{1,0:T(8,128)(2,1)} %fusion.38), channel_id=1, source_target_pairs={{0,1},{1,0},{2,3},{3,2},{4,5},{5,4},{6,7},{7,6},{8,9},{9,8},{10,11... | collective-permute-start | bytes 3145736 | tf_op jit(solution)/shard_map/ppermute | solution.py:63
  268.8 19.3 %collective-permute-start.20 = (bf16[512,1024]{1,0:T(8,128)(2,1)}, bf16[512,1024]{1,0:T(8,128)(2,1)}, u32[]{:S(2)}, u32[]{:S(2)}) collective-permute-start(bf16[512,1024]{1,0:T(8,128)(2,1)} %fusion.35), channel_id=1, source_target_pairs={{0,1},{1,0},{2,3},{3,2},{4,5},{5,4},{6,7},{7,6},{8,9},{9,8},{10,11... | collective-permute-start | bytes 3145736 | tf_op jit(solution)/shard_map/ppermute | solution.py:63
  291.4 25.0 %collective-permute-start.23 = (bf16[1,2,1,2,64,1024]{5,4,3,2,1,0:T(8,128)(2,1)S(1)}, bf16[1,2,1,2,64,1024]{5,4,3,2,1,0:T(8,128)(2,1)S(1)}, u32[]{:S(2)}, u32[]{:S(2)}) collective-permute-start(bf16[1,2,1,2,64,1024]{5,4,3,2,1,0:T(8,128)(2,1)S(1)} %slice.213), channel_id=1, source_target_pairs={{0,4},{4,0},{8,12},{12,8},{1,5},{5,1},{9,13},{13,9},{2,6},{6,2},{1... | collective-permute-start | bytes 1572872 | tf_op jit(solution)/shard_map/ppermute | solution.py:63
  292.2 29.0 %collective-permute-start.27 = (bf16[512,1024]{1,0:T(8,128)(2,1)S(1)}, bf16[512,1024]{1,0:T(8,128)(2,1)S(1)}, u32[]{:S(2)}, u32[]{:S(2)}) collective-permute-start(bf16[512,1024]{1,0:T(8,128)(2,1)S(1)} %convolution_convert_fusion.2), channel_id=1, source_target_pairs={{0,1},{1,0},{2,3},{3,2},{4,5},{5,4},{6,7},{7,6},{8,9},{9,8},{10,11... | collective-permute-start | bytes 3145736 | tf_op jit(solution)/shard_map/ppermute | solution.py:63
  292.7 24.1 %collective-permute-start.22 = (bf16[1,1,2,2,64,1024]{5,4,3,2,1,0:T(8,128)(2,1)S(1)}, bf16[1,1,2,2,64,1024]{5,4,3,2,1,0:T(8,128)(2,1)S(1)}, u32[]{:S(2)}, u32[]{:S(2)}) collective-permute-start(bf16[1,1,2,2,64,1024]{5,4,3,2,1,0:T(8,128)(2,1)S(1)} %slice.211), channel_id=1, source_target_pairs={{0,2},{1,3},{2,0},{3,1},{4,6},{5,7},{6,4},{7,5},{8,10},{9,11},{10,... | collective-permute-start | bytes 1572872 | tf_op jit(solution)/shard_map/ppermute | solution.py:63
  294.2 27.7 %collective-permute-start.26 = (bf16[512,1024]{1,0:T(8,128)(2,1)S(1)}, bf16[512,1024]{1,0:T(8,128)(2,1)S(1)}, u32[]{:S(2)}, u32[]{:S(2)}) collective-permute-start(bf16[512,1024]{1,0:T(8,128)(2,1)S(1)} %convolution_convert_fusion.3), channel_id=1, source_target_pairs={{0,1},{1,0},{2,3},{3,2},{4,5},{5,4},{6,7},{7,6},{8,9},{9,8},{10,11... | collective-permute-start | bytes 3145736 | tf_op jit(solution)/shard_map/ppermute | solution.py:63
  294.5 94.2 %collective-permute-start.34 = (bf16[1024,2048]{1,0:T(8,128)(2,1)}, bf16[1024,2048]{1,0:T(8,128)(2,1)}, u32[]{:S(2)}, u32[]{:S(2)}) collective-permute-start(bf16[1024,2048]{1,0:T(8,128)(2,1)} %convolution_convert_fusion), channel_id=1, source_target_pairs={{0,16},{16,0},{1,17},{17,1},{2,18},{18,2},{3,19},{19,3},{4,20},{20... | collective-permute-start | bytes 12582920 | tf_op jit(solution)/shard_map/ppermute | solution.py:348
  317.1 20.4 %collective-permute-start.25 = (bf16[1,2,1,1,64,1024]{5,4,3,2,1,0:T(8,128)(2,1)S(1)}, bf16[1,2,1,1,64,1024]{5,4,3,2,1,0:T(8,128)(2,1)S(1)}, u32[]{:S(2)}, u32[]{:S(2)}) collective-permute-start(bf16[1,2,1,1,64,1024]{5,4,3,2,1,0:T(8,128)(2,1)S(1)} %slice.217), channel_id=1, source_target_pairs={{0,8},{4,12},{8,0},{12,4},{1,9},{5,13},{9,1},{13,5},{2,10},{6,14},... | collective-permute-start | bytes 786440 | tf_op jit(solution)/shard_map/ppermute | solution.py:63
  319.6 18.7 %collective-permute-start.24 = (bf16[1,1,1,2,64,1024]{5,4,3,2,1,0:T(8,128)(2,1)S(1)}, bf16[1,1,1,2,64,1024]{5,4,3,2,1,0:T(8,128)(2,1)S(1)}, u32[]{:S(2)}, u32[]{:S(2)}) collective-permute-start(bf16[1,1,1,2,64,1024]{5,4,3,2,1,0:T(8,128)(2,1)S(1)} %slice.215), channel_id=1, source_target_pairs={{0,4},{4,0},{8,12},{12,8},{1,5},{5,1},{9,13},{13,9},{2,6},{6,2},{1... | collective-permute-start | bytes 786440 | tf_op jit(solution)/shard_map/ppermute | solution.py:63
  322.7 23.8 %collective-permute-start.29 = (bf16[1,2,1,2,64,1024]{5,4,3,2,1,0:T(8,128)(2,1)S(1)}, bf16[1,2,1,2,64,1024]{5,4,3,2,1,0:T(8,128)(2,1)S(1)}, u32[]{:S(2)}, u32[]{:S(2)}) collective-permute-start(bf16[1,2,1,2,64,1024]{5,4,3,2,1,0:T(8,128)(2,1)S(1)} %slice.260), channel_id=1, source_target_pairs={{0,4},{4,0},{8,12},{12,8},{1,5},{5,1},{9,13},{13,9},{2,6},{6,2},{1... | collective-permute-start | bytes 1572872 | tf_op jit(solution)/shard_map/ppermute | solution.py:63
  325.9 21.5 %collective-permute-start.28 = (bf16[1,1,2,2,64,1024]{5,4,3,2,1,0:T(8,128)(2,1)S(1)}, bf16[1,1,2,2,64,1024]{5,4,3,2,1,0:T(8,128)(2,1)S(1)}, u32[]{:S(2)}, u32[]{:S(2)}) collective-permute-start(bf16[1,1,2,2,64,1024]{5,4,3,2,1,0:T(8,128)(2,1)S(1)} %slice.258), channel_id=1, source_target_pairs={{0,2},{1,3},{2,0},{3,1},{4,6},{5,7},{6,4},{7,5},{8,10},{9,11},{10,... | collective-permute-start | bytes 1572872 | tf_op jit(solution)/shard_map/ppermute | solution.py:63
  349.1 9.4 %collective-permute-start.30 = (bf16[1,1,1,1,64,1024]{5,4,3,2,1,0:T(8,128)(2,1)}, bf16[1,1,1,1,64,1024]{5,4,3,2,1,0:T(8,128)(2,1)}, u32[]{:S(2)}, u32[]{:S(2)}) collective-permute-start(bf16[1,1,1,1,64,1024]{5,4,3,2,1,0:T(8,128)(2,1)} %slice.225), channel_id=1, source_target_pairs={{0,8},{4,12},{8,0},{12,4},{1,9},{5,13},{9,1},{13,5},{2,10},{6,14},... | collective-permute-start | bytes 393224 | tf_op jit(solution)/shard_map/ppermute | solution.py:63
  353.8 5.8 %collective-permute-start.31 = (bf16[1,1,1,1,64,1024]{5,4,3,2,1,0:T(8,128)(2,1)S(1)}, bf16[1,1,1,1,64,1024]{5,4,3,2,1,0:T(8,128)(2,1)S(1)}, u32[]{:S(2)}, u32[]{:S(2)}) collective-permute-start(bf16[1,1,1,1,64,1024]{5,4,3,2,1,0:T(8,128)(2,1)S(1)} %slice.227), channel_id=1, source_target_pairs={{0,2},{1,3},{2,0},{3,1},{4,6},{5,7},{6,4},{7,5},{8,10},{9,11},{10,... | collective-permute-start | bytes 393224 | tf_op jit(solution)/shard_map/ppermute | solution.py:63
  363.6 16.3 %collective-permute-start.33 = (bf16[1,2,1,1,64,1024]{5,4,3,2,1,0:T(8,128)(2,1)S(1)}, bf16[1,2,1,1,64,1024]{5,4,3,2,1,0:T(8,128)(2,1)S(1)}, u32[]{:S(2)}, u32[]{:S(2)}) collective-permute-start(bf16[1,2,1,1,64,1024]{5,4,3,2,1,0:T(8,128)(2,1)S(1)} %slice.231), channel_id=1, source_target_pairs={{0,8},{4,12},{8,0},{12,4},{1,9},{5,13},{9,1},{13,5},{2,10},{6,14},... | collective-permute-start | bytes 786440 | tf_op jit(solution)/shard_map/ppermute | solution.py:63
  364.7 71.9 %collective-permute-start.42 = (bf16[1024,1024]{1,0:T(8,128)(2,1)}, bf16[1024,1024]{1,0:T(8,128)(2,1)S(1)}, u32[]{:S(2)}, u32[]{:S(2)}) collective-permute-start(bf16[1024,1024]{1,0:T(8,128)(2,1)} %convolution_convert_fusion.1), channel_id=1, source_target_pairs={{0,16},{16,0},{1,17},{17,1},{2,18},{18,2},{3,19},{19,3},{4,20},{20... | collective-permute-start | bytes 6291464 | tf_op jit(solution)/shard_map/ppermute | solution.py:348
  366.7 21.0 %collective-permute-start.32 = (bf16[1,1,1,2,64,1024]{5,4,3,2,1,0:T(8,128)(2,1)S(1)}, bf16[1,1,1,2,64,1024]{5,4,3,2,1,0:T(8,128)(2,1)S(1)}, u32[]{:S(2)}, u32[]{:S(2)}) collective-permute-start(bf16[1,1,1,2,64,1024]{5,4,3,2,1,0:T(8,128)(2,1)S(1)} %slice.229), channel_id=1, source_target_pairs={{0,4},{4,0},{8,12},{12,8},{1,5},{5,1},{9,13},{13,9},{2,6},{6,2},{1... | collective-permute-start | bytes 786440 | tf_op jit(solution)/shard_map/ppermute | solution.py:63
  388.7 13.6 %collective-permute-start.36 = (bf16[1,1,1,1,64,1024]{5,4,3,2,1,0:T(8,128)(2,1)S(1)}, bf16[1,1,1,1,64,1024]{5,4,3,2,1,0:T(8,128)(2,1)S(1)}, u32[]{:S(2)}, u32[]{:S(2)}) collective-permute-start(bf16[1,1,1,1,64,1024]{5,4,3,2,1,0:T(8,128)(2,1)S(1)} %slice.235), channel_id=1, source_target_pairs={{0,2},{1,3},{2,0},{3,1},{4,6},{5,7},{6,4},{7,5},{8,10},{9,11},{10,... | collective-permute-start | bytes 393224 | tf_op jit(solution)/shard_map/ppermute | solution.py:63
  390.8 12.6 %collective-permute-start.35 = (bf16[1,1,1,1,64,1024]{5,4,3,2,1,0:T(8,128)(2,1)S(1)}, bf16[1,1,1,1,64,1024]{5,4,3,2,1,0:T(8,128)(2,1)S(1)}, u32[]{:S(2)}, u32[]{:S(2)}) collective-permute-start(bf16[1,1,1,1,64,1024]{5,4,3,2,1,0:T(8,128)(2,1)S(1)} %slice.233), channel_id=1, source_target_pairs={{0,8},{4,12},{8,0},{12,4},{1,9},{5,13},{9,1},{13,5},{2,10},{6,14},... | collective-permute-start | bytes 393224 | tf_op jit(solution)/shard_map/ppermute | solution.py:63
  405.0 1.9 collective-permute-start.39
  406.9 4.0 collective-permute-start.43
  407.0 6.2 %collective-permute-start.38 = (bf16[1,1,1,1,64,1024]{5,4,3,2,1,0:T(8,128)(2,1)S(1)}, bf16[1,1,1,1,64,1024]{5,4,3,2,1,0:T(8,128)(2,1)S(1)}, u32[]{:S(2)}, u32[]{:S(2)}) collective-permute-start(bf16[1,1,1,1,64,1024]{5,4,3,2,1,0:T(8,128)(2,1)S(1)} %get-tuple-element.102), channel_id=1, source_target_pairs={{0,2},{1,3},{2,0},{3,1},{4,6},{5,7},{6,4},{7,5},{8,10},{9,11},{10,... | collective-permute-start | bytes 393224 | tf_op jit(solution)/shard_map/ppermute | solution.py:63
  409.1 13.3 %collective-permute-start.37 = (bf16[1,1,1,1,64,1024]{5,4,3,2,1,0:T(8,128)(2,1)S(1)}, bf16[1,1,1,1,64,1024]{5,4,3,2,1,0:T(8,128)(2,1)S(1)}, u32[]{:S(2)}, u32[]{:S(2)}) collective-permute-start(bf16[1,1,1,1,64,1024]{5,4,3,2,1,0:T(8,128)(2,1)S(1)} %get-tuple-element.101), channel_id=1, source_target_pairs={{0,8},{4,12},{8,0},{12,4},{1,9},{5,13},{9,1},{13,5},{2,10},{6,14},... | collective-permute-start | bytes 393224 | tf_op jit(solution)/shard_map/ppermute | solution.py:63
  413.2 37.1 %copy-start.2 = (bf16[1024,1024]{1,0:T(8,128)(2,1)S(1)}, bf16[1024,1024]{1,0:T(8,128)(2,1)}, u32[]{:S(2)}) copy-start(bf16[1024,1024]{1,0:T(8,128)(2,1)} %get-tuple-element.141.left_ref) | copy-start | bytes 6291460
  413.3 37.1 %copy-start.11 = (bf16[1024,1024]{1,0:T(8,128)(2,1)S(1)}, bf16[1024,1024]{1,0:T(8,128)(2,1)}, u32[]{:S(2)}) copy-start(bf16[1024,1024]{1,0:T(8,128)(2,1)} %copy-done.9) | copy-start | bytes 6291460
  422.4 13.6 %collective-permute-start.41 = (bf16[1,2,1,1,64,1024]{5,4,3,2,1,0:T(8,128)(2,1)S(1)}, bf16[1,2,1,1,64,1024]{5,4,3,2,1,0:T(8,128)(2,1)S(1)}, u32[]{:S(2)}, u32[]{:S(2)}) collective-permute-start(bf16[1,2,1,1,64,1024]{5,4,3,2,1,0:T(8,128)(2,1)S(1)} %pad_maximum_fusion.15), channel_id=1, source_target_pairs={{0,8},{4,12},{8,0},{12,4},{1,9},{5,13},{9,1},{13,5},{2,10},{6,14},... | collective-permute-start | bytes 786440 | tf_op jit(solution)/shard_map/ppermute | solution.py:63
  422.5 14.0 %collective-permute-start.40 = (bf16[1,1,1,2,64,1024]{5,4,3,2,1,0:T(8,128)(2,1)S(1)}, bf16[1,1,1,2,64,1024]{5,4,3,2,1,0:T(8,128)(2,1)S(1)}, u32[]{:S(2)}, u32[]{:S(2)}) collective-permute-start(bf16[1,1,1,2,64,1024]{5,4,3,2,1,0:T(8,128)(2,1)S(1)} %pad_maximum_fusion.14), channel_id=1, source_target_pairs={{0,4},{4,0},{8,12},{12,8},{1,5},{5,1},{9,13},{13,9},{2,6},{6,2},{1... | collective-permute-start | bytes 786440 | tf_op jit(solution)/shard_map/ppermute | solution.py:63
  426.3 32.9 %collective-permute-start.46 = (bf16[1024,512]{1,0:T(8,128)(2,1)S(1)}, bf16[1024,512]{1,0:T(8,128)(2,1)S(1)}, u32[]{:S(2)}, u32[]{:S(2)}) collective-permute-start(bf16[1024,512]{1,0:T(8,128)(2,1)S(1)} %pad_maximum_fusion.6), channel_id=1, source_target_pairs={{0,16},{16,0},{1,17},{17,1},{2,18},{18,2},{3,19},{19,3},{4,20},{20... | collective-permute-start | bytes 3145736 | tf_op jit(solution)/shard_map/ppermute | solution.py:348
  436.6 20.5 %collective-permute-start.45 = (bf16[1,2,1,2,64,1024]{5,4,3,2,1,0:T(8,128)(2,1)S(1)}, bf16[1,2,1,2,64,1024]{5,4,3,2,1,0:T(8,128)(2,1)S(1)}, u32[]{:S(2)}, u32[]{:S(2)}) collective-permute-start(bf16[1,2,1,2,64,1024]{5,4,3,2,1,0:T(8,128)(2,1)S(1)} %pad_maximum_fusion.10), channel_id=1, source_target_pairs={{0,4},{4,0},{8,12},{12,8},{1,5},{5,1},{9,13},{13,9},{2,6},{6,2},{1... | collective-permute-start | bytes 1572872 | tf_op jit(solution)/shard_map/ppermute | solution.py:63
  436.9 21.2 %collective-permute-start.44 = (bf16[1,1,2,2,64,1024]{5,4,3,2,1,0:T(8,128)(2,1)S(1)}, bf16[1,1,2,2,64,1024]{5,4,3,2,1,0:T(8,128)(2,1)S(1)}, u32[]{:S(2)}, u32[]{:S(2)}) collective-permute-start(bf16[1,1,2,2,64,1024]{5,4,3,2,1,0:T(8,128)(2,1)S(1)} %pad_maximum_fusion.9), channel_id=1, source_target_pairs={{0,2},{1,3},{2,0},{3,1},{4,6},{5,7},{6,4},{7,5},{8,10},{9,11},{10,... | collective-permute-start | bytes 1572872 | tf_op jit(solution)/shard_map/ppermute | solution.py:63
  437.6 12.8 %collective-permute-start.47 = (f32[2,2048]{1,0:T(2,128)S(1)}, f32[2,2048]{1,0:T(2,128)S(1)}, u32[]{:S(2)}, u32[]{:S(2)}) collective-permute-start(f32[2,2048]{1,0:T(2,128)S(1)} %fusion.164), channel_id=1, source_target_pairs={{0,4},{4,0},{8,12},{12,8},{1,5},{5,1},{9,13},{13,9},{2,6},{6,2},{1... | collective-permute-start | bytes 49160 | tf_op jit(solution)/shard_map/ppermute | solution.py:63
  460.2 13.8 %collective-permute-start.48 = (bf16[1,2,2,2,64,1024]{5,4,3,2,1,0:T(8,128)(2,1)}, bf16[1,2,2,2,64,1024]{5,4,3,2,1,0:T(8,128)(2,1)}, u32[]{:S(2)}, u32[]{:S(2)}) collective-permute-start(bf16[1,2,2,2,64,1024]{5,4,3,2,1,0:T(8,128)(2,1)} %pad_maximum_fusion.4), channel_id=1, source_target_pairs={{0,1},{1,0},{2,3},{3,2},{4,5},{5,4},{6,7},{7,6},{8,9},{9,8},{10,11... | collective-permute-start | bytes 3145736 | tf_op jit(solution)/shard_map/ppermute | solution.py:63
  460.2 13.8 %collective-permute-start.49 = (bf16[1,2,2,2,64,1024]{5,4,3,2,1,0:T(8,128)(2,1)}, bf16[1,2,2,2,64,1024]{5,4,3,2,1,0:T(8,128)(2,1)}, u32[]{:S(2)}, u32[]{:S(2)}) collective-permute-start(bf16[1,2,2,2,64,1024]{5,4,3,2,1,0:T(8,128)(2,1)} %pad_maximum_fusion.5), channel_id=1, source_target_pairs={{0,1},{1,0},{2,3},{3,2},{4,5},{5,4},{6,7},{7,6},{8,9},{9,8},{10,11... | collective-permute-start | bytes 3145736 | tf_op jit(solution)/shard_map/ppermute | solution.py:63
  460.7 4.6 collective-permute-start.50
  465.4 14.5 %collective-permute-start.51 = (f32[2,2048]{1,0:T(2,128)S(1)}, f32[2,2048]{1,0:T(2,128)S(1)}, u32[]{:S(2)}, u32[]{:S(2)}) collective-permute-start(f32[2,2048]{1,0:T(2,128)S(1)} %add.277), channel_id=1, source_target_pairs={{0,16},{16,0},{1,17},{17,1},{2,18},{18,2},{3,19},{19,3},{4,20},{20... | collective-permute-start | bytes 49160 | tf_op jit(solution)/shard_map/ppermute | solution.py:348
  (52 other events, 397.6 us)
Sparse Core Ops, SparseCore 0:
  11.1 55.7 all-gather.4
  69.0 51.0 all-gather.6
  265.4 71.1 all-gather.8
  361.4 62.5 all-gather.10

commit v4 on v3

--- a/solution.py
+++ b/solution.py
@@ -33,8 +33,7 @@
         "do": ("branch", "mix0", "mix1"),
         "blocks": ("mix2",),
         "core1": ("qkv",),
-        "one1": ("mix3",),
-        "one2": ("in_whole", "attention", "attention_got"),
+        "one2": ("mix3", "in_whole", "attention", "attention_got"),
         "one3": ("output",),
         "stage1": ("out_whole",),
     },
@@ -616,9 +615,16 @@
         *[a + b for a, b in zip(grad_middle, norm_back(grad_one, n_rows, gain_one, r_rows))]
     ).astype(BF)
     grad_rows = event("rows", [grad_rows])[0]
-    input_grad, gain_parts = gather_chain(
-        [grad_rows[:, :half], grad_rows[:, half:]], vector=gain_parts, event=event
-    )
+    at_stage = {}
+
+    def noted(name, now):
+        at_stage[name] = now
+        return event(name, now)
+
+    input_grad, _ = gather_chain([grad_rows[:, :half], grad_rows[:, half:]], event=noted)
+    gain_parts = after(gain_parts, *at_stage["stage2"])
+    for step in ORDER_A:
+        gain_parts = gain_parts + swap(gain_parts, step)
     event("end", [gain_parts])
 
     output, expert_in_grad, expert_out_grad = done["output"], done["in_whole"], done["out_whole"]

time: 499 us -> 495 us (level)
  other arithmetic: 33.5 us -> 28.1 us
    ppermute x44, starting transfers between devices: 42.9 us -> 37.4 us  [swap(): lax.ppermute(v, name, [(i, i ^ bit) for i in range(lax.axis_size(name))])]
    unnamed x118 -> x136, local copies, waits for them, and re-layouts: 8.3 us -> 10.3 us
  transfers between devices with their start and end apart: 58 -> 58, of which waited for: 30 -> 32; matrix products, arithmetic and copies ran while one was open for 21% -> 22% of each run, Pallas kernels for 12% -> 12%
where the time goes in v4:
time: 495 us; the launch traced here: 486 us
  waiting for transfers between devices  209 us (42%)
  matrix products  77.5 us (16%)
  Pallas kernels  77.4 us (16%)
  starting transfers between devices  57.2 us (12%)
  other arithmetic  28.1 us (6%)
  local copies, waits for them, and re-layouts  21.1 us (4%)
  between operations  15.5 us (3%)
    ppermute x44, waiting for transfers between devices, swap(): lax.ppermute(v, name, [(i, i ^ bit) for i in range(lax.axis_size(name))])  148 us
    dot_general x23, matrix products, dot(): lax.dot_general(a, b, (((ca,), (cb,)), ((), ())), preferred_element_type=...  68 us
    all_gather x2, waiting for transfers between devices, local(): w_o_full = [lax.all_gather(w, GROUP, axis=0, tiled=True) for w in w_o]  41.1 us
    ppermute x44, starting transfers between devices, swap(): lax.ppermute(v, name, [(i, i ^ bit) for i in range(lax.axis_size(name))])  37.4 us
    pallas_call x4, Pallas kernels, weight_sum(): pl.pallas_call(kernel, grid=(left.shape[1] // rows,), in_specs=[pl.BlockS...  24.9 us
    pallas_call x1, Pallas kernels, experts(): pl.pallas_call(kernel, grid=(count, tokens // rows), in_specs=[pl.BlockSp...  18.6 us
    pallas_call x1, Pallas kernels, flat(): pl.pallas_call(kernel, grid=(count // rows,), in_specs=[spec(v) for v in...  15.1 us
    pallas_call x3, Pallas kernels, reorder(): pl.pallas_call(kernel, grid_spec=pltpu.PrefetchScalarGridSpec(num_scalar_...  12.8 us
  transfers between devices with their start and end apart: 58, of which 32 were waited for; matrix products, arithmetic and copies ran while one was open for 22% of the time, Pallas kernels for 12%

profile of v4, /device:TPU:0, one launch (start us, length us, event | category | flops | bytes accessed | tf_op | source)
XLA Modules:
  0.0 486.2 jit_solution(16851929677922457135)
XLA Ops:
  8.9 2.1 convert_bitcast_fusion
  11.0 3.0 collective-permute-start.1
  16.8 2.2 copy-done.4
  19.0 15.1 %shard_map.162.wa = bf16[1024,3072]{1,0:T(8,128)(2,1)} custom-call(f32[1024,2,4,256]{3,2,1,0:T(4,128)} %refs_0_.2, f32[1024,4,256]{2,1,0:T(4,128)S(1)} %copy-done.4), custom_call_target="tpu_custom_call" | custom-call | bytes 18874368 | tf_op jit(solution)/shard_map/pallas_call | solution.py:195
  34.1 3.3 fusion.3
  39.5 2.3 add_convert_fusion.6
  44.4 2.6 shard_map.163.named_ref
  47.6 7.4 %shard_map.164 = bf16[1024,2048]{1,0:T(8,128)(2,1)} custom-call(s32[2]{0:T(128)} %pad_add_fusion.1.at, bf16[1024,2048]{1,0:T(8,128)(2,1)} %refs_0_.3), custom_call_target="tpu_custom_call" | custom-call | bytes 16777216 | tf_op jit(solution)/shard_map/pallas_call | solution.py:153
  58.5 6.6 %all-to-all-start = ((bf16[16,64,128]{2,1,0:T(8,128)(2,1)}), bf16[16,64,128]{2,1,0:T(8,128)(2,1)S(1)}, u32[]{:S(2)}, u32[]{:S(2)}) async-start(bf16[16,64,128]{2,1,0:T(8,128)(2,1)} %bitcast.3), calls=%async_computation | async-start | bytes 524288 | tf_op jit(solution)/shard_map/all_to_all | solution.py:463
  65.1 6.6 %fusion.33.part = f32[1024,1024]{1,0:T(8,128)} fusion(bf16[1024,3072]{1,0:T(8,128)(2,1)} %shard_map.162.wa, bf16[1024,2048]{1,0:T(8,128)(2,1)} %shard_map.164), kind=kOutput, calls=%fused_computation.53 | convolution fusion | flops 2147483648 | bytes 8388608 | tf_op jit(solution)/shard_map/dot_general | solution.py:53
  71.7 3.4 all-to-all-done
  75.2 3.8 multiply_reduce_fusion.2
  79.0 41.1 %all-gather.7.cloned.1.call-done = bf16[2048,1024]{0,1:T(8,128)(2,1)} async-done(((bf16[128,1024]{0,1:T(8,128)(2,1)}), bf16[2048,1024]{0,1:T(8,128)(2,1)}) %all-gather.7.cloned.1.call-update) | async-done | bytes 4194320 | tf_op jit(solution)/shard_map/all_gather | solution.py:448
  120.1 3.7 multiply_reduce_fusion.1
  126.1 3.6 collective-permute-done.7
  131.3 7.3 %collective-permute-done.3 = bf16[1,1,1,1,64,1024]{5,4,3,2,1,0:T(8,128)(2,1)S(1)} collective-permute-done((bf16[1,1,1,1,64,1024]{5,4,3,2,1,0:T(8,128)(2,1)S(1)}, bf16[1,1,1,1,64,1024]{5,4,3,2,1,0:T(8,128)(2,1)S(1)}, u32[]{:S(2)}, u32[]{:S(2)}) %collective-permute-start.3) | collective-permute-done | bytes 131104 | tf_op jit(solution)/shard_map/ppermute | solution.py:62
  139.0 5.1 %collective-permute-done.8 = bf16[1,2,1,1,64,1024]{5,4,3,2,1,0:T(8,128)(2,1)S(1)} collective-permute-done((bf16[1,2,1,1,64,1024]{5,4,3,2,1,0:T(8,128)(2,1)S(1)}, bf16[1,2,1,1,64,1024]{5,4,3,2,1,0:T(8,128)(2,1)S(1)}, u32[]{:S(2)}, u32[]{:S(2)}) %collective-permute-start.8) | collective-permute-done | bytes 262176 | tf_op jit(solution)/shard_map/ppermute | solution.py:62
  144.3 5.5 %collective-permute-done.4 = bf16[1,1,1,2,64,1024]{5,4,3,2,1,0:T(8,128)(2,1)S(1)} collective-permute-done((bf16[1,1,1,2,64,1024]{5,4,3,2,1,0:T(8,128)(2,1)S(1)}, bf16[1,1,1,2,64,1024]{5,4,3,2,1,0:T(8,128)(2,1)S(1)}, u32[]{:S(2)}, u32[]{:S(2)}) %collective-permute-start.4) | collective-permute-done | bytes 262176 | tf_op jit(solution)/shard_map/ppermute | solution.py:62
  151.3 9.6 %collective-permute-done.9 = bf16[1,2,1,2,64,1024]{5,4,3,2,1,0:T(8,128)(2,1)S(1)} collective-permute-done((bf16[1,2,1,2,64,1024]{5,4,3,2,1,0:T(8,128)(2,1)S(1)}, bf16[1,2,1,2,64,1024]{5,4,3,2,1,0:T(8,128)(2,1)S(1)}, u32[]{:S(2)}, u32[]{:S(2)}) %collective-permute-start.9) | collective-permute-done | bytes 524320 | tf_op jit(solution)/shard_map/ppermute | solution.py:62
  161.2 2.5 collective-permute-done.5
  163.9 2.5 fusion.134
  168.3 11.0 %collective-permute-done.11.wb.ob = bf16[1024,3072]{1,0:T(8,128)(2,1)} collective-permute-done((bf16[1024,3072]{1,0:T(8,128)(2,1)}, bf16[1024,3072]{1,0:T(8,128)(2,1)}, u32[]{:S(2)}, u32[]{:S(2)}) %collective-permute-start.11) | collective-permute-done | bytes 6291488 | tf_op jit(solution)/shard_map/ppermute | solution.py:347
  179.3 18.6 %shard_map.165 = (bf16[1024,1024]{1,0:T(8,128)(2,1)S(1)}, bf16[1024,2048]{1,0:T(8,128)(2,1)}) custom-call(s32[1]{0:T(128)} %bitcast.8.first_ref, f32[1024,128]{1,0:T(8,128)S(1)} %copy-done.12, bf16[1024,1024]{1,0:T(8,128)(2,1)S(1)} %pad_maximum_fusion.ha.left_ref, bf16[1024,1024]{1,0:T(8,128)(2,1)} %pad_maximum_fusion.1.hb, ...), custom_call_target="tpu_custom_call" | custom-call | flops 10737418240 | bytes 29360128 | tf_op jit(solution)/shard_map/pallas_call | solution.py:277
  198.0 6.0 %fusion.46 = bf16[512,1024]{1,0:T(8,128)(2,1)S(1)} fusion(bf16[1024,3072]{1,0:T(8,128)(2,1)} %collective-permute-done.11.wb.ob, bf16[1024,2048]{1,0:T(8,128)(2,1)} %get-tuple-element.91.right_ref), kind=kOutput, calls=%fused_computation.61 | convolution fusion | flops 2148007936 | bytes 7340032 | tf_op jit(solution)/shard_map/dot_general | solution.py:53
  204.1 2.4 fusion.41
  207.1 4.6 add_convert_fusion.4
  213.3 2.4 add_convert_fusion.5
  217.4 6.4 %convolution_convert_fusion = bf16[1024,2048]{1,0:T(8,128)(2,1)} fusion(bf16[1024,2048]{1,0:T(8,128)(2,1)S(1)} %copy-done.26, bf16[512,1024]{1,0:T(8,128)(2,1)S(1)} %bitcast.142, bf16[512,1024]{1,0:T(8,128)(2,1)S(1)} %bitcast.130), kind=kOutput, calls=%fused_computation.17 | convolution fusion | flops 4301258752 | bytes 10485760 | tf_op jit(solution)/shard_map/dot_general | solution.py:53
  225.8 3.6 collective-permute-done.13
  229.7 2.7 collective-permute-start.17
  232.8 3.8 convolution_convert_fusion.1
  236.6 6.9 %collective-permute-done.17 = bf16[1,2,1,1,64,1024]{5,4,3,2,1,0:T(8,128)(2,1)S(1)} collective-permute-done((bf16[1,2,1,1,64,1024]{5,4,3,2,1,0:T(8,128)(2,1)S(1)}, bf16[1,2,1,1,64,1024]{5,4,3,2,1,0:T(8,128)(2,1)S(1)}, u32[]{:S(2)}, u32[]{:S(2)}) %collective-permute-start.17) | collective-permute-done | bytes 262176 | tf_op jit(solution)/shard_map/ppermute | solution.py:62
  246.5 3.9 fusion.38
  250.4 3.2 collective-permute-done.18
  258.2 4.2 all-to-all-start.1
  262.5 4.2 fusion.35
  268.0 4.5 all-to-all-done.1
  272.5 3.4 multiply_reduce_fusion
  281.7 2.8 shard_map.166
  286.6 3.6 add_convert_fusion.2
  290.2 3.2 add_convert_fusion.3
  295.9 23.0 %collective-permute-done.23 = bf16[1,2,1,2,64,1024]{5,4,3,2,1,0:T(8,128)(2,1)S(1)} collective-permute-done((bf16[1,2,1,2,64,1024]{5,4,3,2,1,0:T(8,128)(2,1)S(1)}, bf16[1,2,1,2,64,1024]{5,4,3,2,1,0:T(8,128)(2,1)S(1)}, u32[]{:S(2)}, u32[]{:S(2)}) %collective-permute-start.23) | collective-permute-done | bytes 524320 | tf_op jit(solution)/shard_map/ppermute | solution.py:62
  324.1 2.3 convolution_convert_fusion.4
  326.5 16.6 %collective-permute-done.29 = bf16[1,2,1,2,64,1024]{5,4,3,2,1,0:T(8,128)(2,1)S(1)} collective-permute-done((bf16[1,2,1,2,64,1024]{5,4,3,2,1,0:T(8,128)(2,1)S(1)}, bf16[1,2,1,2,64,1024]{5,4,3,2,1,0:T(8,128)(2,1)S(1)}, u32[]{:S(2)}, u32[]{:S(2)}) %collective-permute-start.29) | collective-permute-done | bytes 524320 | tf_op jit(solution)/shard_map/ppermute | solution.py:62
  345.7 2.5 collective-permute-start.30
  350.3 7.9 %collective-permute-done.31 = bf16[1,2,1,1,64,1024]{5,4,3,2,1,0:T(8,128)(2,1)S(1)} collective-permute-done((bf16[1,2,1,1,64,1024]{5,4,3,2,1,0:T(8,128)(2,1)S(1)}, bf16[1,2,1,1,64,1024]{5,4,3,2,1,0:T(8,128)(2,1)S(1)}, u32[]{:S(2)}, u32[]{:S(2)}) %collective-permute-start.31) | collective-permute-done | bytes 262176 | tf_op jit(solution)/shard_map/ppermute | solution.py:62
  363.5 2.5 collective-permute-start.34
  366.0 4.9 %collective-permute-done.33 = bf16[1,1,1,1,64,1024]{5,4,3,2,1,0:T(8,128)(2,1)} collective-permute-done((bf16[1,1,1,1,64,1024]{5,4,3,2,1,0:T(8,128)(2,1)}, bf16[1,1,1,1,64,1024]{5,4,3,2,1,0:T(8,128)(2,1)}, u32[]{:S(2)}, u32[]{:S(2)}) %collective-permute-start.33) | collective-permute-done | bytes 131104 | tf_op jit(solution)/shard_map/ppermute | solution.py:62
  377.5 11.6 %shard_map.167 = f32[1024,2,4,256]{3,2,1,0:T(4,128)} custom-call(bf16[1024,1024]{1,0:T(8,128)(2,1)S(1)} %pad_maximum_fusion.ha.left_ref, bf16[1024,2048]{1,0:T(8,128)(2,1)} %get-tuple-element.91.right_ref, bf16[1024,2048]{1,0:T(8,128)(2,1)} %collective-permute-done.32.refs_0_), custom_call_target="tpu_custom_call" | custom-call | flops 4294967296 | bytes 18874368 | tf_op jit(solution)/shard_map/pallas_call | solution.py:229
  394.5 3.0 collective-permute-start.37
  399.5 4.2 collective-permute-done.37
  403.8 2.4 collective-permute-start.39
  408.0 2.0 collective-permute-start.44
  410.0 15.9 %collective-permute-done.40 = bf16[1,2,1,1,64,1024]{5,4,3,2,1,0:T(8,128)(2,1)S(1)} collective-permute-done((bf16[1,2,1,1,64,1024]{5,4,3,2,1,0:T(8,128)(2,1)S(1)}, bf16[1,2,1,1,64,1024]{5,4,3,2,1,0:T(8,128)(2,1)S(1)}, u32[]{:S(2)}, u32[]{:S(2)}) %collective-permute-start.40) | collective-permute-done | bytes 262176 | tf_op jit(solution)/shard_map/ppermute | solution.py:62
  426.0 5.2 %collective-permute-done.39 = bf16[1,1,1,2,64,1024]{5,4,3,2,1,0:T(8,128)(2,1)S(1)} collective-permute-done((bf16[1,1,1,2,64,1024]{5,4,3,2,1,0:T(8,128)(2,1)S(1)}, bf16[1,1,1,2,64,1024]{5,4,3,2,1,0:T(8,128)(2,1)S(1)}, u32[]{:S(2)}, u32[]{:S(2)}) %collective-permute-start.39) | collective-permute-done | bytes 262176 | tf_op jit(solution)/shard_map/ppermute | solution.py:62
  433.8 6.7 %shard_map.168 = f32[1024,4,256]{2,1,0:T(4,128)} custom-call(bf16[1024,1024]{1,0:T(8,128)(2,1)S(1)} %copy-done.2, bf16[1024,1024]{1,0:T(8,128)(2,1)S(1)} %copy-done.11, bf16[1024,1024]{1,0:T(8,128)(2,1)} %copy-done.29), custom_call_target="tpu_custom_call" | custom-call | flops 2147483648 | bytes 10485760 | tf_op jit(solution)/shard_map/pallas_call | solution.py:229
  446.9 2.0 collective-permute-done.47
  449.7 3.1 collective-permute-done.48
  452.9 3.7 collective-permute-done.49
  457.9 3.4 collective-permute-done.50
  463.9 3.2 shard_map.170
  467.2 3.5 shard_map.171
  470.7 6.0 %shard_map.169 = f32[1024,2048]{1,0:T(8,128)} custom-call(s32[1]{0:T(128)} %bitcast.33.at, bf16[512,1024]{1,0:T(8,128)(2,1)} %bitcast.38.refs_0_, bf16[512,1024]{1,0:T(8,128)(2,1)} %bitcast.39.refs_1_, bf16[512,1024]{1,0:T(8,128)(2,1)S(1)} %bitcast.118, bf16[512,1024]{1,0:T(8,128)(2,1)} %bitcast.41.refs_3_), custom_call_target="tpu_custom_call" | custom-call | bytes 12582912 | tf_op jit(solution)/shard_map/pallas_call | solution.py:326
  477.2 2.0 copy.48
  (326 shorter events, 92.3 us)
Async XLA Ops:
  7.2 68.0 %all-gather.5.cloned.1.call-start = ((), (), s32[]{:S(2)}) async-start(), calls=%async_computation.2 | async-start | bytes 4456448 | tf_op jit(solution)/shard_map/all_gather | solution.py:448
  8.9 285.1 %copy-start.20 = (bf16[1024,3,128]{0,2,1:T(8,128)(2,1)}, bf16[1024,3,128]{0,2,1:T(8,128)(2,1)S(1)}, u32[]{:S(2)}) copy-start(bf16[1024,3,128]{0,2,1:T(8,128)(2,1)S(1)} %copy.31) | copy-start | bytes 2359300
  11.0 109.1 %all-gather.7.cloned.1.call-start = ((), (), s32[]{:S(2)}) async-start(), calls=%async_computation.3 | async-start | bytes 4456448 | tf_op jit(solution)/shard_map/all_gather | solution.py:448
  11.0 28.5 %collective-permute-start.1 = (bf16[1024,384]{0,1:T(8,128)(2,1)S(1)}, bf16[1024,384]{0,1:T(8,128)(2,1)S(1)}, u32[]{:S(2)}, u32[]{:S(2)}) collective-permute-start(bf16[1024,384]{0,1:T(8,128)(2,1)S(1)} %bitcast.119), channel_id=1, source_target_pairs={{0,16},{16,0},{1,17},{17,1},{2,18},{18,2},{3,19},{19,3},{4,20},{20... | collective-permute-start | bytes 2359304 | tf_op jit(solution)/shard_map/ppermute | solution.py:347
  14.1 27.7 %collective-permute-start.2 = (bf16[128,1024]{0,1:T(8,128)(2,1)}, bf16[128,1024]{0,1:T(8,128)(2,1)S(1)}, u32[]{:S(2)}, u32[]{:S(2)}) collective-permute-start(bf16[128,1024]{0,1:T(8,128)(2,1)} %convert_bitcast_fusion), channel_id=1, source_target_pairs={{0,16},{16,0},{1,17},{17,1},{2,18},{18,2},{3,19},{19,3},{4,20},{20... | collective-permute-start | bytes 786440 | tf_op jit(solution)/shard_map/ppermute | solution.py:347
  14.8 24.6 %collective-permute-start = (bf16[2,1024]{1,0:T(2,128)(2,1)S(1)}, bf16[2,1024]{1,0:T(2,128)(2,1)S(1)}, u32[]{:S(2)}, u32[]{:S(2)}) collective-permute-start(bf16[2,1024]{1,0:T(2,128)(2,1)S(1)} %convert_element_type.355), channel_id=1, source_target_pairs={{0,16},{16,0},{1,17},{17,1},{2,18},{18,2},{3,19},{19,3},{4,20},{20... | collective-permute-start | bytes 12296 | tf_op jit(solution)/shard_map/ppermute | solution.py:347
  42.5 136.8 %collective-permute-start.11 = (bf16[1024,3072]{1,0:T(8,128)(2,1)}, bf16[1024,3072]{1,0:T(8,128)(2,1)}, u32[]{:S(2)}, u32[]{:S(2)}) collective-permute-start(bf16[1024,3072]{1,0:T(8,128)(2,1)} %shard_map.162.wa), channel_id=1, source_target_pairs={{0,16},{16,0},{1,17},{17,1},{2,18},{18,2},{3,19},{19,3},{4,20},{20... | collective-permute-start | bytes 18874376 | tf_op jit(solution)/shard_map/ppermute | solution.py:347
  58.5 16.6 %all-to-all-start = ((bf16[16,64,128]{2,1,0:T(8,128)(2,1)}), bf16[16,64,128]{2,1,0:T(8,128)(2,1)S(1)}, u32[]{:S(2)}, u32[]{:S(2)}) async-start(bf16[16,64,128]{2,1,0:T(8,128)(2,1)} %bitcast.3), calls=%async_computation | async-start | bytes 524288 | tf_op jit(solution)/shard_map/all_to_all | solution.py:463
  123.8 40.1 %copy-start.17 = (bf16[1024,2048]{1,0:T(8,128)(2,1)S(1)}, bf16[1024,2048]{1,0:T(8,128)(2,1)}, u32[]{:S(2)}) copy-start(bf16[1024,2048]{1,0:T(8,128)(2,1)} %shard_map.164) | copy-start | bytes 12582916
  123.8 130.6 %copy-start.56 = (f32[64]{0:T(128)}, f32[64]{0:T(128)S(1)}, u32[]{:S(2)}) copy-start(f32[64]{0:T(128)S(1)} %add_rsqrt_fusion.2) | copy-start | bytes 772
  123.9 5.7 %collective-permute-start.7 = (bf16[1,1,1,1,64,1024]{5,4,3,2,1,0:T(8,128)(2,1)S(1)}, bf16[1,1,1,1,64,1024]{5,4,3,2,1,0:T(8,128)(2,1)S(1)}, u32[]{:S(2)}, u32[]{:S(2)}) collective-permute-start(bf16[1,1,1,1,64,1024]{5,4,3,2,1,0:T(8,128)(2,1)S(1)} %get-tuple-element.135), channel_id=1, source_target_pairs={{0,2},{1,3},{2,0},{3,1},{4,6},{5,7},{6,4},{7,5},{8,10},{9,11},{10,... | collective-permute-start | bytes 393224 | tf_op jit(solution)/shard_map/ppermute | solution.py:62
  125.4 13.1 %collective-permute-start.3 = (bf16[1,1,1,1,64,1024]{5,4,3,2,1,0:T(8,128)(2,1)S(1)}, bf16[1,1,1,1,64,1024]{5,4,3,2,1,0:T(8,128)(2,1)S(1)}, u32[]{:S(2)}, u32[]{:S(2)}) collective-permute-start(bf16[1,1,1,1,64,1024]{5,4,3,2,1,0:T(8,128)(2,1)S(1)} %get-tuple-element.136), channel_id=1, source_target_pairs={{0,8},{4,12},{8,0},{12,4},{1,9},{5,13},{9,1},{13,5},{2,10},{6,14},... | collective-permute-start | bytes 393224 | tf_op jit(solution)/shard_map/ppermute | solution.py:62
  129.7 14.5 %collective-permute-start.8 = (bf16[1,2,1,1,64,1024]{5,4,3,2,1,0:T(8,128)(2,1)S(1)}, bf16[1,2,1,1,64,1024]{5,4,3,2,1,0:T(8,128)(2,1)S(1)}, u32[]{:S(2)}, u32[]{:S(2)}) collective-permute-start(bf16[1,2,1,1,64,1024]{5,4,3,2,1,0:T(8,128)(2,1)S(1)} %pad_maximum_fusion.10), channel_id=1, source_target_pairs={{0,8},{4,12},{8,0},{12,4},{1,9},{5,13},{9,1},{13,5},{2,10},{6,14},... | collective-permute-start | bytes 786440 | tf_op jit(solution)/shard_map/ppermute | solution.py:62
  138.6 11.2 %collective-permute-start.4 = (bf16[1,1,1,2,64,1024]{5,4,3,2,1,0:T(8,128)(2,1)S(1)}, bf16[1,1,1,2,64,1024]{5,4,3,2,1,0:T(8,128)(2,1)S(1)}, u32[]{:S(2)}, u32[]{:S(2)}) collective-permute-start(bf16[1,1,1,2,64,1024]{5,4,3,2,1,0:T(8,128)(2,1)S(1)} %pad_maximum_fusion.9), channel_id=1, source_target_pairs={{0,4},{4,0},{8,12},{12,8},{1,5},{5,1},{9,13},{13,9},{2,6},{6,2},{1... | collective-permute-start | bytes 786440 | tf_op jit(solution)/shard_map/ppermute | solution.py:62
  144.2 16.7 %collective-permute-start.9 = (bf16[1,2,1,2,64,1024]{5,4,3,2,1,0:T(8,128)(2,1)S(1)}, bf16[1,2,1,2,64,1024]{5,4,3,2,1,0:T(8,128)(2,1)S(1)}, u32[]{:S(2)}, u32[]{:S(2)}) collective-permute-start(bf16[1,2,1,2,64,1024]{5,4,3,2,1,0:T(8,128)(2,1)S(1)} %pad_maximum_fusion.6), channel_id=1, source_target_pairs={{0,4},{4,0},{8,12},{12,8},{1,5},{5,1},{9,13},{13,9},{2,6},{6,2},{1... | collective-permute-start | bytes 1572872 | tf_op jit(solution)/shard_map/ppermute | solution.py:62
  149.8 13.9 %collective-permute-start.5 = (bf16[1,1,2,2,64,1024]{5,4,3,2,1,0:T(8,128)(2,1)S(1)}, bf16[1,1,2,2,64,1024]{5,4,3,2,1,0:T(8,128)(2,1)S(1)}, u32[]{:S(2)}, u32[]{:S(2)}) collective-permute-start(bf16[1,1,2,2,64,1024]{5,4,3,2,1,0:T(8,128)(2,1)S(1)} %pad_maximum_fusion.5), channel_id=1, source_target_pairs={{0,2},{1,3},{2,0},{3,1},{4,6},{5,7},{6,4},{7,5},{8,10},{9,11},{10,... | collective-permute-start | bytes 1572872 | tf_op jit(solution)/shard_map/ppermute | solution.py:62
  161.0 5.5 %collective-permute-start.10 = (bf16[1,2,2,2,64,1024]{5,4,3,2,1,0:T(8,128)(2,1)S(1)}, bf16[1,2,2,2,64,1024]{5,4,3,2,1,0:T(8,128)(2,1)S(1)}, u32[]{:S(2)}, u32[]{:S(2)}) collective-permute-start(bf16[1,2,2,2,64,1024]{5,4,3,2,1,0:T(8,128)(2,1)S(1)} %pad_maximum_fusion.3), channel_id=1, source_target_pairs={{0,1},{1,0},{2,3},{3,2},{4,5},{5,4},{6,7},{7,6},{8,9},{9,8},{10,11... | collective-permute-start | bytes 3145736 | tf_op jit(solution)/shard_map/ppermute | solution.py:62
  163.9 4.2 collective-permute-start.6
  168.2 35.9 %slice-start = ((s8[6291456]{0:T(1024)(128)(4,1)}), s8[4194304]{0:T(1024)(128)(4,1)S(1)}, s32[]{:S(2)}) async-start(s8[6291456]{0:T(1024)(128)(4,1)} %bitcast.123), calls=%async_computation.6 | async-start | bytes 8388608
  198.0 48.5 %copy-start.9 = (bf16[1024,1024]{1,0:T(8,128)(2,1)}, bf16[1024,1024]{1,0:T(8,128)(2,1)S(1)}, u32[]{:S(2)}) copy-start(bf16[1024,1024]{1,0:T(8,128)(2,1)S(1)} %get-tuple-element.98.right_ref) | copy-start | bytes 6291460
  204.0 3.1 collective-permute-start.14
  206.5 6.8 %collective-permute-start.12 = (bf16[512,1024]{1,0:T(8,128)(2,1)S(1)}, bf16[512,1024]{1,0:T(8,128)(2,1)S(1)}, u32[]{:S(2)}, u32[]{:S(2)}) collective-permute-start(bf16[512,1024]{1,0:T(8,128)(2,1)S(1)} %fusion.41), channel_id=1, source_target_pairs={{0,1},{1,0},{2,3},{3,2},{4,5},{5,4},{6,7},{7,6},{8,9},{9,8},{10,11... | collective-permute-start | bytes 3145736 | tf_op jit(solution)/shard_map/ppermute | solution.py:62
  211.7 13.9 %collective-permute-start.15 = (bf16[1,2,1,2,64,1024]{5,4,3,2,1,0:T(8,128)(2,1)S(1)}, bf16[1,2,1,2,64,1024]{5,4,3,2,1,0:T(8,128)(2,1)S(1)}, u32[]{:S(2)}, u32[]{:S(2)}) collective-permute-start(bf16[1,2,1,2,64,1024]{5,4,3,2,1,0:T(8,128)(2,1)S(1)} %slice.253), channel_id=1, source_target_pairs={{0,4},{4,0},{8,12},{12,8},{1,5},{5,1},{9,13},{13,9},{2,6},{6,2},{1... | collective-permute-start | bytes 1572872 | tf_op jit(solution)/shard_map/ppermute | solution.py:62
  215.8 13.7 %collective-permute-start.13 = (bf16[1,1,2,2,64,1024]{5,4,3,2,1,0:T(8,128)(2,1)S(1)}, bf16[1,1,2,2,64,1024]{5,4,3,2,1,0:T(8,128)(2,1)S(1)}, u32[]{:S(2)}, u32[]{:S(2)}) collective-permute-start(bf16[1,1,2,2,64,1024]{5,4,3,2,1,0:T(8,128)(2,1)S(1)} %slice.250), channel_id=1, source_target_pairs={{0,2},{1,3},{2,0},{3,1},{4,6},{5,7},{6,4},{7,5},{8,10},{9,11},{10,... | collective-permute-start | bytes 1572872 | tf_op jit(solution)/shard_map/ppermute | solution.py:62
  223.8 137.1 %collective-permute-start.32 = (bf16[1024,2048]{1,0:T(8,128)(2,1)}, bf16[1024,2048]{1,0:T(8,128)(2,1)}, u32[]{:S(2)}, u32[]{:S(2)}) collective-permute-start(bf16[1024,2048]{1,0:T(8,128)(2,1)} %convolution_convert_fusion), channel_id=1, source_target_pairs={{0,16},{16,0},{1,17},{17,1},{2,18},{18,2},{3,19},{19,3},{4,20},{20... | collective-permute-start | bytes 12582920 | tf_op jit(solution)/shard_map/ppermute | solution.py:347
  229.7 13.8 %collective-permute-start.17 = (bf16[1,2,1,1,64,1024]{5,4,3,2,1,0:T(8,128)(2,1)S(1)}, bf16[1,2,1,1,64,1024]{5,4,3,2,1,0:T(8,128)(2,1)S(1)}, u32[]{:S(2)}, u32[]{:S(2)}) collective-permute-start(bf16[1,2,1,1,64,1024]{5,4,3,2,1,0:T(8,128)(2,1)S(1)} %slice.202), channel_id=1, source_target_pairs={{0,8},{4,12},{8,0},{12,4},{1,9},{5,13},{9,1},{13,5},{2,10},{6,14},... | collective-permute-start | bytes 786440 | tf_op jit(solution)/shard_map/ppermute | solution.py:62
  232.4 12.4 %collective-permute-start.16 = (bf16[1,1,1,2,64,1024]{5,4,3,2,1,0:T(8,128)(2,1)S(1)}, bf16[1,1,1,2,64,1024]{5,4,3,2,1,0:T(8,128)(2,1)S(1)}, u32[]{:S(2)}, u32[]{:S(2)}) collective-permute-start(bf16[1,1,1,2,64,1024]{5,4,3,2,1,0:T(8,128)(2,1)S(1)} %slice.200), channel_id=1, source_target_pairs={{0,4},{4,0},{8,12},{12,8},{1,5},{5,1},{9,13},{13,9},{2,6},{6,2},{1... | collective-permute-start | bytes 786440 | tf_op jit(solution)/shard_map/ppermute | solution.py:62
  244.9 5.4 %collective-permute-start.19 = (bf16[1,1,1,1,64,1024]{5,4,3,2,1,0:T(8,128)(2,1)S(1)}, bf16[1,1,1,1,64,1024]{5,4,3,2,1,0:T(8,128)(2,1)S(1)}, u32[]{:S(2)}, u32[]{:S(2)}) collective-permute-start(bf16[1,1,1,1,64,1024]{5,4,3,2,1,0:T(8,128)(2,1)S(1)} %slice.206), channel_id=1, source_target_pairs={{0,2},{1,3},{2,0},{3,1},{4,6},{5,7},{6,4},{7,5},{8,10},{9,11},{10,... | collective-permute-start | bytes 393224 | tf_op jit(solution)/shard_map/ppermute | solution.py:62
  246.5 7.1 %collective-permute-start.18 = (bf16[1,1,1,1,64,1024]{5,4,3,2,1,0:T(8,128)(2,1)S(1)}, bf16[1,1,1,1,64,1024]{5,4,3,2,1,0:T(8,128)(2,1)S(1)}, u32[]{:S(2)}, u32[]{:S(2)}) collective-permute-start(bf16[1,1,1,1,64,1024]{5,4,3,2,1,0:T(8,128)(2,1)S(1)} %slice.204), channel_id=1, source_target_pairs={{0,8},{4,12},{8,0},{12,4},{1,9},{5,13},{9,1},{13,5},{2,10},{6,14},... | collective-permute-start | bytes 393224 | tf_op jit(solution)/shard_map/ppermute | solution.py:62
  250.3 36.2 %collective-permute-start.21 = (bf16[512,1024]{1,0:T(8,128)(2,1)}, bf16[512,1024]{1,0:T(8,128)(2,1)}, u32[]{:S(2)}, u32[]{:S(2)}) collective-permute-start(bf16[512,1024]{1,0:T(8,128)(2,1)} %fusion.38), channel_id=1, source_target_pairs={{0,1},{1,0},{2,3},{3,2},{4,5},{5,4},{6,7},{7,6},{8,9},{9,8},{10,11... | collective-permute-start | bytes 3145736 | tf_op jit(solution)/shard_map/ppermute | solution.py:62
  258.2 14.3 %all-to-all-start.1 = ((bf16[64,16,128]{2,0,1:T(8,128)(2,1)}), bf16[64,16,128]{2,0,1:T(8,128)(2,1)}, u32[]{:S(2)}, u32[]{:S(2)}) async-start(bf16[64,16,128]{2,0,1:T(8,128)(2,1)} %copy_bitcast_fusion.1), calls=%async_computation.1 | async-start | bytes 524288 | tf_op jit(solution)/shard_map/all_to_all | solution.py:588
  262.5 111.2 %all-gather.9.cloned.1.call-start = ((), (), s32[]{:S(2)}) async-start(), calls=%async_computation.4 | async-start | bytes 4456448 | tf_op jit(solution)/shard_map/all_gather | solution.py:517
  266.7 23.5 %collective-permute-start.20 = (bf16[512,1024]{1,0:T(8,128)(2,1)}, bf16[512,1024]{1,0:T(8,128)(2,1)}, u32[]{:S(2)}, u32[]{:S(2)}) collective-permute-start(bf16[512,1024]{1,0:T(8,128)(2,1)} %fusion.35), channel_id=1, source_target_pairs={{0,1},{1,0},{2,3},{3,2},{4,5},{5,4},{6,7},{7,6},{8,9},{9,8},{10,11... | collective-permute-start | bytes 3145736 | tf_op jit(solution)/shard_map/ppermute | solution.py:62
  267.7 178.5 %all-gather.11.cloned.1.call-start = ((), (), s32[]{:S(2)}) async-start(), calls=%async_computation.5 | async-start | bytes 4456448 | tf_op jit(solution)/shard_map/all_gather | solution.py:522
  286.5 32.7 %collective-permute-start.27 = (bf16[512,1024]{1,0:T(8,128)(2,1)S(1)}, bf16[512,1024]{1,0:T(8,128)(2,1)S(1)}, u32[]{:S(2)}, u32[]{:S(2)}) collective-permute-start(bf16[512,1024]{1,0:T(8,128)(2,1)S(1)} %convolution_convert_fusion.2), channel_id=1, source_target_pairs={{0,1},{1,0},{2,3},{3,2},{4,5},{5,4},{6,7},{7,6},{8,9},{9,8},{10,11... | collective-permute-start | bytes 3145736 | tf_op jit(solution)/shard_map/ppermute | solution.py:62
  293.5 25.5 %collective-permute-start.23 = (bf16[1,2,1,2,64,1024]{5,4,3,2,1,0:T(8,128)(2,1)S(1)}, bf16[1,2,1,2,64,1024]{5,4,3,2,1,0:T(8,128)(2,1)S(1)}, u32[]{:S(2)}, u32[]{:S(2)}) collective-permute-start(bf16[1,2,1,2,64,1024]{5,4,3,2,1,0:T(8,128)(2,1)S(1)} %slice.213), channel_id=1, source_target_pairs={{0,4},{4,0},{8,12},{12,8},{1,5},{5,1},{9,13},{13,9},{2,6},{6,2},{1... | collective-permute-start | bytes 1572872 | tf_op jit(solution)/shard_map/ppermute | solution.py:62
  294.7 25.3 %collective-permute-start.26 = (bf16[512,1024]{1,0:T(8,128)(2,1)S(1)}, bf16[512,1024]{1,0:T(8,128)(2,1)S(1)}, u32[]{:S(2)}, u32[]{:S(2)}) collective-permute-start(bf16[512,1024]{1,0:T(8,128)(2,1)S(1)} %convolution_convert_fusion.3), channel_id=1, source_target_pairs={{0,1},{1,0},{2,3},{3,2},{4,5},{5,4},{6,7},{7,6},{8,9},{9,8},{10,11... | collective-permute-start | bytes 3145736 | tf_op jit(solution)/shard_map/ppermute | solution.py:62
  294.8 26.2 %collective-permute-start.22 = (bf16[1,1,2,2,64,1024]{5,4,3,2,1,0:T(8,128)(2,1)S(1)}, bf16[1,1,2,2,64,1024]{5,4,3,2,1,0:T(8,128)(2,1)S(1)}, u32[]{:S(2)}, u32[]{:S(2)}) collective-permute-start(bf16[1,1,2,2,64,1024]{5,4,3,2,1,0:T(8,128)(2,1)S(1)} %slice.211), channel_id=1, source_target_pairs={{0,2},{1,3},{2,0},{3,1},{4,6},{5,7},{6,4},{7,5},{8,10},{9,11},{10,... | collective-permute-start | bytes 1572872 | tf_op jit(solution)/shard_map/ppermute | solution.py:62
  320.7 22.3 %collective-permute-start.29 = (bf16[1,2,1,2,64,1024]{5,4,3,2,1,0:T(8,128)(2,1)S(1)}, bf16[1,2,1,2,64,1024]{5,4,3,2,1,0:T(8,128)(2,1)S(1)}, u32[]{:S(2)}, u32[]{:S(2)}) collective-permute-start(bf16[1,2,1,2,64,1024]{5,4,3,2,1,0:T(8,128)(2,1)S(1)} %slice.260), channel_id=1, source_target_pairs={{0,4},{4,0},{8,12},{12,8},{1,5},{5,1},{9,13},{13,9},{2,6},{6,2},{1... | collective-permute-start | bytes 1572872 | tf_op jit(solution)/shard_map/ppermute | solution.py:62
  321.2 23.7 %collective-permute-start.25 = (bf16[1,2,1,1,64,1024]{5,4,3,2,1,0:T(8,128)(2,1)S(1)}, bf16[1,2,1,1,64,1024]{5,4,3,2,1,0:T(8,128)(2,1)S(1)}, u32[]{:S(2)}, u32[]{:S(2)}) collective-permute-start(bf16[1,2,1,1,64,1024]{5,4,3,2,1,0:T(8,128)(2,1)S(1)} %slice.217), channel_id=1, source_target_pairs={{0,8},{4,12},{8,0},{12,4},{1,9},{5,13},{9,1},{13,5},{2,10},{6,14},... | collective-permute-start | bytes 786440 | tf_op jit(solution)/shard_map/ppermute | solution.py:62
  322.0 28.2 %collective-permute-start.24 = (bf16[1,1,1,2,64,1024]{5,4,3,2,1,0:T(8,128)(2,1)S(1)}, bf16[1,1,1,2,64,1024]{5,4,3,2,1,0:T(8,128)(2,1)S(1)}, u32[]{:S(2)}, u32[]{:S(2)}) collective-permute-start(bf16[1,1,1,2,64,1024]{5,4,3,2,1,0:T(8,128)(2,1)S(1)} %slice.215), channel_id=1, source_target_pairs={{0,4},{4,0},{8,12},{12,8},{1,5},{5,1},{9,13},{13,9},{2,6},{6,2},{1... | collective-permute-start | bytes 786440 | tf_op jit(solution)/shard_map/ppermute | solution.py:62
  323.4 19.8 %collective-permute-start.28 = (bf16[1,1,2,2,64,1024]{5,4,3,2,1,0:T(8,128)(2,1)S(1)}, bf16[1,1,2,2,64,1024]{5,4,3,2,1,0:T(8,128)(2,1)S(1)}, u32[]{:S(2)}, u32[]{:S(2)}) collective-permute-start(bf16[1,1,2,2,64,1024]{5,4,3,2,1,0:T(8,128)(2,1)S(1)} %slice.258), channel_id=1, source_target_pairs={{0,2},{1,3},{2,0},{3,1},{4,6},{5,7},{6,4},{7,5},{8,10},{9,11},{10,... | collective-permute-start | bytes 1572872 | tf_op jit(solution)/shard_map/ppermute | solution.py:62
  343.4 14.8 %collective-permute-start.31 = (bf16[1,2,1,1,64,1024]{5,4,3,2,1,0:T(8,128)(2,1)S(1)}, bf16[1,2,1,1,64,1024]{5,4,3,2,1,0:T(8,128)(2,1)S(1)}, u32[]{:S(2)}, u32[]{:S(2)}) collective-permute-start(bf16[1,2,1,1,64,1024]{5,4,3,2,1,0:T(8,128)(2,1)S(1)} %slice.227), channel_id=1, source_target_pairs={{0,8},{4,12},{8,0},{12,4},{1,9},{5,13},{9,1},{13,5},{2,10},{6,14},... | collective-permute-start | bytes 786440 | tf_op jit(solution)/shard_map/ppermute | solution.py:62
  345.7 14.1 %collective-permute-start.30 = (bf16[1,1,1,2,64,1024]{5,4,3,2,1,0:T(8,128)(2,1)S(1)}, bf16[1,1,1,2,64,1024]{5,4,3,2,1,0:T(8,128)(2,1)S(1)}, u32[]{:S(2)}, u32[]{:S(2)}) collective-permute-start(bf16[1,1,1,2,64,1024]{5,4,3,2,1,0:T(8,128)(2,1)S(1)} %slice.225), channel_id=1, source_target_pairs={{0,4},{4,0},{8,12},{12,8},{1,5},{5,1},{9,13},{13,9},{2,6},{6,2},{1... | collective-permute-start | bytes 786440 | tf_op jit(solution)/shard_map/ppermute | solution.py:62
  361.5 9.4 %collective-permute-start.33 = (bf16[1,1,1,1,64,1024]{5,4,3,2,1,0:T(8,128)(2,1)}, bf16[1,1,1,1,64,1024]{5,4,3,2,1,0:T(8,128)(2,1)}, u32[]{:S(2)}, u32[]{:S(2)}) collective-permute-start(bf16[1,1,1,1,64,1024]{5,4,3,2,1,0:T(8,128)(2,1)} %slice.229), channel_id=1, source_target_pairs={{0,8},{4,12},{8,0},{12,4},{1,9},{5,13},{9,1},{13,5},{2,10},{6,14},... | collective-permute-start | bytes 393224 | tf_op jit(solution)/shard_map/ppermute | solution.py:62
  363.5 8.4 %collective-permute-start.34 = (bf16[1,1,1,1,64,1024]{5,4,3,2,1,0:T(8,128)(2,1)S(1)}, bf16[1,1,1,1,64,1024]{5,4,3,2,1,0:T(8,128)(2,1)S(1)}, u32[]{:S(2)}, u32[]{:S(2)}) collective-permute-start(bf16[1,1,1,1,64,1024]{5,4,3,2,1,0:T(8,128)(2,1)S(1)} %slice.231), channel_id=1, source_target_pairs={{0,2},{1,3},{2,0},{3,1},{4,6},{5,7},{6,4},{7,5},{8,10},{9,11},{10,... | collective-permute-start | bytes 393224 | tf_op jit(solution)/shard_map/ppermute | solution.py:62
  375.0 56.3 %collective-permute-start.41 = (bf16[1024,1024]{1,0:T(8,128)(2,1)}, bf16[1024,1024]{1,0:T(8,128)(2,1)S(1)}, u32[]{:S(2)}, u32[]{:S(2)}) collective-permute-start(bf16[1024,1024]{1,0:T(8,128)(2,1)} %convolution_convert_fusion.1), channel_id=1, source_target_pairs={{0,16},{16,0},{1,17},{17,1},{2,18},{18,2},{3,19},{19,3},{4,20},{20... | collective-permute-start | bytes 6291464 | tf_op jit(solution)/shard_map/ppermute | solution.py:347
  376.9 12.1 %collective-permute-start.36 = (bf16[1,1,1,1,64,1024]{5,4,3,2,1,0:T(8,128)(2,1)S(1)}, bf16[1,1,1,1,64,1024]{5,4,3,2,1,0:T(8,128)(2,1)S(1)}, u32[]{:S(2)}, u32[]{:S(2)}) collective-permute-start(bf16[1,1,1,1,64,1024]{5,4,3,2,1,0:T(8,128)(2,1)S(1)} %slice.235), channel_id=1, source_target_pairs={{0,2},{1,3},{2,0},{3,1},{4,6},{5,7},{6,4},{7,5},{8,10},{9,11},{10,... | collective-permute-start | bytes 393224 | tf_op jit(solution)/shard_map/ppermute | solution.py:62
  377.5 13.2 %collective-permute-start.35 = (bf16[1,1,1,1,64,1024]{5,4,3,2,1,0:T(8,128)(2,1)S(1)}, bf16[1,1,1,1,64,1024]{5,4,3,2,1,0:T(8,128)(2,1)S(1)}, u32[]{:S(2)}, u32[]{:S(2)}) collective-permute-start(bf16[1,1,1,1,64,1024]{5,4,3,2,1,0:T(8,128)(2,1)S(1)} %slice.233), channel_id=1, source_target_pairs={{0,8},{4,12},{8,0},{12,4},{1,9},{5,13},{9,1},{13,5},{2,10},{6,14},... | collective-permute-start | bytes 393224 | tf_op jit(solution)/shard_map/ppermute | solution.py:62
  394.4 5.0 %collective-permute-start.38 = (bf16[1,1,1,1,64,1024]{5,4,3,2,1,0:T(8,128)(2,1)S(1)}, bf16[1,1,1,1,64,1024]{5,4,3,2,1,0:T(8,128)(2,1)S(1)}, u32[]{:S(2)}, u32[]{:S(2)}) collective-permute-start(bf16[1,1,1,1,64,1024]{5,4,3,2,1,0:T(8,128)(2,1)S(1)} %get-tuple-element.129), channel_id=1, source_target_pairs={{0,2},{1,3},{2,0},{3,1},{4,6},{5,7},{6,4},{7,5},{8,10},{9,11},{10,... | collective-permute-start | bytes 393224 | tf_op jit(solution)/shard_map/ppermute | solution.py:62
  394.5 9.2 %collective-permute-start.37 = (bf16[1,1,1,1,64,1024]{5,4,3,2,1,0:T(8,128)(2,1)S(1)}, bf16[1,1,1,1,64,1024]{5,4,3,2,1,0:T(8,128)(2,1)S(1)}, u32[]{:S(2)}, u32[]{:S(2)}) collective-permute-start(bf16[1,1,1,1,64,1024]{5,4,3,2,1,0:T(8,128)(2,1)S(1)} %get-tuple-element.130), channel_id=1, source_target_pairs={{0,8},{4,12},{8,0},{12,4},{1,9},{5,13},{9,1},{13,5},{2,10},{6,14},... | collective-permute-start | bytes 393224 | tf_op jit(solution)/shard_map/ppermute | solution.py:62
  403.7 30.1 %copy-start.2 = (bf16[1024,1024]{1,0:T(8,128)(2,1)S(1)}, bf16[1024,1024]{1,0:T(8,128)(2,1)}, u32[]{:S(2)}) copy-start(bf16[1024,1024]{1,0:T(8,128)(2,1)} %get-tuple-element.127.left_ref) | copy-start | bytes 6291460
  403.8 22.2 %collective-permute-start.40 = (bf16[1,2,1,1,64,1024]{5,4,3,2,1,0:T(8,128)(2,1)S(1)}, bf16[1,2,1,1,64,1024]{5,4,3,2,1,0:T(8,128)(2,1)S(1)}, u32[]{:S(2)}, u32[]{:S(2)}) collective-permute-start(bf16[1,2,1,1,64,1024]{5,4,3,2,1,0:T(8,128)(2,1)S(1)} %pad_maximum_fusion.13), channel_id=1, source_target_pairs={{0,8},{4,12},{8,0},{12,4},{1,9},{5,13},{9,1},{13,5},{2,10},{6,14},... | collective-permute-start | bytes 786440 | tf_op jit(solution)/shard_map/ppermute | solution.py:62
  403.8 27.4 %collective-permute-start.39 = (bf16[1,1,1,2,64,1024]{5,4,3,2,1,0:T(8,128)(2,1)S(1)}, bf16[1,1,1,2,64,1024]{5,4,3,2,1,0:T(8,128)(2,1)S(1)}, u32[]{:S(2)}, u32[]{:S(2)}) collective-permute-start(bf16[1,1,1,2,64,1024]{5,4,3,2,1,0:T(8,128)(2,1)S(1)} %pad_maximum_fusion.12), channel_id=1, source_target_pairs={{0,4},{4,0},{8,12},{12,8},{1,5},{5,1},{9,13},{13,9},{2,6},{6,2},{1... | collective-permute-start | bytes 786440 | tf_op jit(solution)/shard_map/ppermute | solution.py:62
  408.0 37.3 %collective-permute-start.44 = (bf16[1024,512]{1,0:T(8,128)(2,1)S(1)}, bf16[1024,512]{1,0:T(8,128)(2,1)S(1)}, u32[]{:S(2)}, u32[]{:S(2)}) collective-permute-start(bf16[1024,512]{1,0:T(8,128)(2,1)S(1)} %pad_maximum_fusion.4), channel_id=1, source_target_pairs={{0,16},{16,0},{1,17},{17,1},{2,18},{18,2},{3,19},{19,3},{4,20},{20... | collective-permute-start | bytes 3145736 | tf_op jit(solution)/shard_map/ppermute | solution.py:347
  431.3 11.1 %collective-permute-start.43 = (bf16[1,2,1,2,64,1024]{5,4,3,2,1,0:T(8,128)(2,1)S(1)}, bf16[1,2,1,2,64,1024]{5,4,3,2,1,0:T(8,128)(2,1)S(1)}, u32[]{:S(2)}, u32[]{:S(2)}) collective-permute-start(bf16[1,2,1,2,64,1024]{5,4,3,2,1,0:T(8,128)(2,1)S(1)} %pad_maximum_fusion.8), channel_id=1, source_target_pairs={{0,4},{4,0},{8,12},{12,8},{1,5},{5,1},{9,13},{13,9},{2,6},{6,2},{1... | collective-permute-start | bytes 1572872 | tf_op jit(solution)/shard_map/ppermute | solution.py:62
  431.4 11.1 %collective-permute-start.42 = (bf16[1,1,2,2,64,1024]{5,4,3,2,1,0:T(8,128)(2,1)S(1)}, bf16[1,1,2,2,64,1024]{5,4,3,2,1,0:T(8,128)(2,1)S(1)}, u32[]{:S(2)}, u32[]{:S(2)}) collective-permute-start(bf16[1,1,2,2,64,1024]{5,4,3,2,1,0:T(8,128)(2,1)S(1)} %pad_maximum_fusion.7), channel_id=1, source_target_pairs={{0,2},{1,3},{2,0},{3,1},{4,6},{5,7},{6,4},{7,5},{8,10},{9,11},{10,... | collective-permute-start | bytes 1572872 | tf_op jit(solution)/shard_map/ppermute | solution.py:62
  446.3 24.4 %collective-permute-start.45 = (bf16[1,2,2,2,64,1024]{5,4,3,2,1,0:T(8,128)(2,1)}, bf16[1,2,2,2,64,1024]{5,4,3,2,1,0:T(8,128)(2,1)}, u32[]{:S(2)}, u32[]{:S(2)}) collective-permute-start(bf16[1,2,2,2,64,1024]{5,4,3,2,1,0:T(8,128)(2,1)} %constant_dynamic-update-slice_fusion), channel_id=1, source_target_pairs={{0,1},{1,0},{2,3},{3,2},{4,5},{5,4},{6,7},{7,6},{8,9},{9,8},{10,11... | collective-permute-start | bytes 3145736 | tf_op jit(solution)/shard_map/ppermute | solution.py:62
  446.3 24.4 %collective-permute-start.46 = (bf16[1,2,2,2,64,1024]{5,4,3,2,1,0:T(8,128)(2,1)}, bf16[1,2,2,2,64,1024]{5,4,3,2,1,0:T(8,128)(2,1)}, u32[]{:S(2)}, u32[]{:S(2)}) collective-permute-start(bf16[1,2,2,2,64,1024]{5,4,3,2,1,0:T(8,128)(2,1)} %copy-done.7), channel_id=1, source_target_pairs={{0,1},{1,0},{2,3},{3,2},{4,5},{5,4},{6,7},{7,6},{8,9},{9,8},{10,11... | collective-permute-start | bytes 3145736 | tf_op jit(solution)/shard_map/ppermute | solution.py:62
  446.9 2.1 collective-permute-start.47
  449.0 3.8 collective-permute-start.48
  452.8 3.8 collective-permute-start.49
  456.6 4.7 collective-permute-start.50
  461.3 15.3 %collective-permute-start.51 = (f32[2,2048]{1,0:T(2,128)S(1)}, f32[2,2048]{1,0:T(2,128)S(1)}, u32[]{:S(2)}, u32[]{:S(2)}) collective-permute-start(f32[2,2048]{1,0:T(2,128)S(1)} %add.277), channel_id=1, source_target_pairs={{0,16},{16,0},{1,17},{17,1},{2,18},{18,2},{3,19},{19,3},{4,20},{20... | collective-permute-start | bytes 49160 | tf_op jit(solution)/shard_map/ppermute | solution.py:347
  (60 other events, 478.4 us)
Sparse Core Ops, SparseCore 0:
  11.1 55.7 all-gather.4
  69.0 51.0 all-gather.6
  267.8 63.1 all-gather.8
  373.8 60.0 all-gather.10

commit v5 on v4

--- a/solution.py
+++ b/solution.py
@@ -175,7 +175,7 @@
 
 
 def flat(weights, orders):
-    rows = min(256, weights[0].shape[0])
+    rows = min(128, weights[0].shape[0])
     spots = [indices(v.shape, order) for v, order in zip(weights, orders)]
     wide = weights[0].shape[-1]
     columns = sum(len(s) for s in spots) * wide
@@ -206,7 +206,7 @@
 
 
 def weight_sum(left, right, got, column, shape, order, planes=False):
-    rows, wide = min(256, shape[0]), shape[-1]
+    rows, wide = min(512, shape[0]), shape[-1]
     tokens, columns = right.shape
     spots = indices(shape, order)
     widths = [columns] if column or len(got) == 1 else [v.shape[1] for v in got]
@@ -302,7 +302,7 @@
     )(first.reshape(1), named, *h, *weights, grad_part, grad_rest, weights[1])
 
 
-def ordered(pairs, start, dtype, tile=512):
+def ordered(pairs, start, dtype, tile=1024):
     rows, cols = pairs[0][0].shape
     per, block = cols // tile, rows // 8
 

time: 495 us -> 493 us (level)
  no operation moved by 1% of the time
where the time goes in v5:
time: 493 us; the launch traced here: 485 us
  waiting for transfers between devices  207 us (42%)
  matrix products  77.7 us (16%)
  Pallas kernels  75.2 us (15%)
  starting transfers between devices  59.8 us (12%)
  other arithmetic  28.2 us (6%)
  local copies, waits for them, and re-layouts  21.1 us (4%)
  between operations  15.5 us (3%)
    ppermute x44, waiting for transfers between devices, swap(): lax.ppermute(v, name, [(i, i ^ bit) for i in range(lax.axis_size(name))])  146 us
    dot_general x23, matrix products, dot(): lax.dot_general(a, b, (((ca,), (cb,)), ((), ())), preferred_element_type=...  68.2 us
    all_gather x2, waiting for transfers between devices, local(): w_o_full = [lax.all_gather(w, GROUP, axis=0, tiled=True) for w in w_o]  41.7 us
    ppermute x44, starting transfers between devices, swap(): lax.ppermute(v, name, [(i, i ^ bit) for i in range(lax.axis_size(name))])  38.1 us
    pallas_call x4, Pallas kernels, weight_sum(): pl.pallas_call(kernel, grid=(left.shape[1] // rows,), in_specs=[pl.BlockS...  23.4 us
    pallas_call x1, Pallas kernels, experts(): pl.pallas_call(kernel, grid=(count, tokens // rows), in_specs=[pl.BlockSp...  18.6 us
    pallas_call x1, Pallas kernels, flat(): pl.pallas_call(kernel, grid=(count // rows,), in_specs=[spec(v) for v in...  14.6 us
    pallas_call x3, Pallas kernels, reorder(): pl.pallas_call(kernel, grid_spec=pltpu.PrefetchScalarGridSpec(num_scalar_...  12.8 us
  transfers between devices with their start and end apart: 58, of which 32 were waited for; matrix products, arithmetic and copies ran while one was open for 22% of the time, Pallas kernels for 12%

profile of v5, /device:TPU:0, one launch (start us, length us, event | category | flops | bytes accessed | tf_op | source)
XLA Modules:
  0.0 484.6 jit_solution(8089230652872632948)
XLA Ops:
  8.9 2.1 convert_bitcast_fusion
  11.0 3.0 collective-permute-start.1
  16.8 2.2 copy-done.4
  19.0 14.6 %shard_map.162.wa = bf16[1024,3072]{1,0:T(8,128)(2,1)} custom-call(f32[1024,2,4,256]{3,2,1,0:T(4,128)} %refs_0_.2, f32[1024,4,256]{2,1,0:T(4,128)S(1)} %copy-done.4), custom_call_target="tpu_custom_call" | custom-call | bytes 18874368 | tf_op jit(solution)/shard_map/pallas_call | solution.py:195
  33.6 3.3 fusion.3
  39.0 2.3 add_convert_fusion.6
  43.9 2.6 shard_map.163.named_ref
  47.1 7.4 %shard_map.164 = bf16[1024,2048]{1,0:T(8,128)(2,1)} custom-call(s32[2]{0:T(128)} %pad_add_fusion.1.at, bf16[1024,2048]{1,0:T(8,128)(2,1)} %refs_0_.3), custom_call_target="tpu_custom_call" | custom-call | bytes 16777216 | tf_op jit(solution)/shard_map/pallas_call | solution.py:153
  58.0 6.5 %all-to-all-start = ((bf16[16,64,128]{2,1,0:T(8,128)(2,1)}), bf16[16,64,128]{2,1,0:T(8,128)(2,1)S(1)}, u32[]{:S(2)}, u32[]{:S(2)}) async-start(bf16[16,64,128]{2,1,0:T(8,128)(2,1)} %bitcast.3), calls=%async_computation | async-start | bytes 524288 | tf_op jit(solution)/shard_map/all_to_all | solution.py:463
  64.5 6.8 %fusion.33.part = f32[1024,1024]{1,0:T(8,128)} fusion(bf16[1024,3072]{1,0:T(8,128)(2,1)} %shard_map.162.wa, bf16[1024,2048]{1,0:T(8,128)(2,1)} %shard_map.164), kind=kOutput, calls=%fused_computation.53 | convolution fusion | flops 2147483648 | bytes 8388608 | tf_op jit(solution)/shard_map/dot_general | solution.py:53
  71.3 3.2 all-to-all-done
  74.6 3.8 multiply_reduce_fusion.2
  78.4 41.7 %all-gather.7.cloned.1.call-done = bf16[2048,1024]{0,1:T(8,128)(2,1)} async-done(((bf16[128,1024]{0,1:T(8,128)(2,1)}), bf16[2048,1024]{0,1:T(8,128)(2,1)}) %all-gather.7.cloned.1.call-update) | async-done | bytes 4194320 | tf_op jit(solution)/shard_map/all_gather | solution.py:448
  120.1 3.7 multiply_reduce_fusion.1
  126.1 3.6 collective-permute-done.7
  131.3 7.3 %collective-permute-done.3 = bf16[1,1,1,1,64,1024]{5,4,3,2,1,0:T(8,128)(2,1)S(1)} collective-permute-done((bf16[1,1,1,1,64,1024]{5,4,3,2,1,0:T(8,128)(2,1)S(1)}, bf16[1,1,1,1,64,1024]{5,4,3,2,1,0:T(8,128)(2,1)S(1)}, u32[]{:S(2)}, u32[]{:S(2)}) %collective-permute-start.3) | collective-permute-done | bytes 131104 | tf_op jit(solution)/shard_map/ppermute | solution.py:62
  139.1 5.1 %collective-permute-done.8 = bf16[1,2,1,1,64,1024]{5,4,3,2,1,0:T(8,128)(2,1)S(1)} collective-permute-done((bf16[1,2,1,1,64,1024]{5,4,3,2,1,0:T(8,128)(2,1)S(1)}, bf16[1,2,1,1,64,1024]{5,4,3,2,1,0:T(8,128)(2,1)S(1)}, u32[]{:S(2)}, u32[]{:S(2)}) %collective-permute-start.8) | collective-permute-done | bytes 262176 | tf_op jit(solution)/shard_map/ppermute | solution.py:62
  144.3 5.5 %collective-permute-done.4 = bf16[1,1,1,2,64,1024]{5,4,3,2,1,0:T(8,128)(2,1)S(1)} collective-permute-done((bf16[1,1,1,2,64,1024]{5,4,3,2,1,0:T(8,128)(2,1)S(1)}, bf16[1,1,1,2,64,1024]{5,4,3,2,1,0:T(8,128)(2,1)S(1)}, u32[]{:S(2)}, u32[]{:S(2)}) %collective-permute-start.4) | collective-permute-done | bytes 262176 | tf_op jit(solution)/shard_map/ppermute | solution.py:62
  151.3 9.6 %collective-permute-done.9 = bf16[1,2,1,2,64,1024]{5,4,3,2,1,0:T(8,128)(2,1)S(1)} collective-permute-done((bf16[1,2,1,2,64,1024]{5,4,3,2,1,0:T(8,128)(2,1)S(1)}, bf16[1,2,1,2,64,1024]{5,4,3,2,1,0:T(8,128)(2,1)S(1)}, u32[]{:S(2)}, u32[]{:S(2)}) %collective-permute-start.9) | collective-permute-done | bytes 524320 | tf_op jit(solution)/shard_map/ppermute | solution.py:62
  161.3 2.5 collective-permute-done.5
  164.0 2.5 fusion.134
  168.4 10.4 %collective-permute-done.11.wb.ob = bf16[1024,3072]{1,0:T(8,128)(2,1)} collective-permute-done((bf16[1024,3072]{1,0:T(8,128)(2,1)}, bf16[1024,3072]{1,0:T(8,128)(2,1)}, u32[]{:S(2)}, u32[]{:S(2)}) %collective-permute-start.11) | collective-permute-done | bytes 6291488 | tf_op jit(solution)/shard_map/ppermute | solution.py:347
  178.8 18.6 %shard_map.165 = (bf16[1024,1024]{1,0:T(8,128)(2,1)S(1)}, bf16[1024,2048]{1,0:T(8,128)(2,1)}) custom-call(s32[1]{0:T(128)} %bitcast.8.first_ref, f32[1024,128]{1,0:T(8,128)S(1)} %copy-done.12, bf16[1024,1024]{1,0:T(8,128)(2,1)S(1)} %pad_maximum_fusion.ha.left_ref, bf16[1024,1024]{1,0:T(8,128)(2,1)} %pad_maximum_fusion.1.hb, ...), custom_call_target="tpu_custom_call" | custom-call | flops 10737418240 | bytes 29360128 | tf_op jit(solution)/shard_map/pallas_call | solution.py:277
  197.5 6.0 %fusion.46 = bf16[512,1024]{1,0:T(8,128)(2,1)S(1)} fusion(bf16[1024,3072]{1,0:T(8,128)(2,1)} %collective-permute-done.11.wb.ob, bf16[1024,2048]{1,0:T(8,128)(2,1)} %get-tuple-element.91.right_ref), kind=kOutput, calls=%fused_computation.61 | convolution fusion | flops 2148007936 | bytes 7340032 | tf_op jit(solution)/shard_map/dot_general | solution.py:53
  203.6 2.4 fusion.41
  206.5 4.6 add_convert_fusion.4
  212.8 2.4 add_convert_fusion.5
  216.8 6.4 %convolution_convert_fusion = bf16[1024,2048]{1,0:T(8,128)(2,1)} fusion(bf16[1024,2048]{1,0:T(8,128)(2,1)S(1)} %copy-done.26, bf16[512,1024]{1,0:T(8,128)(2,1)S(1)} %bitcast.142, bf16[512,1024]{1,0:T(8,128)(2,1)S(1)} %bitcast.130), kind=kOutput, calls=%fused_computation.17 | convolution fusion | flops 4301258752 | bytes 10485760 | tf_op jit(solution)/shard_map/dot_general | solution.py:53
  225.3 3.6 collective-permute-done.13
  229.2 2.7 collective-permute-start.17
  232.3 3.8 convolution_convert_fusion.1
  236.1 6.9 %collective-permute-done.17 = bf16[1,2,1,1,64,1024]{5,4,3,2,1,0:T(8,128)(2,1)S(1)} collective-permute-done((bf16[1,2,1,1,64,1024]{5,4,3,2,1,0:T(8,128)(2,1)S(1)}, bf16[1,2,1,1,64,1024]{5,4,3,2,1,0:T(8,128)(2,1)S(1)}, u32[]{:S(2)}, u32[]{:S(2)}) %collective-permute-start.17) | collective-permute-done | bytes 262176 | tf_op jit(solution)/shard_map/ppermute | solution.py:62
  246.0 3.9 fusion.38
  249.9 3.2 collective-permute-done.18
  257.7 4.2 all-to-all-start.1
  262.0 4.2 fusion.35
  267.4 4.5 all-to-all-done.1
  272.0 3.4 multiply_reduce_fusion
  281.2 2.8 shard_map.166
  286.0 3.6 add_convert_fusion.2
  289.7 3.2 add_convert_fusion.3
  295.4 23.0 %collective-permute-done.23 = bf16[1,2,1,2,64,1024]{5,4,3,2,1,0:T(8,128)(2,1)S(1)} collective-permute-done((bf16[1,2,1,2,64,1024]{5,4,3,2,1,0:T(8,128)(2,1)S(1)}, bf16[1,2,1,2,64,1024]{5,4,3,2,1,0:T(8,128)(2,1)S(1)}, u32[]{:S(2)}, u32[]{:S(2)}) %collective-permute-start.23) | collective-permute-done | bytes 524320 | tf_op jit(solution)/shard_map/ppermute | solution.py:62
  323.6 2.3 convolution_convert_fusion.4
  325.9 16.6 %collective-permute-done.29 = bf16[1,2,1,2,64,1024]{5,4,3,2,1,0:T(8,128)(2,1)S(1)} collective-permute-done((bf16[1,2,1,2,64,1024]{5,4,3,2,1,0:T(8,128)(2,1)S(1)}, bf16[1,2,1,2,64,1024]{5,4,3,2,1,0:T(8,128)(2,1)S(1)}, u32[]{:S(2)}, u32[]{:S(2)}) %collective-permute-start.29) | collective-permute-done | bytes 524320 | tf_op jit(solution)/shard_map/ppermute | solution.py:62
  345.1 2.5 collective-permute-start.30
  349.8 8.0 %collective-permute-done.31 = bf16[1,2,1,1,64,1024]{5,4,3,2,1,0:T(8,128)(2,1)S(1)} collective-permute-done((bf16[1,2,1,1,64,1024]{5,4,3,2,1,0:T(8,128)(2,1)S(1)}, bf16[1,2,1,1,64,1024]{5,4,3,2,1,0:T(8,128)(2,1)S(1)}, u32[]{:S(2)}, u32[]{:S(2)}) %collective-permute-start.31) | collective-permute-done | bytes 262176 | tf_op jit(solution)/shard_map/ppermute | solution.py:62
  363.0 2.5 collective-permute-start.34
  365.5 4.9 %collective-permute-done.33 = bf16[1,1,1,1,64,1024]{5,4,3,2,1,0:T(8,128)(2,1)} collective-permute-done((bf16[1,1,1,1,64,1024]{5,4,3,2,1,0:T(8,128)(2,1)}, bf16[1,1,1,1,64,1024]{5,4,3,2,1,0:T(8,128)(2,1)}, u32[]{:S(2)}, u32[]{:S(2)}) %collective-permute-start.33) | collective-permute-done | bytes 131104 | tf_op jit(solution)/shard_map/ppermute | solution.py:62
  377.0 11.9 %shard_map.167 = f32[1024,2,4,256]{3,2,1,0:T(4,128)} custom-call(bf16[1024,1024]{1,0:T(8,128)(2,1)S(1)} %pad_maximum_fusion.ha.left_ref, bf16[1024,2048]{1,0:T(8,128)(2,1)} %get-tuple-element.91.right_ref, bf16[1024,2048]{1,0:T(8,128)(2,1)} %collective-permute-done.32.refs_0_), custom_call_target="tpu_custom_call" | custom-call | flops 4294967296 | bytes 18874368 | tf_op jit(solution)/shard_map/pallas_call | solution.py:229
  394.3 3.0 collective-permute-start.37
  399.0 4.4 collective-permute-done.37
  403.6 2.3 collective-permute-start.39
  407.7 3.5 collective-permute-start.44
  411.2 14.7 %collective-permute-done.40 = bf16[1,2,1,1,64,1024]{5,4,3,2,1,0:T(8,128)(2,1)S(1)} collective-permute-done((bf16[1,2,1,1,64,1024]{5,4,3,2,1,0:T(8,128)(2,1)S(1)}, bf16[1,2,1,1,64,1024]{5,4,3,2,1,0:T(8,128)(2,1)S(1)}, u32[]{:S(2)}, u32[]{:S(2)}) %collective-permute-start.40) | collective-permute-done | bytes 262176 | tf_op jit(solution)/shard_map/ppermute | solution.py:62
  425.9 4.9 %collective-permute-done.39 = bf16[1,1,1,2,64,1024]{5,4,3,2,1,0:T(8,128)(2,1)S(1)} collective-permute-done((bf16[1,1,1,2,64,1024]{5,4,3,2,1,0:T(8,128)(2,1)S(1)}, bf16[1,1,1,2,64,1024]{5,4,3,2,1,0:T(8,128)(2,1)S(1)}, u32[]{:S(2)}, u32[]{:S(2)}) %collective-permute-start.39) | collective-permute-done | bytes 262176 | tf_op jit(solution)/shard_map/ppermute | solution.py:62
  433.5 6.2 %shard_map.168 = f32[1024,4,256]{2,1,0:T(4,128)} custom-call(bf16[1024,1024]{1,0:T(8,128)(2,1)S(1)} %copy-done.2, bf16[1024,1024]{1,0:T(8,128)(2,1)S(1)} %copy-done.11, bf16[1024,1024]{1,0:T(8,128)(2,1)} %copy-done.29), custom_call_target="tpu_custom_call" | custom-call | flops 2147483648 | bytes 10485760 | tf_op jit(solution)/shard_map/pallas_call | solution.py:229
  439.7 2.5 collective-permute-done.43
  446.4 2.0 collective-permute-done.47
  449.5 2.8 collective-permute-done.48
  452.3 3.7 collective-permute-done.49
  457.6 3.2 collective-permute-done.50
  463.9 2.6 shard_map.170
  466.5 2.7 shard_map.171
  469.2 5.7 %shard_map.169 = f32[1024,2048]{1,0:T(8,128)} custom-call(s32[1]{0:T(128)} %bitcast.33.at, bf16[512,1024]{1,0:T(8,128)(2,1)} %bitcast.38.refs_0_, bf16[512,1024]{1,0:T(8,128)(2,1)} %bitcast.39.refs_1_, bf16[512,1024]{1,0:T(8,128)(2,1)S(1)} %bitcast.118, bf16[512,1024]{1,0:T(8,128)(2,1)} %bitcast.41.refs_3_), custom_call_target="tpu_custom_call" | custom-call | bytes 12582912 | tf_op jit(solution)/shard_map/pallas_call | solution.py:326
  (326 shorter events, 93.0 us)
Async XLA Ops:
  7.2 67.4 %all-gather.5.cloned.1.call-start = ((), (), s32[]{:S(2)}) async-start(), calls=%async_computation.2 | async-start | bytes 4456448 | tf_op jit(solution)/shard_map/all_gather | solution.py:448
  8.9 284.5 %copy-start.20 = (bf16[1024,3,128]{0,2,1:T(8,128)(2,1)}, bf16[1024,3,128]{0,2,1:T(8,128)(2,1)S(1)}, u32[]{:S(2)}) copy-start(bf16[1024,3,128]{0,2,1:T(8,128)(2,1)S(1)} %copy.31) | copy-start | bytes 2359300
  11.0 109.1 %all-gather.7.cloned.1.call-start = ((), (), s32[]{:S(2)}) async-start(), calls=%async_computation.3 | async-start | bytes 4456448 | tf_op jit(solution)/shard_map/all_gather | solution.py:448
  11.0 27.9 %collective-permute-start.1 = (bf16[1024,384]{0,1:T(8,128)(2,1)S(1)}, bf16[1024,384]{0,1:T(8,128)(2,1)S(1)}, u32[]{:S(2)}, u32[]{:S(2)}) collective-permute-start(bf16[1024,384]{0,1:T(8,128)(2,1)S(1)} %bitcast.119), channel_id=1, source_target_pairs={{0,16},{16,0},{1,17},{17,1},{2,18},{18,2},{3,19},{19,3},{4,20},{20... | collective-permute-start | bytes 2359304 | tf_op jit(solution)/shard_map/ppermute | solution.py:347
  14.1 27.2 %collective-permute-start.2 = (bf16[128,1024]{0,1:T(8,128)(2,1)}, bf16[128,1024]{0,1:T(8,128)(2,1)S(1)}, u32[]{:S(2)}, u32[]{:S(2)}) collective-permute-start(bf16[128,1024]{0,1:T(8,128)(2,1)} %convert_bitcast_fusion), channel_id=1, source_target_pairs={{0,16},{16,0},{1,17},{17,1},{2,18},{18,2},{3,19},{19,3},{4,20},{20... | collective-permute-start | bytes 786440 | tf_op jit(solution)/shard_map/ppermute | solution.py:347
  14.8 24.1 %collective-permute-start = (bf16[2,1024]{1,0:T(2,128)(2,1)S(1)}, bf16[2,1024]{1,0:T(2,128)(2,1)S(1)}, u32[]{:S(2)}, u32[]{:S(2)}) collective-permute-start(bf16[2,1024]{1,0:T(2,128)(2,1)S(1)} %convert_element_type.355), channel_id=1, source_target_pairs={{0,16},{16,0},{1,17},{17,1},{2,18},{18,2},{3,19},{19,3},{4,20},{20... | collective-permute-start | bytes 12296 | tf_op jit(solution)/shard_map/ppermute | solution.py:347
  42.0 136.8 %collective-permute-start.11 = (bf16[1024,3072]{1,0:T(8,128)(2,1)}, bf16[1024,3072]{1,0:T(8,128)(2,1)}, u32[]{:S(2)}, u32[]{:S(2)}) collective-permute-start(bf16[1024,3072]{1,0:T(8,128)(2,1)} %shard_map.162.wa), channel_id=1, source_target_pairs={{0,16},{16,0},{1,17},{17,1},{2,18},{18,2},{3,19},{19,3},{4,20},{20... | collective-permute-start | bytes 18874376 | tf_op jit(solution)/shard_map/ppermute | solution.py:347
  58.0 16.6 %all-to-all-start = ((bf16[16,64,128]{2,1,0:T(8,128)(2,1)}), bf16[16,64,128]{2,1,0:T(8,128)(2,1)S(1)}, u32[]{:S(2)}, u32[]{:S(2)}) async-start(bf16[16,64,128]{2,1,0:T(8,128)(2,1)} %bitcast.3), calls=%async_computation | async-start | bytes 524288 | tf_op jit(solution)/shard_map/all_to_all | solution.py:463
  123.8 40.1 %copy-start.17 = (bf16[1024,2048]{1,0:T(8,128)(2,1)S(1)}, bf16[1024,2048]{1,0:T(8,128)(2,1)}, u32[]{:S(2)}) copy-start(bf16[1024,2048]{1,0:T(8,128)(2,1)} %shard_map.164) | copy-start | bytes 12582916
  123.9 130.1 %copy-start.56 = (f32[64]{0:T(128)}, f32[64]{0:T(128)S(1)}, u32[]{:S(2)}) copy-start(f32[64]{0:T(128)S(1)} %add_rsqrt_fusion.2) | copy-start | bytes 772
  124.0 5.7 %collective-permute-start.7 = (bf16[1,1,1,1,64,1024]{5,4,3,2,1,0:T(8,128)(2,1)S(1)}, bf16[1,1,1,1,64,1024]{5,4,3,2,1,0:T(8,128)(2,1)S(1)}, u32[]{:S(2)}, u32[]{:S(2)}) collective-permute-start(bf16[1,1,1,1,64,1024]{5,4,3,2,1,0:T(8,128)(2,1)S(1)} %get-tuple-element.135), channel_id=1, source_target_pairs={{0,2},{1,3},{2,0},{3,1},{4,6},{5,7},{6,4},{7,5},{8,10},{9,11},{10,... | collective-permute-start | bytes 393224 | tf_op jit(solution)/shard_map/ppermute | solution.py:62
  125.5 13.1 %collective-permute-start.3 = (bf16[1,1,1,1,64,1024]{5,4,3,2,1,0:T(8,128)(2,1)S(1)}, bf16[1,1,1,1,64,1024]{5,4,3,2,1,0:T(8,128)(2,1)S(1)}, u32[]{:S(2)}, u32[]{:S(2)}) collective-permute-start(bf16[1,1,1,1,64,1024]{5,4,3,2,1,0:T(8,128)(2,1)S(1)} %get-tuple-element.136), channel_id=1, source_target_pairs={{0,8},{4,12},{8,0},{12,4},{1,9},{5,13},{9,1},{13,5},{2,10},{6,14},... | collective-permute-start | bytes 393224 | tf_op jit(solution)/shard_map/ppermute | solution.py:62
  129.7 14.5 %collective-permute-start.8 = (bf16[1,2,1,1,64,1024]{5,4,3,2,1,0:T(8,128)(2,1)S(1)}, bf16[1,2,1,1,64,1024]{5,4,3,2,1,0:T(8,128)(2,1)S(1)}, u32[]{:S(2)}, u32[]{:S(2)}) collective-permute-start(bf16[1,2,1,1,64,1024]{5,4,3,2,1,0:T(8,128)(2,1)S(1)} %pad_maximum_fusion.10), channel_id=1, source_target_pairs={{0,8},{4,12},{8,0},{12,4},{1,9},{5,13},{9,1},{13,5},{2,10},{6,14},... | collective-permute-start | bytes 786440 | tf_op jit(solution)/shard_map/ppermute | solution.py:62
  138.6 11.2 %collective-permute-start.4 = (bf16[1,1,1,2,64,1024]{5,4,3,2,1,0:T(8,128)(2,1)S(1)}, bf16[1,1,1,2,64,1024]{5,4,3,2,1,0:T(8,128)(2,1)S(1)}, u32[]{:S(2)}, u32[]{:S(2)}) collective-permute-start(bf16[1,1,1,2,64,1024]{5,4,3,2,1,0:T(8,128)(2,1)S(1)} %pad_maximum_fusion.9), channel_id=1, source_target_pairs={{0,4},{4,0},{8,12},{12,8},{1,5},{5,1},{9,13},{13,9},{2,6},{6,2},{1... | collective-permute-start | bytes 786440 | tf_op jit(solution)/shard_map/ppermute | solution.py:62
  144.3 16.7 %collective-permute-start.9 = (bf16[1,2,1,2,64,1024]{5,4,3,2,1,0:T(8,128)(2,1)S(1)}, bf16[1,2,1,2,64,1024]{5,4,3,2,1,0:T(8,128)(2,1)S(1)}, u32[]{:S(2)}, u32[]{:S(2)}) collective-permute-start(bf16[1,2,1,2,64,1024]{5,4,3,2,1,0:T(8,128)(2,1)S(1)} %pad_maximum_fusion.6), channel_id=1, source_target_pairs={{0,4},{4,0},{8,12},{12,8},{1,5},{5,1},{9,13},{13,9},{2,6},{6,2},{1... | collective-permute-start | bytes 1572872 | tf_op jit(solution)/shard_map/ppermute | solution.py:62
  149.9 13.9 %collective-permute-start.5 = (bf16[1,1,2,2,64,1024]{5,4,3,2,1,0:T(8,128)(2,1)S(1)}, bf16[1,1,2,2,64,1024]{5,4,3,2,1,0:T(8,128)(2,1)S(1)}, u32[]{:S(2)}, u32[]{:S(2)}) collective-permute-start(bf16[1,1,2,2,64,1024]{5,4,3,2,1,0:T(8,128)(2,1)S(1)} %pad_maximum_fusion.5), channel_id=1, source_target_pairs={{0,2},{1,3},{2,0},{3,1},{4,6},{5,7},{6,4},{7,5},{8,10},{9,11},{10,... | collective-permute-start | bytes 1572872 | tf_op jit(solution)/shard_map/ppermute | solution.py:62
  161.1 5.5 %collective-permute-start.10 = (bf16[1,2,2,2,64,1024]{5,4,3,2,1,0:T(8,128)(2,1)S(1)}, bf16[1,2,2,2,64,1024]{5,4,3,2,1,0:T(8,128)(2,1)S(1)}, u32[]{:S(2)}, u32[]{:S(2)}) collective-permute-start(bf16[1,2,2,2,64,1024]{5,4,3,2,1,0:T(8,128)(2,1)S(1)} %pad_maximum_fusion.3), channel_id=1, source_target_pairs={{0,1},{1,0},{2,3},{3,2},{4,5},{5,4},{6,7},{7,6},{8,9},{9,8},{10,11... | collective-permute-start | bytes 3145736 | tf_op jit(solution)/shard_map/ppermute | solution.py:62
  163.9 4.2 collective-permute-start.6
  168.2 35.3 %slice-start = ((s8[6291456]{0:T(1024)(128)(4,1)}), s8[4194304]{0:T(1024)(128)(4,1)S(1)}, s32[]{:S(2)}) async-start(s8[6291456]{0:T(1024)(128)(4,1)} %bitcast.123), calls=%async_computation.6 | async-start | bytes 8388608
  197.4 48.5 %copy-start.9 = (bf16[1024,1024]{1,0:T(8,128)(2,1)}, bf16[1024,1024]{1,0:T(8,128)(2,1)S(1)}, u32[]{:S(2)}) copy-start(bf16[1024,1024]{1,0:T(8,128)(2,1)S(1)} %get-tuple-element.98.right_ref) | copy-start | bytes 6291460
  203.4 3.1 collective-permute-start.14
  206.0 6.8 %collective-permute-start.12 = (bf16[512,1024]{1,0:T(8,128)(2,1)S(1)}, bf16[512,1024]{1,0:T(8,128)(2,1)S(1)}, u32[]{:S(2)}, u32[]{:S(2)}) collective-permute-start(bf16[512,1024]{1,0:T(8,128)(2,1)S(1)} %fusion.41), channel_id=1, source_target_pairs={{0,1},{1,0},{2,3},{3,2},{4,5},{5,4},{6,7},{7,6},{8,9},{9,8},{10,11... | collective-permute-start | bytes 3145736 | tf_op jit(solution)/shard_map/ppermute | solution.py:62
  211.2 13.9 %collective-permute-start.15 = (bf16[1,2,1,2,64,1024]{5,4,3,2,1,0:T(8,128)(2,1)S(1)}, bf16[1,2,1,2,64,1024]{5,4,3,2,1,0:T(8,128)(2,1)S(1)}, u32[]{:S(2)}, u32[]{:S(2)}) collective-permute-start(bf16[1,2,1,2,64,1024]{5,4,3,2,1,0:T(8,128)(2,1)S(1)} %slice.253), channel_id=1, source_target_pairs={{0,4},{4,0},{8,12},{12,8},{1,5},{5,1},{9,13},{13,9},{2,6},{6,2},{1... | collective-permute-start | bytes 1572872 | tf_op jit(solution)/shard_map/ppermute | solution.py:62
  215.3 13.7 %collective-permute-start.13 = (bf16[1,1,2,2,64,1024]{5,4,3,2,1,0:T(8,128)(2,1)S(1)}, bf16[1,1,2,2,64,1024]{5,4,3,2,1,0:T(8,128)(2,1)S(1)}, u32[]{:S(2)}, u32[]{:S(2)}) collective-permute-start(bf16[1,1,2,2,64,1024]{5,4,3,2,1,0:T(8,128)(2,1)S(1)} %slice.250), channel_id=1, source_target_pairs={{0,2},{1,3},{2,0},{3,1},{4,6},{5,7},{6,4},{7,5},{8,10},{9,11},{10,... | collective-permute-start | bytes 1572872 | tf_op jit(solution)/shard_map/ppermute | solution.py:62
  223.2 137.1 %collective-permute-start.32 = (bf16[1024,2048]{1,0:T(8,128)(2,1)}, bf16[1024,2048]{1,0:T(8,128)(2,1)}, u32[]{:S(2)}, u32[]{:S(2)}) collective-permute-start(bf16[1024,2048]{1,0:T(8,128)(2,1)} %convolution_convert_fusion), channel_id=1, source_target_pairs={{0,16},{16,0},{1,17},{17,1},{2,18},{18,2},{3,19},{19,3},{4,20},{20... | collective-permute-start | bytes 12582920 | tf_op jit(solution)/shard_map/ppermute | solution.py:347
  229.2 13.8 %collective-permute-start.17 = (bf16[1,2,1,1,64,1024]{5,4,3,2,1,0:T(8,128)(2,1)S(1)}, bf16[1,2,1,1,64,1024]{5,4,3,2,1,0:T(8,128)(2,1)S(1)}, u32[]{:S(2)}, u32[]{:S(2)}) collective-permute-start(bf16[1,2,1,1,64,1024]{5,4,3,2,1,0:T(8,128)(2,1)S(1)} %slice.202), channel_id=1, source_target_pairs={{0,8},{4,12},{8,0},{12,4},{1,9},{5,13},{9,1},{13,5},{2,10},{6,14},... | collective-permute-start | bytes 786440 | tf_op jit(solution)/shard_map/ppermute | solution.py:62
  231.8 12.4 %collective-permute-start.16 = (bf16[1,1,1,2,64,1024]{5,4,3,2,1,0:T(8,128)(2,1)S(1)}, bf16[1,1,1,2,64,1024]{5,4,3,2,1,0:T(8,128)(2,1)S(1)}, u32[]{:S(2)}, u32[]{:S(2)}) collective-permute-start(bf16[1,1,1,2,64,1024]{5,4,3,2,1,0:T(8,128)(2,1)S(1)} %slice.200), channel_id=1, source_target_pairs={{0,4},{4,0},{8,12},{12,8},{1,5},{5,1},{9,13},{13,9},{2,6},{6,2},{1... | collective-permute-start | bytes 786440 | tf_op jit(solution)/shard_map/ppermute | solution.py:62
  244.4 5.4 %collective-permute-start.19 = (bf16[1,1,1,1,64,1024]{5,4,3,2,1,0:T(8,128)(2,1)S(1)}, bf16[1,1,1,1,64,1024]{5,4,3,2,1,0:T(8,128)(2,1)S(1)}, u32[]{:S(2)}, u32[]{:S(2)}) collective-permute-start(bf16[1,1,1,1,64,1024]{5,4,3,2,1,0:T(8,128)(2,1)S(1)} %slice.206), channel_id=1, source_target_pairs={{0,2},{1,3},{2,0},{3,1},{4,6},{5,7},{6,4},{7,5},{8,10},{9,11},{10,... | collective-permute-start | bytes 393224 | tf_op jit(solution)/shard_map/ppermute | solution.py:62
  245.9 7.1 %collective-permute-start.18 = (bf16[1,1,1,1,64,1024]{5,4,3,2,1,0:T(8,128)(2,1)S(1)}, bf16[1,1,1,1,64,1024]{5,4,3,2,1,0:T(8,128)(2,1)S(1)}, u32[]{:S(2)}, u32[]{:S(2)}) collective-permute-start(bf16[1,1,1,1,64,1024]{5,4,3,2,1,0:T(8,128)(2,1)S(1)} %slice.204), channel_id=1, source_target_pairs={{0,8},{4,12},{8,0},{12,4},{1,9},{5,13},{9,1},{13,5},{2,10},{6,14},... | collective-permute-start | bytes 393224 | tf_op jit(solution)/shard_map/ppermute | solution.py:62
  249.8 36.2 %collective-permute-start.21 = (bf16[512,1024]{1,0:T(8,128)(2,1)}, bf16[512,1024]{1,0:T(8,128)(2,1)}, u32[]{:S(2)}, u32[]{:S(2)}) collective-permute-start(bf16[512,1024]{1,0:T(8,128)(2,1)} %fusion.38), channel_id=1, source_target_pairs={{0,1},{1,0},{2,3},{3,2},{4,5},{5,4},{6,7},{7,6},{8,9},{9,8},{10,11... | collective-permute-start | bytes 3145736 | tf_op jit(solution)/shard_map/ppermute | solution.py:62
  257.7 14.3 %all-to-all-start.1 = ((bf16[64,16,128]{2,0,1:T(8,128)(2,1)}), bf16[64,16,128]{2,0,1:T(8,128)(2,1)}, u32[]{:S(2)}, u32[]{:S(2)}) async-start(bf16[64,16,128]{2,0,1:T(8,128)(2,1)} %copy_bitcast_fusion.1), calls=%async_computation.1 | async-start | bytes 524288 | tf_op jit(solution)/shard_map/all_to_all | solution.py:588
  261.9 111.2 %all-gather.9.cloned.1.call-start = ((), (), s32[]{:S(2)}) async-start(), calls=%async_computation.4 | async-start | bytes 4456448 | tf_op jit(solution)/shard_map/all_gather | solution.py:517
  266.2 23.5 %collective-permute-start.20 = (bf16[512,1024]{1,0:T(8,128)(2,1)}, bf16[512,1024]{1,0:T(8,128)(2,1)}, u32[]{:S(2)}, u32[]{:S(2)}) collective-permute-start(bf16[512,1024]{1,0:T(8,128)(2,1)} %fusion.35), channel_id=1, source_target_pairs={{0,1},{1,0},{2,3},{3,2},{4,5},{5,4},{6,7},{7,6},{8,9},{9,8},{10,11... | collective-permute-start | bytes 3145736 | tf_op jit(solution)/shard_map/ppermute | solution.py:62
  267.2 178.5 %all-gather.11.cloned.1.call-start = ((), (), s32[]{:S(2)}) async-start(), calls=%async_computation.5 | async-start | bytes 4456448 | tf_op jit(solution)/shard_map/all_gather | solution.py:522
  286.0 32.7 %collective-permute-start.27 = (bf16[512,1024]{1,0:T(8,128)(2,1)S(1)}, bf16[512,1024]{1,0:T(8,128)(2,1)S(1)}, u32[]{:S(2)}, u32[]{:S(2)}) collective-permute-start(bf16[512,1024]{1,0:T(8,128)(2,1)S(1)} %convolution_convert_fusion.2), channel_id=1, source_target_pairs={{0,1},{1,0},{2,3},{3,2},{4,5},{5,4},{6,7},{7,6},{8,9},{9,8},{10,11... | collective-permute-start | bytes 3145736 | tf_op jit(solution)/shard_map/ppermute | solution.py:62
  293.0 25.5 %collective-permute-start.23 = (bf16[1,2,1,2,64,1024]{5,4,3,2,1,0:T(8,128)(2,1)S(1)}, bf16[1,2,1,2,64,1024]{5,4,3,2,1,0:T(8,128)(2,1)S(1)}, u32[]{:S(2)}, u32[]{:S(2)}) collective-permute-start(bf16[1,2,1,2,64,1024]{5,4,3,2,1,0:T(8,128)(2,1)S(1)} %slice.213), channel_id=1, source_target_pairs={{0,4},{4,0},{8,12},{12,8},{1,5},{5,1},{9,13},{13,9},{2,6},{6,2},{1... | collective-permute-start | bytes 1572872 | tf_op jit(solution)/shard_map/ppermute | solution.py:62
  294.2 25.3 %collective-permute-start.26 = (bf16[512,1024]{1,0:T(8,128)(2,1)S(1)}, bf16[512,1024]{1,0:T(8,128)(2,1)S(1)}, u32[]{:S(2)}, u32[]{:S(2)}) collective-permute-start(bf16[512,1024]{1,0:T(8,128)(2,1)S(1)} %convolution_convert_fusion.3), channel_id=1, source_target_pairs={{0,1},{1,0},{2,3},{3,2},{4,5},{5,4},{6,7},{7,6},{8,9},{9,8},{10,11... | collective-permute-start | bytes 3145736 | tf_op jit(solution)/shard_map/ppermute | solution.py:62
  294.3 26.2 %collective-permute-start.22 = (bf16[1,1,2,2,64,1024]{5,4,3,2,1,0:T(8,128)(2,1)S(1)}, bf16[1,1,2,2,64,1024]{5,4,3,2,1,0:T(8,128)(2,1)S(1)}, u32[]{:S(2)}, u32[]{:S(2)}) collective-permute-start(bf16[1,1,2,2,64,1024]{5,4,3,2,1,0:T(8,128)(2,1)S(1)} %slice.211), channel_id=1, source_target_pairs={{0,2},{1,3},{2,0},{3,1},{4,6},{5,7},{6,4},{7,5},{8,10},{9,11},{10,... | collective-permute-start | bytes 1572872 | tf_op jit(solution)/shard_map/ppermute | solution.py:62
  320.2 22.3 %collective-permute-start.29 = (bf16[1,2,1,2,64,1024]{5,4,3,2,1,0:T(8,128)(2,1)S(1)}, bf16[1,2,1,2,64,1024]{5,4,3,2,1,0:T(8,128)(2,1)S(1)}, u32[]{:S(2)}, u32[]{:S(2)}) collective-permute-start(bf16[1,2,1,2,64,1024]{5,4,3,2,1,0:T(8,128)(2,1)S(1)} %slice.260), channel_id=1, source_target_pairs={{0,4},{4,0},{8,12},{12,8},{1,5},{5,1},{9,13},{13,9},{2,6},{6,2},{1... | collective-permute-start | bytes 1572872 | tf_op jit(solution)/shard_map/ppermute | solution.py:62
  320.7 23.7 %collective-permute-start.25 = (bf16[1,2,1,1,64,1024]{5,4,3,2,1,0:T(8,128)(2,1)S(1)}, bf16[1,2,1,1,64,1024]{5,4,3,2,1,0:T(8,128)(2,1)S(1)}, u32[]{:S(2)}, u32[]{:S(2)}) collective-permute-start(bf16[1,2,1,1,64,1024]{5,4,3,2,1,0:T(8,128)(2,1)S(1)} %slice.217), channel_id=1, source_target_pairs={{0,8},{4,12},{8,0},{12,4},{1,9},{5,13},{9,1},{13,5},{2,10},{6,14},... | collective-permute-start | bytes 786440 | tf_op jit(solution)/shard_map/ppermute | solution.py:62
  321.5 28.2 %collective-permute-start.24 = (bf16[1,1,1,2,64,1024]{5,4,3,2,1,0:T(8,128)(2,1)S(1)}, bf16[1,1,1,2,64,1024]{5,4,3,2,1,0:T(8,128)(2,1)S(1)}, u32[]{:S(2)}, u32[]{:S(2)}) collective-permute-start(bf16[1,1,1,2,64,1024]{5,4,3,2,1,0:T(8,128)(2,1)S(1)} %slice.215), channel_id=1, source_target_pairs={{0,4},{4,0},{8,12},{12,8},{1,5},{5,1},{9,13},{13,9},{2,6},{6,2},{1... | collective-permute-start | bytes 786440 | tf_op jit(solution)/shard_map/ppermute | solution.py:62
  322.8 19.8 %collective-permute-start.28 = (bf16[1,1,2,2,64,1024]{5,4,3,2,1,0:T(8,128)(2,1)S(1)}, bf16[1,1,2,2,64,1024]{5,4,3,2,1,0:T(8,128)(2,1)S(1)}, u32[]{:S(2)}, u32[]{:S(2)}) collective-permute-start(bf16[1,1,2,2,64,1024]{5,4,3,2,1,0:T(8,128)(2,1)S(1)} %slice.258), channel_id=1, source_target_pairs={{0,2},{1,3},{2,0},{3,1},{4,6},{5,7},{6,4},{7,5},{8,10},{9,11},{10,... | collective-permute-start | bytes 1572872 | tf_op jit(solution)/shard_map/ppermute | solution.py:62
  342.9 14.8 %collective-permute-start.31 = (bf16[1,2,1,1,64,1024]{5,4,3,2,1,0:T(8,128)(2,1)S(1)}, bf16[1,2,1,1,64,1024]{5,4,3,2,1,0:T(8,128)(2,1)S(1)}, u32[]{:S(2)}, u32[]{:S(2)}) collective-permute-start(bf16[1,2,1,1,64,1024]{5,4,3,2,1,0:T(8,128)(2,1)S(1)} %slice.227), channel_id=1, source_target_pairs={{0,8},{4,12},{8,0},{12,4},{1,9},{5,13},{9,1},{13,5},{2,10},{6,14},... | collective-permute-start | bytes 786440 | tf_op jit(solution)/shard_map/ppermute | solution.py:62
  345.1 14.2 %collective-permute-start.30 = (bf16[1,1,1,2,64,1024]{5,4,3,2,1,0:T(8,128)(2,1)S(1)}, bf16[1,1,1,2,64,1024]{5,4,3,2,1,0:T(8,128)(2,1)S(1)}, u32[]{:S(2)}, u32[]{:S(2)}) collective-permute-start(bf16[1,1,1,2,64,1024]{5,4,3,2,1,0:T(8,128)(2,1)S(1)} %slice.225), channel_id=1, source_target_pairs={{0,4},{4,0},{8,12},{12,8},{1,5},{5,1},{9,13},{13,9},{2,6},{6,2},{1... | collective-permute-start | bytes 786440 | tf_op jit(solution)/shard_map/ppermute | solution.py:62
  361.0 9.4 %collective-permute-start.33 = (bf16[1,1,1,1,64,1024]{5,4,3,2,1,0:T(8,128)(2,1)}, bf16[1,1,1,1,64,1024]{5,4,3,2,1,0:T(8,128)(2,1)}, u32[]{:S(2)}, u32[]{:S(2)}) collective-permute-start(bf16[1,1,1,1,64,1024]{5,4,3,2,1,0:T(8,128)(2,1)} %slice.229), channel_id=1, source_target_pairs={{0,8},{4,12},{8,0},{12,4},{1,9},{5,13},{9,1},{13,5},{2,10},{6,14},... | collective-permute-start | bytes 393224 | tf_op jit(solution)/shard_map/ppermute | solution.py:62
  363.0 8.4 %collective-permute-start.34 = (bf16[1,1,1,1,64,1024]{5,4,3,2,1,0:T(8,128)(2,1)S(1)}, bf16[1,1,1,1,64,1024]{5,4,3,2,1,0:T(8,128)(2,1)S(1)}, u32[]{:S(2)}, u32[]{:S(2)}) collective-permute-start(bf16[1,1,1,1,64,1024]{5,4,3,2,1,0:T(8,128)(2,1)S(1)} %slice.231), channel_id=1, source_target_pairs={{0,2},{1,3},{2,0},{3,1},{4,6},{5,7},{6,4},{7,5},{8,10},{9,11},{10,... | collective-permute-start | bytes 393224 | tf_op jit(solution)/shard_map/ppermute | solution.py:62
  374.4 56.4 %collective-permute-start.41 = (bf16[1024,1024]{1,0:T(8,128)(2,1)}, bf16[1024,1024]{1,0:T(8,128)(2,1)S(1)}, u32[]{:S(2)}, u32[]{:S(2)}) collective-permute-start(bf16[1024,1024]{1,0:T(8,128)(2,1)} %convolution_convert_fusion.1), channel_id=1, source_target_pairs={{0,16},{16,0},{1,17},{17,1},{2,18},{18,2},{3,19},{19,3},{4,20},{20... | collective-permute-start | bytes 6291464 | tf_op jit(solution)/shard_map/ppermute | solution.py:347
  376.4 12.4 %collective-permute-start.36 = (bf16[1,1,1,1,64,1024]{5,4,3,2,1,0:T(8,128)(2,1)S(1)}, bf16[1,1,1,1,64,1024]{5,4,3,2,1,0:T(8,128)(2,1)S(1)}, u32[]{:S(2)}, u32[]{:S(2)}) collective-permute-start(bf16[1,1,1,1,64,1024]{5,4,3,2,1,0:T(8,128)(2,1)S(1)} %slice.235), channel_id=1, source_target_pairs={{0,2},{1,3},{2,0},{3,1},{4,6},{5,7},{6,4},{7,5},{8,10},{9,11},{10,... | collective-permute-start | bytes 393224 | tf_op jit(solution)/shard_map/ppermute | solution.py:62
  377.0 13.2 %collective-permute-start.35 = (bf16[1,1,1,1,64,1024]{5,4,3,2,1,0:T(8,128)(2,1)S(1)}, bf16[1,1,1,1,64,1024]{5,4,3,2,1,0:T(8,128)(2,1)S(1)}, u32[]{:S(2)}, u32[]{:S(2)}) collective-permute-start(bf16[1,1,1,1,64,1024]{5,4,3,2,1,0:T(8,128)(2,1)S(1)} %slice.233), channel_id=1, source_target_pairs={{0,8},{4,12},{8,0},{12,4},{1,9},{5,13},{9,1},{13,5},{2,10},{6,14},... | collective-permute-start | bytes 393224 | tf_op jit(solution)/shard_map/ppermute | solution.py:62
  394.0 5.0 %collective-permute-start.38 = (bf16[1,1,1,1,64,1024]{5,4,3,2,1,0:T(8,128)(2,1)S(1)}, bf16[1,1,1,1,64,1024]{5,4,3,2,1,0:T(8,128)(2,1)S(1)}, u32[]{:S(2)}, u32[]{:S(2)}) collective-permute-start(bf16[1,1,1,1,64,1024]{5,4,3,2,1,0:T(8,128)(2,1)S(1)} %get-tuple-element.129), channel_id=1, source_target_pairs={{0,2},{1,3},{2,0},{3,1},{4,6},{5,7},{6,4},{7,5},{8,10},{9,11},{10,... | collective-permute-start | bytes 393224 | tf_op jit(solution)/shard_map/ppermute | solution.py:62
  394.3 9.2 %collective-permute-start.37 = (bf16[1,1,1,1,64,1024]{5,4,3,2,1,0:T(8,128)(2,1)S(1)}, bf16[1,1,1,1,64,1024]{5,4,3,2,1,0:T(8,128)(2,1)S(1)}, u32[]{:S(2)}, u32[]{:S(2)}) collective-permute-start(bf16[1,1,1,1,64,1024]{5,4,3,2,1,0:T(8,128)(2,1)S(1)} %get-tuple-element.130), channel_id=1, source_target_pairs={{0,8},{4,12},{8,0},{12,4},{1,9},{5,13},{9,1},{13,5},{2,10},{6,14},... | collective-permute-start | bytes 393224 | tf_op jit(solution)/shard_map/ppermute | solution.py:62
  403.5 29.9 %copy-start.2 = (bf16[1024,1024]{1,0:T(8,128)(2,1)S(1)}, bf16[1024,1024]{1,0:T(8,128)(2,1)}, u32[]{:S(2)}) copy-start(bf16[1024,1024]{1,0:T(8,128)(2,1)} %get-tuple-element.127.left_ref) | copy-start | bytes 6291460
  403.5 22.3 %collective-permute-start.40 = (bf16[1,2,1,1,64,1024]{5,4,3,2,1,0:T(8,128)(2,1)S(1)}, bf16[1,2,1,1,64,1024]{5,4,3,2,1,0:T(8,128)(2,1)S(1)}, u32[]{:S(2)}, u32[]{:S(2)}) collective-permute-start(bf16[1,2,1,1,64,1024]{5,4,3,2,1,0:T(8,128)(2,1)S(1)} %pad_maximum_fusion.13), channel_id=1, source_target_pairs={{0,8},{4,12},{8,0},{12,4},{1,9},{5,13},{9,1},{13,5},{2,10},{6,14},... | collective-permute-start | bytes 786440 | tf_op jit(solution)/shard_map/ppermute | solution.py:62
  403.6 27.2 %collective-permute-start.39 = (bf16[1,1,1,2,64,1024]{5,4,3,2,1,0:T(8,128)(2,1)S(1)}, bf16[1,1,1,2,64,1024]{5,4,3,2,1,0:T(8,128)(2,1)S(1)}, u32[]{:S(2)}, u32[]{:S(2)}) collective-permute-start(bf16[1,1,1,2,64,1024]{5,4,3,2,1,0:T(8,128)(2,1)S(1)} %pad_maximum_fusion.12), channel_id=1, source_target_pairs={{0,4},{4,0},{8,12},{12,8},{1,5},{5,1},{9,13},{13,9},{2,6},{6,2},{1... | collective-permute-start | bytes 786440 | tf_op jit(solution)/shard_map/ppermute | solution.py:62
  407.7 37.0 %collective-permute-start.44 = (bf16[1024,512]{1,0:T(8,128)(2,1)S(1)}, bf16[1024,512]{1,0:T(8,128)(2,1)S(1)}, u32[]{:S(2)}, u32[]{:S(2)}) collective-permute-start(bf16[1024,512]{1,0:T(8,128)(2,1)S(1)} %pad_maximum_fusion.4), channel_id=1, source_target_pairs={{0,16},{16,0},{1,17},{17,1},{2,18},{18,2},{3,19},{19,3},{4,20},{20... | collective-permute-start | bytes 3145736 | tf_op jit(solution)/shard_map/ppermute | solution.py:347
  430.9 11.3 %collective-permute-start.43 = (bf16[1,2,1,2,64,1024]{5,4,3,2,1,0:T(8,128)(2,1)S(1)}, bf16[1,2,1,2,64,1024]{5,4,3,2,1,0:T(8,128)(2,1)S(1)}, u32[]{:S(2)}, u32[]{:S(2)}) collective-permute-start(bf16[1,2,1,2,64,1024]{5,4,3,2,1,0:T(8,128)(2,1)S(1)} %pad_maximum_fusion.8), channel_id=1, source_target_pairs={{0,4},{4,0},{8,12},{12,8},{1,5},{5,1},{9,13},{13,9},{2,6},{6,2},{1... | collective-permute-start | bytes 1572872 | tf_op jit(solution)/shard_map/ppermute | solution.py:62
  431.0 11.3 %collective-permute-start.42 = (bf16[1,1,2,2,64,1024]{5,4,3,2,1,0:T(8,128)(2,1)S(1)}, bf16[1,1,2,2,64,1024]{5,4,3,2,1,0:T(8,128)(2,1)S(1)}, u32[]{:S(2)}, u32[]{:S(2)}) collective-permute-start(bf16[1,1,2,2,64,1024]{5,4,3,2,1,0:T(8,128)(2,1)S(1)} %pad_maximum_fusion.7), channel_id=1, source_target_pairs={{0,2},{1,3},{2,0},{3,1},{4,6},{5,7},{6,4},{7,5},{8,10},{9,11},{10,... | collective-permute-start | bytes 1572872 | tf_op jit(solution)/shard_map/ppermute | solution.py:62
  445.7 23.5 %collective-permute-start.45 = (bf16[1,2,2,2,64,1024]{5,4,3,2,1,0:T(8,128)(2,1)}, bf16[1,2,2,2,64,1024]{5,4,3,2,1,0:T(8,128)(2,1)}, u32[]{:S(2)}, u32[]{:S(2)}) collective-permute-start(bf16[1,2,2,2,64,1024]{5,4,3,2,1,0:T(8,128)(2,1)} %constant_dynamic-update-slice_fusion), channel_id=1, source_target_pairs={{0,1},{1,0},{2,3},{3,2},{4,5},{5,4},{6,7},{7,6},{8,9},{9,8},{10,11... | collective-permute-start | bytes 3145736 | tf_op jit(solution)/shard_map/ppermute | solution.py:62
  445.7 23.5 %collective-permute-start.46 = (bf16[1,2,2,2,64,1024]{5,4,3,2,1,0:T(8,128)(2,1)}, bf16[1,2,2,2,64,1024]{5,4,3,2,1,0:T(8,128)(2,1)}, u32[]{:S(2)}, u32[]{:S(2)}) collective-permute-start(bf16[1,2,2,2,64,1024]{5,4,3,2,1,0:T(8,128)(2,1)} %copy-done.7), channel_id=1, source_target_pairs={{0,1},{1,0},{2,3},{3,2},{4,5},{5,4},{6,7},{7,6},{8,9},{9,8},{10,11... | collective-permute-start | bytes 3145736 | tf_op jit(solution)/shard_map/ppermute | solution.py:62
  446.3 2.1 collective-permute-start.47
  448.4 3.8 collective-permute-start.48
  452.3 3.8 collective-permute-start.49
  456.1 4.7 collective-permute-start.50
  460.8 14.2 %collective-permute-start.51 = (f32[2,2048]{1,0:T(2,128)S(1)}, f32[2,2048]{1,0:T(2,128)S(1)}, u32[]{:S(2)}, u32[]{:S(2)}) collective-permute-start(f32[2,2048]{1,0:T(2,128)S(1)} %add.277), channel_id=1, source_target_pairs={{0,16},{16,0},{1,17},{17,1},{2,18},{18,2},{3,19},{19,3},{4,20},{20... | collective-permute-start | bytes 49160 | tf_op jit(solution)/shard_map/ppermute | solution.py:347
  (60 other events, 476.9 us)
Sparse Core Ops, SparseCore 0:
  11.1 55.7 all-gather.4
  69.0 51.0 all-gather.6
  267.3 63.1 all-gather.8
  373.3 60.3 all-gather.10
